TPU v7x, 32 devices: a whole 2x2x4 slice. The times are simulated.
32 devices in a mesh: seq: 8 (over z, x), dp: 4 (over y, core).
Axes of the slice: x: 2, y: 2, z: 4, core: 2. Of those that a mesh axis runs over, the one named last changes fastest.
Arguments:
- linear_queries: bfloat16 [4, 1024, 2048], P('dp', 'seq'), may hold values from -6 to 6
- linear_keys: bfloat16 [4, 1024, 2048], P('dp', 'seq'), may hold values from -6 to 6
- window_queries: bfloat16 [4, 1024, 2048], P('dp', 'seq'), may hold values from -41 to 41
- window_keys: bfloat16 [4, 1024, 2048], P('dp', 'seq'), may hold values from -12 to 12
- values: bfloat16 [4, 1024, 2048], P('dp', 'seq'), may hold values from -8 to 8
- cotangent: bfloat16 [4, 1024, 2048], P('dp', 'seq'), may hold values from -10 to 10
- feature_map: bfloat16 [16, 128, 128], replicated, may hold values from -0.5 to 0.5
Outputs:
- attended: bfloat16 [4, 1024, 2048], P('dp', 'seq')
- dlinear_queries: bfloat16 [4, 1024, 2048], P('dp', 'seq')
- dlinear_keys: bfloat16 [4, 1024, 2048], P('dp', 'seq')
- dwindow_queries: bfloat16 [4, 1024, 2048], P('dp', 'seq')
- dwindow_keys: bfloat16 [4, 1024, 2048], P('dp', 'seq')
- dvalues: bfloat16 [4, 1024, 2048], P('dp', 'seq')
- dfeature_map: float32 [16, 128, 128], replicated
All inputs are finite; a program needn't handle non-finite values.
Results may differ from a plain program's by a relative error of at most 0.009.
Values may be sent and summed in bfloat16 or wider, within the bound.
No kernel may reach another device: no remote copies, remote signals or barrier semaphores. Data moves between devices by JAX's collectives and lax.ppermute only.
A program may use at most 192 MiB of HBM per device.

v0:
```python
import jax
import jax.numpy as jnp
from jax import lax
from jax.sharding import PartitionSpec as P

HEADS = 16
HD = 128
WINDOW = 64


def entering(shard, axis, join, neutral, backward):
    count = lax.axis_size(axis)
    place = lax.axis_index(axis)
    ahead = count - 1 - place if backward else place
    gathered = lax.all_gather(shard.astype(jnp.bfloat16), axis)
    state = jnp.zeros_like(shard) + jnp.asarray(neutral, shard.dtype)

    def one(turn, state):
        source = count - 1 - turn if backward else turn
        return join(state, lax.dynamic_index_in_dim(gathered, source, 0, False).astype(shard.dtype))

    return lax.fori_loop(0, ahead, one, state)


def passed_along(block, axis, distance):
    devices = range(lax.axis_size(axis))
    route = [(i - distance, i) for i in devices if i - distance in devices]
    return lax.ppermute(block, axis, route)


def plain(form, left, right):
    return jnp.einsum(form, left, right, preferred_element_type=jnp.float32)


def exact(form, left, right):
    return jnp.einsum(
        form, left.astype(jnp.float32), right.astype(jnp.float32), precision=lax.Precision.HIGHEST
    )


def feature(inputs, feature_map):
    before = plain("htd,hde->hte", inputs, feature_map)
    mapped = jnp.where(before > 0, before + 1.0, jnp.exp(jnp.minimum(before, 0.0)))
    return (before, mapped.astype(jnp.bfloat16))


def slope(before):
    return jnp.where(before > 0, 1.0, jnp.exp(jnp.minimum(before, 0.0)))


def split_heads(matrix):
    return matrix.reshape(matrix.shape[0], HEADS, HD).transpose(1, 0, 2)


def join_heads(tensor):
    return tensor.transpose(1, 0, 2).reshape(tensor.shape[1], HEADS * HD)


def exclusive(terms, reverse):
    zero = jnp.zeros_like(terms[:1])
    if reverse:
        totals = jnp.flip(jnp.cumsum(jnp.flip(terms, 0), axis=0), 0)
        return jnp.concatenate([totals[1:], zero], axis=0)
    totals = jnp.cumsum(terms, axis=0)
    return jnp.concatenate([zero, totals[:-1]], axis=0)


def band_mask():
    rows = lax.broadcasted_iota(jnp.int32, (WINDOW, 2 * WINDOW), 0)
    cols = lax.broadcasted_iota(jnp.int32, (WINDOW, 2 * WINDOW), 1)
    offset = cols - rows
    return (offset >= 1) & (offset <= WINDOW)


def window_mask(blocks, start):
    cols = lax.broadcasted_iota(jnp.int32, (blocks, WINDOW, 2 * WINDOW), 2)
    block = lax.broadcasted_iota(jnp.int32, (blocks, WINDOW, 2 * WINDOW), 0)
    keypos = start + block * WINDOW + cols - WINDOW
    return band_mask()[None] & (keypos >= 0)


def causal_mask():
    rows = lax.broadcasted_iota(jnp.int32, (WINDOW, WINDOW), 0)
    cols = lax.broadcasted_iota(jnp.int32, (WINDOW, WINDOW), 1)
    return rows >= cols


def pairs(rim, inputs):
    blocks = inputs.shape[1] // WINDOW
    early = jnp.concatenate([rim, inputs[:, : inputs.shape[1] - WINDOW]], axis=1).reshape(
        HEADS, blocks, WINDOW, HD
    )
    late = inputs.reshape(HEADS, blocks, WINDOW, HD)
    return jnp.concatenate([early, late], axis=2)


def softmax_rows(score, mask):
    top = jnp.max(jnp.where(mask, score, -jnp.inf), axis=-1, keepdims=True)
    expo = jnp.exp(jnp.where(mask, score - top, -jnp.inf))
    return expo / jnp.sum(expo, axis=-1, keepdims=True)


def fold_pairs(pair, rim):
    after = jnp.concatenate([pair[:, 1:, :WINDOW], rim[:, None]], axis=1)
    return pair[:, :, WINDOW:] + after


def add_up(earlier, later):
    return earlier + later


def carry_states(totals, reverse):
    if reverse:
        return entering(totals, "seq", add_up, jnp.zeros_like(totals), True)
    return entering(totals, "seq", add_up, jnp.zeros_like(totals), False)


def on_device(
    linear_queries, linear_keys, window_queries, window_keys, values, cotangent, feature_map
):
    tokens = linear_queries.shape[1]
    blocks = tokens // WINDOW
    block_shape = (HEADS, blocks, WINDOW, HD)
    length = tokens * lax.axis_size("seq")
    lin_scale = 1.0 / (HD * length)
    inverse_root = HD ** (-0.5)
    win_heads = split_heads(window_queries[0])
    wkey_heads = split_heads(window_keys[0])
    value_heads = split_heads(values[0])
    grad_full = split_heads(cotangent[0])
    key_rim, value_rim = passed_along(
        (wkey_heads[:, tokens - WINDOW :], value_heads[:, tokens - WINDOW :]), "seq", 1
    )
    query_heads = split_heads(linear_queries[0])
    key_heads = split_heads(linear_keys[0])
    pre_query, feat_query = feature(query_heads, feature_map)
    pre_key, feat_key = feature(key_heads, feature_map)
    query_blocks = feat_query.reshape(block_shape)
    key_blocks = feat_key.reshape(block_shape)
    value_blocks = value_heads.reshape(block_shape)
    causal = causal_mask()
    lin_scores = jnp.where(causal, plain("hncf,hnsf->hncs", query_blocks, key_blocks), 0.0)
    block_states = plain("hnsf,hnsd->nhfd", key_blocks, value_blocks)
    state_in = carry_states(jnp.sum(block_states, axis=0), False)[None] + exclusive(
        block_states, False
    )
    lin = (
        exact("hncs,hnsd->hncd", lin_scores, value_blocks)
        + exact("hncf,nhfd->hncd", query_blocks, state_in)
    ) * lin_scale
    win_queries = win_heads.reshape(block_shape)
    key_pairs = pairs(key_rim, wkey_heads)
    value_pairs = pairs(value_rim, value_heads)
    mask = window_mask(blocks, lax.axis_index("seq") * tokens)
    prob = softmax_rows(plain("hncd,hnsd->hncs", win_queries, key_pairs) * inverse_root, mask[None])
    prob_b = prob.astype(jnp.bfloat16)
    win = plain("hncs,hnsd->hncd", prob_b, value_pairs)
    attended = join_heads((lin + win).astype(jnp.bfloat16).reshape(HEADS, tokens, HD))
    grad_heads = grad_full.reshape(block_shape)
    grad_lin = grad_heads.astype(jnp.float32) * lin_scale
    mixed = jnp.where(causal, plain("hncd,hnsd->hncs", grad_heads, value_blocks), 0.0) * lin_scale
    dfeat_query = exact("hncs,hnsf->hncf", mixed, key_blocks) + exact(
        "hncd,nhfd->hncf", grad_lin, state_in
    )
    grad_states = plain("hncf,hncd->nhfd", query_blocks, grad_heads) * lin_scale
    state_after = carry_states(jnp.sum(grad_states, axis=0), True)[None] + exclusive(
        grad_states, True
    )
    dfeat_key = exact("hncs,hncf->hnsf", mixed, query_blocks) + exact(
        "nhfd,hnsd->hnsf", state_after, value_blocks
    )
    dvalue_lin = exact("hncs,hncd->hnsd", lin_scores, grad_lin) + exact(
        "hnsf,nhfd->hnsd", key_blocks, state_after
    )
    dpre_query = (dfeat_query.reshape(HEADS, tokens, HD) * slope(pre_query)).astype(jnp.bfloat16)
    dpre_key = (dfeat_key.reshape(HEADS, tokens, HD) * slope(pre_key)).astype(jnp.bfloat16)
    dlin_queries = join_heads(plain("htf,hdf->htd", dpre_query, feature_map).astype(jnp.bfloat16))
    dlin_keys = join_heads(plain("htf,hdf->htd", dpre_key, feature_map).astype(jnp.bfloat16))
    map_terms = plain("htd,hte->hde", query_heads, dpre_query) + plain(
        "htd,hte->hde", key_heads, dpre_key
    )
    dprob = plain("hncd,hnsd->hncs", grad_heads, value_pairs)
    delta = jnp.sum(prob * dprob, axis=-1, keepdims=True)
    dscore = (prob * (dprob - delta) * inverse_root).astype(jnp.bfloat16)
    dwin_queries = join_heads(
        plain("hncs,hnsd->hncd", dscore, key_pairs).reshape(HEADS, tokens, HD).astype(jnp.bfloat16)
    )
    key_pair_grads = plain("hncs,hncd->hnsd", dscore, win_queries)
    value_pair_grads = plain("hncs,hncd->hnsd", prob_b, grad_heads)
    rim_keys, rim_values = (
        passed_along(key_pair_grads[:, 0, :WINDOW].astype(jnp.bfloat16), "seq", -1).astype(
            jnp.float32
        ),
        passed_along(value_pair_grads[:, 0, :WINDOW].astype(jnp.bfloat16), "seq", -1).astype(
            jnp.float32
        ),
    )
    dkey_win = fold_pairs(key_pair_grads, rim_keys)
    dvalue_win = fold_pairs(value_pair_grads, rim_values)
    dwin_keys = join_heads(dkey_win.reshape(HEADS, tokens, HD).astype(jnp.bfloat16))
    dvalue_all = join_heads(
        (dvalue_lin + dvalue_win).reshape(HEADS, tokens, HD).astype(jnp.bfloat16)
    )
    total_tokens = length * lax.axis_size("dp") * linear_queries.shape[0]
    map_grad = lax.psum(map_terms, ("seq", "dp")) * total_tokens ** (-0.5)
    return (
        attended[None],
        dlin_queries[None],
        dlin_keys[None],
        dwin_queries[None],
        dwin_keys[None],
        dvalue_all[None],
        map_grad,
    )


def solution(mesh):
    return jax.shard_map(
        on_device,
        mesh=mesh,
        in_specs=(
            P("dp", "seq", None),
            P("dp", "seq", None),
            P("dp", "seq", None),
            P("dp", "seq", None),
            P("dp", "seq", None),
            P("dp", "seq", None),
            P(),
        ),
        out_specs=(
            P("dp", "seq", None),
            P("dp", "seq", None),
            P("dp", "seq", None),
            P("dp", "seq", None),
            P("dp", "seq", None),
            P("dp", "seq", None),
            P(),
        ),
        check_vma=False,
    )
```

profile of v0, /device:TPU:0, one launch (start us, length us, event | category | flops | bytes accessed | tf_op | source)
XLA Modules:
  0.0 374.6 jit_solution(10899480268621206970)
XLA Ops:
  10.4 2.8 multiply_reduce_fusion
  13.3 3.2 reverse.4
  20.4 69.1 %all-gather.7.cloned.1.call-done = bf16[128,128,128]{2,1,0:T(8,128)(2,1)} async-done(((bf16[16,128,128]{2,1,0:T(8,128)(2,1)}), bf16[128,128,128]{2,1,0:T(8,128)(2,1)}) %all-gather.7.cloned.1.call-update) | async-done | bytes 4194320 | tf_op jit(solution)/shard_map/all_gather | solution.py:15
  89.6 9.2 %while.23 = (s32[]{:T(128)}, f32[16,128,128]{2,1,0:T(8,128)S(1)}, s32[]{:T(128)}, bf16[8,16,128,128]{3,2,1,0:T(8,128)(2,1)}, s32[]{:T(128)}, /*index=5*/s32[]{:T(128)}, s32[]{:T(128)}, s32[]{:T(128)}) while((s32[]{:T(128)}, f32[16,128,128]{2,1,0:T(8,128)S(1)}, s32[]{:T(128)}, bf16[8,16,128,128]{3,2,1,0:T(8,128)(2,1)}, s32[]{:T(128)}, ...), condition=%wide.region_8.9_spmd, body=%wide.region_7.8_spmd.sunk | while | flops 524294 | bytes 2621575 | solution.py:22
  100.8 2.3 fusion.14
  105.3 2.8 fusion.112
  113.7 2.2 collective-permute-start.1
  117.4 7.1 %collective-permute-done = bf16[16,64,128]{2,1,0:T(8,128)(2,1)} collective-permute-done((bf16[16,64,128]{2,1,0:T(8,128)(2,1)}, bf16[16,64,128]{2,1,0:T(8,128)(2,1)}, u32[]{:S(2)}, u32[]{:S(2)}) %collective-permute-start) | collective-permute-done | bytes 262176 | tf_op jit(solution)/shard_map/ppermute | solution.py:28
  125.6 2.9 collective-permute-done.1
  134.5 15.4 %fusion.51 = f32[16,2,128,128]{3,2,1,0:T(8,128)} fusion(bf16[16,2,64,128]{3,2,1,0:T(8,128)(2,1)} %bitcast.171, f32[16,2,64,128]{3,2,1,0:T(8,128)} %convolution_bitcast_fusion, f32[16,2,64,128]{3,2,1,0:T(8,128)} %get-tuple-element.151, f32[16,2,64]{2,1,0:T(2,128)S(1)} %get-tuple-element.150), kind=kOutput, calls=%fused_computation.71 | convolution fusion | flops 68946048 | bytes 4726784 | tf_op jit(solution)/shard_map/hncs,hncd->hnsd/dot_general | solution.py:32
  153.2 7.1 %fusion.83 = f32[16,2,128,128]{3,2,1,0:T(8,128)} fusion(bf16[16,2,64,128]{3,2,1,0:T(8,128)(2,1)S(1)} %bitcast.154, f32[16,2,64]{2,1,0:T(2,128)S(1)} %get-tuple-element.150, f32[16,2,64,128]{3,2,1,0:T(8,128)} %copy-done.20, pred[2,64,128]{2,1,0:T(8,128)(4,1)S(1)} %fusion.86), kind=kOutput, calls=%fused_computation.111 | convolution fusion | flops 68421760 | bytes 3694592 | tf_op jit(solution)/shard_map/hncs,hncd->hnsd/dot_general | solution.py:32
  162.0 14.3 %convolution_convert_fusion.2 = bf16[16,2,64,128]{3,2,1,0:T(8,128)(2,1)} fusion(f32[16,2,64,128]{3,2,1,0:T(8,128)} %convolution_bitcast_fusion, bf16[16,2,64,128]{3,2,1,0:T(8,128)(2,1)} %bitcast.160, bf16[16,2,64,128]{3,2,1,0:T(8,128)(2,1)} %bitcast.173, f32[16,2,64,128]{3,2,1,0:T(8,128)} %get-tuple-element.151, f32[16,2,64]{2,1,0:T(2,128)S(1)} %get-tuple-element.150), kind=kOutput, calls=%fused_computation.43 | convolution fusion | flops 71305344 | bytes 3678208 | tf_op jit(solution)/shard_map/hncs,hnsd->hncd/dot_general | solution.py:32
  179.6 2.2 copy.114
  181.7 2.1 broadcast_in_dim_reshape.21
  188.1 2.0 copy.118
  190.2 2.0 copy.127
  201.2 2.1 broadcast_in_dim_reshape.23
  204.6 2.0 copy.126
  206.6 2.8 fusion.115
  209.8 5.7 %fusion.17 = f32[16,2,64,128]{3,2,1,0:T(8,128)S(1)} fusion(f32[16,2,64,128]{3,2,1,0:T(8,128)} %fusion.115, bf16[16,2,64,128]{3,2,1,0:T(8,128)(2,1)S(1)} %bitcast.156, f32[1,16,128,128]{3,2,1,0:T(8,128)} %slice.49, f32[16,128,128]{2,1,0:T(8,128)S(1)} %get-tuple-element.86), kind=kOutput, calls=%fused_computation.20 | convolution fusion | flops 403963904 | bytes 4718592 | tf_op jit(solution)/shard_map/hncd,nhfd->hncf/dot_general | solution.py:36
  218.2 2.1 fusion.10
  222.8 2.9 fusion.33
  225.7 5.6 %fusion.35 = bf16[16,2,64,128]{3,2,1,0:T(8,128)(2,1)S(1)} fusion(f32[16,2,64,128]{3,2,1,0:T(8,128)} %fusion.33, bf16[16,2,64,128]{3,2,1,0:T(8,128)(2,1)S(1)} %bitcast.143, bf16[16,2,64,128]{3,2,1,0:T(8,128)(2,1)S(1)} %bitcast.169, f32[16,2,64]{2,1,0:T(2,128)S(1)} %get-tuple-element.150, f32[16,2,64,128]{3,2,1,0:T(8,128)} %copy-done.20, ...), kind=kOutput, calls=%fused_computation.40 | convolution fusion | flops 71043200 | bytes 3694592 | tf_op jit(solution)/shard_map/hncs,hnsd->hncd/dot_general | solution.py:32
  232.7 132.8 %all-reduce.3.cloned.1.call-done = f32[16,128,128]{1,2,0:T(8,128)} async-done(((f32[16,128,128]{1,2,0:T(8,128)}), f32[16,128,128]{1,2,0:T(8,128)}) %all-reduce.3.cloned.1.call-update) | async-done | bytes 1048592 | tf_op jit(solution)/shard_map/psum | solution.py:205
  (138 shorter events, 66.6 us)
Async XLA Ops:
  7.2 2.6 copy-start
  7.2 82.3 %all-gather.7.cloned.1.call-start = ((), (), s32[]{:S(2)}) async-start(), calls=%async_computation.2 | async-start | bytes 4718592 | tf_op jit(solution)/shard_map/all_gather | solution.py:15
  10.1 3.1 copy-start.7
  13.2 196.2 %all-gather.5.cloned.1.call-start = ((), (), s32[]{:S(2)}) async-start(), calls=%async_computation.1 | async-start | bytes 4718592 | tf_op jit(solution)/shard_map/all_gather | solution.py:15
  13.3 3.2 copy-start.29
  17.7 2.7 copy-start.17
  89.6 9.2 %copy-start.31 = (pred[2]{0:T(512)(128)(4,1)S(1)}, pred[2]{0:T(512)(128)(4,1)}, u32[]{:S(2)}) copy-start(pred[2]{0:T(512)(128)(4,1)} %constant.73.clone.1) | copy-start | bytes 10
  100.8 3.4 copy-start.1
  100.8 2.3 copy-start.5
  104.7 98.5 %copy-start.9 = (bf16[16,128,128]{2,1,0:T(8,128)(2,1)}, bf16[16,128,128]{2,1,0:T(8,128)(2,1)S(1)}, u32[]{:S(2)}) copy-start(bf16[16,128,128]{2,1,0:T(8,128)(2,1)S(1)} %get-tuple-element.132) | copy-start | bytes 1572868
  108.0 257.4 %all-reduce.3.cloned.1.call-start = ((), (), s32[]{:S(2)}) async-start(), calls=%async_computation | async-start | bytes 2097152 | tf_op jit(solution)/shard_map/psum | solution.py:205
  111.0 13.5 %collective-permute-start = (bf16[16,64,128]{2,1,0:T(8,128)(2,1)}, bf16[16,64,128]{2,1,0:T(8,128)(2,1)}, u32[]{:S(2)}, u32[]{:S(2)}) collective-permute-start(bf16[16,64,128]{2,1,0:T(8,128)(2,1)} %get-tuple-element.134), channel_id=1, source_target_pairs={{0,4},{4,8},{8,12},{12,16},{16,20},{20,24},{24,28},{1,5},{5,9},{9,... | collective-permute-start | bytes 786440 | tf_op jit(solution)/shard_map/ppermute | solution.py:28
  113.7 14.8 %collective-permute-start.1 = (bf16[16,64,128]{2,1,0:T(8,128)(2,1)}, bf16[16,64,128]{2,1,0:T(8,128)(2,1)}, u32[]{:S(2)}, u32[]{:S(2)}) collective-permute-start(bf16[16,64,128]{2,1,0:T(8,128)(2,1)} %get-tuple-element.138), channel_id=1, source_target_pairs={{0,4},{4,8},{8,12},{12,16},{16,20},{20,24},{24,28},{1,5},{5,9},{9,... | collective-permute-start | bytes 786440 | tf_op jit(solution)/shard_map/ppermute | solution.py:28
  116.0 8.6 %copy-start.28 = (bf16[16,64,128]{2,1,0:T(8,128)(2,1)S(1)}, bf16[16,64,128]{2,1,0:T(8,128)(2,1)}, u32[]{:S(2)}) copy-start(bf16[16,64,128]{2,1,0:T(8,128)(2,1)} %get-tuple-element.135) | copy-start | bytes 786436
  117.3 14.0 %copy-start.24 = (bf16[16,128,128]{2,1,0:T(8,128)(2,1)}, bf16[16,128,128]{2,1,0:T(8,128)(2,1)S(1)}, u32[]{:S(2)}) copy-start(bf16[16,128,128]{2,1,0:T(8,128)(2,1)S(1)} %copy.106) | copy-start | bytes 1572868
  125.5 6.6 %copy-start.25 = (bf16[16,128,128]{2,1,0:T(8,128)(2,1)}, bf16[16,128,128]{2,1,0:T(8,128)(2,1)S(1)}, u32[]{:S(2)}) copy-start(bf16[16,128,128]{2,1,0:T(8,128)(2,1)S(1)} %pad_maximum_fusion.6) | copy-start | bytes 1572868
  125.6 5.7 %copy-start.14 = (bf16[128,16,128]{2,0,1:T(8,128)(2,1)S(1)}, bf16[128,16,128]{2,0,1:T(8,128)(2,1)}, u32[]{:S(2)}) copy-start(bf16[128,16,128]{2,0,1:T(8,128)(2,1)} %copy-done.13) | copy-start | bytes 1572868
  151.7 33.2 %collective-permute-start.2 = (bf16[16,64,128]{2,1,0:T(8,128)(2,1)}, bf16[16,64,128]{2,1,0:T(8,128)(2,1)}, u32[]{:S(2)}, u32[]{:S(2)}) collective-permute-start(bf16[16,64,128]{2,1,0:T(8,128)(2,1)} %fusion.81), channel_id=1, source_target_pairs={{4,0},{8,4},{12,8},{16,12},{20,16},{24,20},{28,24},{5,1},{9,5},{13... | collective-permute-start | bytes 786440 | tf_op jit(solution)/shard_map/ppermute | solution.py:28
  178.3 13.9 %collective-permute-start.3 = (bf16[16,64,128]{2,1,0:T(8,128)(2,1)}, bf16[16,64,128]{2,1,0:T(8,128)(2,1)S(1)}, u32[]{:S(2)}, u32[]{:S(2)}) collective-permute-start(bf16[16,64,128]{2,1,0:T(8,128)(2,1)} %fusion.82), channel_id=1, source_target_pairs={{4,0},{8,4},{12,8},{16,12},{20,16},{24,20},{28,24},{5,1},{9,5},{13... | collective-permute-start | bytes 786440 | tf_op jit(solution)/shard_map/ppermute | solution.py:28
  196.0 4.1 %copy-start.3 = (f32[16,2,64,64]{3,2,1,0:T(8,128)}, f32[16,2,64,64]{3,2,1,0:T(8,128)S(1)}, u32[]{:S(2)}) copy-start(f32[16,2,64,64]{3,2,1,0:T(8,128)S(1)} %convolution_select_fusion.1) | copy-start | bytes 1572868
  209.8 5.7 %copy-start.8 = (f32[16,128,128]{2,1,0:T(8,128)S(1)}, f32[16,128,128]{2,1,0:T(8,128)}, u32[]{:S(2)}) copy-start(f32[16,128,128]{2,1,0:T(8,128)} %copy-done.7) | copy-start | bytes 3145732
  218.2 2.1 copy-start.18
  220.4 2.4 copy-start.4
  222.8 2.9 copy-start.22
  (15 other events, 21.2 us)
Sparse Core Ops, SparseCore 0:
  13.3 76.0 all-gather.6
  108.2 82.5 all-gather.4
  221.9 143.5 all-reduce.2
where the time goes:
time: 376 us; the launch traced here: 375 us
  waiting for transfers between devices  212 us (56%)
  matrix products  78.2 us (21%)
  local copies, waits for them, and re-layouts  41.8 us (11%)
  other arithmetic  20.9 us (6%)
  between operations  14.3 us (4%)
  starting transfers between devices  7.03 us (2%)
    psum x1, waiting for transfers between devices, on_device(): map_grad = lax.psum(map_terms, ('seq', 'dp')) * total_tokens ** (-0.5)  133 us
    all_gather x2, waiting for transfers between devices, entering(): gathered = lax.all_gather(shard.astype(jnp.bfloat16), axis)  69.1 us
    dot_general x16, matrix products, plain(): return jnp.einsum(form, left, right, preferred_element_type=jnp.float32)  58.2 us
    dot_general x8, matrix products, exact(): jnp.einsum(form, left.astype(jnp.float32), right.astype(jnp.float32), pre...  20 us
    unnamed x75, local copies, waits for them, and re-layouts  18 us
    ppermute x4, waiting for transfers between devices, passed_along(): return lax.ppermute(block, axis, route)  10.1 us
    add x7, other arithmetic, add_up(): return earlier + later  8.98 us
  transfers between devices with their start and end apart: 7, of which 4 were waited for; matrix products, arithmetic and copies ran while one was open for 26% of the time, Pallas kernels for 0%

commit v1 on v0

v1 whole, which is shorter than its diff:
```python
import jax
import jax.numpy as jnp
from jax import lax
from jax.experimental import pallas as pl
from jax.experimental.pallas import tpu as pltpu
from jax.sharding import PartitionSpec as P

HEADS = 16
HD = 128
WINDOW = 64
HALF = HEADS // 2
GROUP = 4
LANES = GROUP * HD
BF = jnp.bfloat16
F32 = jnp.float32
WIDE = HEADS * HD


def dot(left, right):
    return jnp.dot(left, right, preferred_element_type=F32)


def dot_nt(left, right):
    return lax.dot_general(left, right, (((1,), (1,)), ((), ())), preferred_element_type=F32)


def dot_tn(left, right):
    return lax.dot_general(left, right, (((0,), (0,)), ((), ())), preferred_element_type=F32)


def phi(before):
    return jnp.where(before > 0, before + 1.0, jnp.exp(jnp.minimum(before, 0.0)))


def col(head):
    return slice(head * HD, (head + 1) * HD)


def feature_kernel(off, lq, lk, v, g, fm, *rest):
    fq_out, fk_out, t_out = rest[-3:]
    for h in range(GROUP):
        c = col(h)
        w = fm[h]
        fq = phi(dot(lq[:, c], w)).astype(BF)
        fk = phi(dot(lk[:, c], w)).astype(BF)
        fq_out[:, c] = fq
        fk_out[:, c] = fk
        t_out[h, 0] = dot_tn(fk, v[:, c]).astype(BF)
        t_out[h, 1] = dot_tn(fq, g[:, c]).astype(BF)


def cost(flops, moved):
    return pl.CostEstimate(flops=flops, bytes_accessed=moved, transcendentals=0)


def features(off, lq, lk, v, g, fm, earlier):
    tokens = lq.shape[0]
    cols = pl.BlockSpec((tokens, LANES), lambda i, o: (0, o[0] + i))
    maps = pl.BlockSpec((GROUP, HD, HD), lambda i, o: (o[0] + i, 0, 0))
    kept = pl.BlockSpec(memory_space=pl.ANY)
    row = jax.ShapeDtypeStruct((tokens, WIDE), BF)
    return pl.pallas_call(
        feature_kernel,
        grid_spec=pltpu.PrefetchScalarGridSpec(
            num_scalar_prefetch=1,
            grid=(HALF // GROUP,),
            in_specs=[cols] * 4 + [maps] + [kept] * len(earlier),
            out_specs=[cols, cols, pl.BlockSpec((GROUP, 2, HD, HD), lambda i, o: (i, 0, 0, 0))],
        ),
        out_shape=[row, row, jax.ShapeDtypeStruct((HALF, 2, HD, HD), BF)],
        input_output_aliases={6: 0, 7: 1} if earlier else {},
        cost_estimate=cost(2 * HALF * 4 * tokens * HD * HD, 4_000_000),
        compiler_params=pltpu.CompilerParams(vmem_limit_bytes=32 * 1024 * 1024),
        name="features",
    )(off, lq, lk, v, g, fm, *earlier)


def local_kernel(
    info, wq, wk, v, g, rim_k, rim_v, fq, fk,
    att, dv, dfq, dfk, dwq, dwk, tail_k, send_k, send_v,
):
    tokens = wq.shape[0]
    scale = jnp.float32(1.0 / HD) / info[1].astype(F32)
    root = HD ** (-0.5)
    rows = lax.broadcasted_iota(jnp.int32, (tokens, 2 * WINDOW), 0)
    cols = lax.broadcasted_iota(jnp.int32, (tokens, 2 * WINDOW), 1)
    offset = cols - rows % WINDOW
    absent = (info[0] == 0) & (rows < WINDOW) & (cols < WINDOW)
    band = (offset >= 1) & (offset <= WINDOW) & jnp.logical_not(absent)
    causal_r = lax.broadcasted_iota(jnp.int32, (tokens, tokens), 0)
    causal_c = lax.broadcasted_iota(jnp.int32, (tokens, tokens), 1)
    causal = causal_r >= causal_c
    for h in range(GROUP):
        c = col(h)
        q, k, val, grad = wq[:, c], wk[:, c], v[:, c], g[:, c]
        kp = jnp.concatenate([rim_k[:, c], k[:WINDOW]], axis=0)
        vp = jnp.concatenate([rim_v[:, c], val[:WINDOW]], axis=0)
        score = jnp.concatenate([dot_nt(q[:WINDOW], kp), dot_nt(q[WINDOW:], k)], axis=0) * root
        score = jnp.where(band, score, -jnp.inf)
        expo = jnp.exp(score - jnp.max(score, axis=-1, keepdims=True))
        prob = expo / jnp.sum(expo, axis=-1, keepdims=True)
        prob_b = prob.astype(BF)
        mixed = dot_nt(grad, val)
        dprob = jnp.concatenate([dot_nt(grad[:WINDOW], vp), mixed[WINDOW:]], axis=0)
        delta = jnp.sum(prob * dprob, axis=-1, keepdims=True)
        dscore = (prob * (dprob - delta) * root).astype(BF)
        win = jnp.concatenate([dot(prob_b[:WINDOW], vp), dot(prob_b[WINDOW:], val)], axis=0)
        dwq[:, c] = jnp.concatenate(
            [dot(dscore[:WINDOW], kp), dot(dscore[WINDOW:], k)], axis=0
        ).astype(BF)
        dk0 = dot_tn(dscore[:WINDOW], q[:WINDOW])
        dk1 = dot_tn(dscore[WINDOW:], q[WINDOW:])
        dv0 = dot_tn(prob_b[:WINDOW], grad[:WINDOW])
        dv1 = dot_tn(prob_b[WINDOW:], grad[WINDOW:])
        send_k[:, c] = dk0[:WINDOW].astype(BF)
        send_v[:, c] = dv0[:WINDOW].astype(BF)
        dwk[:, c] = jnp.concatenate([dk0[WINDOW:] + dk1[:WINDOW], dk1[WINDOW:]], axis=0).astype(BF)
        tail_k[:, c] = dk1[WINDOW:]
        dv_win = jnp.concatenate([dv0[WINDOW:] + dv1[:WINDOW], dv1[WINDOW:]], axis=0)
        q_feat, k_feat = fq[:, c], fk[:, c]
        scores = jnp.where(causal, dot_nt(q_feat, k_feat), 0.0).astype(BF)
        mixed = jnp.where(causal, mixed, 0.0).astype(BF)
        att[:, c] = dot(scores, val) * scale + win
        dv[:, c] = dot_tn(scores, grad) * scale + dv_win
        dfq[:, c] = dot(mixed, k_feat)
        dfk[:, c] = dot_tn(mixed, q_feat)


def local_part(info, wq, wk, v, g, rim_k, rim_v, fq, fk):
    tokens = wq.shape[0]
    cols = pl.BlockSpec((tokens, LANES), lambda i, o: (0, i))
    rims = pl.BlockSpec((WINDOW, LANES), lambda i, o: (0, i))
    wide = jax.ShapeDtypeStruct((tokens, WIDE), F32)
    narrow = jax.ShapeDtypeStruct((tokens, WIDE), BF)
    rim = jax.ShapeDtypeStruct((WINDOW, WIDE), BF)
    return pl.pallas_call(
        local_kernel,
        grid_spec=pltpu.PrefetchScalarGridSpec(
            num_scalar_prefetch=1,
            grid=(HEADS // GROUP,),
            in_specs=[cols] * 4 + [rims] * 2 + [cols] * 2,
            out_specs=[cols] * 6 + [rims] * 3,
        ),
        out_shape=[wide] * 4 + [narrow] * 2 + [jax.ShapeDtypeStruct((WINDOW, WIDE), F32), rim, rim],
        cost_estimate=cost(2 * HEADS * 15 * tokens * HD * HD, 10_000_000),
        compiler_params=pltpu.CompilerParams(vmem_limit_bytes=32 * 1024 * 1024),
        name="local_part",
    )(info, wq, wk, v, g, rim_k, rim_v, fq, fk)


def state_kernel(off, lq, lk, v, g, fm, fq, fk, state, att_p, dv_p, dfq_p, dfk_p, *rest):
    att, dlq, dlk, dv, tail_v, dmap = rest[-6:]
    scale = jnp.float32(1.0 / HD) / off[1].astype(F32)
    for h in range(GROUP):
        c = col(h)
        before, after = state[h, 0], state[h, 1]
        w = fm[h]
        q_feat, k_feat, val, grad = fq[:, c], fk[:, c], v[:, c], g[:, c]
        dfq = (dfq_p[:, c] + dot_nt(grad, before)) * scale
        dfk = (dfk_p[:, c] + dot_nt(val, after)) * scale
        dpq = (dfq * jnp.minimum(q_feat.astype(F32), 1.0)).astype(BF)
        dpk = (dfk * jnp.minimum(k_feat.astype(F32), 1.0)).astype(BF)
        dmap[h] = (dot_tn(lq[:, c], dpq) + dot_tn(lk[:, c], dpk)).astype(BF)
        dlq[:, c] = dot_nt(dpq, w).astype(BF)
        dlk[:, c] = dot_nt(dpk, w).astype(BF)
        att[:, c] = (att_p[:, c] + dot(q_feat, before) * scale).astype(BF)
        grad_v = dv_p[:, c] + dot(k_feat, after) * scale
        dv[:, c] = grad_v.astype(BF)
        tail_v[:, c] = grad_v[WINDOW:]


def state_part(off, lq, lk, v, g, fm, fq, fk, state, parts, earlier):
    tokens = lq.shape[0]
    cols = pl.BlockSpec((tokens, LANES), lambda i, o: (0, o[0] + i))
    tails = pl.BlockSpec((WINDOW, LANES), lambda i, o: (0, o[0] + i))
    maps = pl.BlockSpec((GROUP, HD, HD), lambda i, o: (o[0] + i, 0, 0))
    own = pl.BlockSpec((GROUP, HD, HD), lambda i, o: (i, 0, 0))
    states = pl.BlockSpec((GROUP, 2, HD, HD), lambda i, o: (i, 0, 0, 0))
    kept = pl.BlockSpec(memory_space=pl.ANY)
    narrow = jax.ShapeDtypeStruct((tokens, WIDE), BF)
    return pl.pallas_call(
        state_kernel,
        grid_spec=pltpu.PrefetchScalarGridSpec(
            num_scalar_prefetch=1,
            grid=(HALF // GROUP,),
            in_specs=[cols] * 4 + [maps] + [cols] * 2 + [states] + [cols] * 4 + [kept] * len(earlier),
            out_specs=[cols] * 4 + [tails, own],
        ),
        out_shape=[narrow] * 4
        + [
            jax.ShapeDtypeStruct((WINDOW, WIDE), F32),
            jax.ShapeDtypeStruct((HALF, HD, HD), BF),
        ],
        input_output_aliases={13 + i: i for i in range(5)} if earlier else {},
        cost_estimate=cost(2 * HALF * 8 * tokens * HD * HD, 8_000_000),
        compiler_params=pltpu.CompilerParams(vmem_limit_bytes=32 * 1024 * 1024),
        name="state_part",
    )(off, lq, lk, v, g, fm, fq, fk, state, *parts, *earlier)


def finish_kernel(tail_k, rim_k, tail_v, rim_v, k_in, v_in, dk, dv):
    dk[...] = (tail_k[...] + rim_k[...].astype(F32)).astype(BF)
    dv[...] = (tail_v[...] + rim_v[...].astype(F32)).astype(BF)


def finish(tail_k, rim_k, tail_v, rim_v, dwk, dv):
    rims = pl.BlockSpec((WINDOW, WIDE), lambda i: (0, 0))
    last = pl.BlockSpec((WINDOW, WIDE), lambda i: (dwk.shape[0] // WINDOW - 1, 0))
    kept = pl.BlockSpec(memory_space=pl.ANY)
    row = jax.ShapeDtypeStruct(dwk.shape, BF)
    return pl.pallas_call(
        finish_kernel,
        grid=(1,),
        in_specs=[rims] * 4 + [kept] * 2,
        out_specs=[last, last],
        out_shape=[row, row],
        input_output_aliases={4: 0, 5: 1},
        cost_estimate=cost(1_000_000, 2_500_000),
        compiler_params=pltpu.CompilerParams(vmem_limit_bytes=32 * 1024 * 1024),
        name="finish",
    )(tail_k, rim_k, tail_v, rim_v, dwk, dv)


def flipped(block, bit):
    count = lax.axis_size("seq")
    return lax.ppermute(block, "seq", [(i, i ^ bit) for i in range(count)])


def flat_flipped(block, seq_bits, dp_bits):
    rows, width = lax.axis_size("seq"), lax.axis_size("dp")
    route = [
        (s * width + d, (s ^ seq_bits) * width + (d ^ dp_bits))
        for s in range(rows)
        for d in range(width)
    ]
    return lax.ppermute(block, ("seq", "dp"), route)


def passed_along(block, distance):
    devices = range(lax.axis_size("seq"))
    route = [(i - distance, i) for i in devices if i - distance in devices]
    return lax.ppermute(block, "seq", route)


def spread(block, level):
    count = lax.axis_size("seq")
    size = 2 << level
    total = None
    for turn in range(1 << level):
        route = []
        for base in range(0, count // 2, size):
            low, high = base + size // 2 - 1, base + size // 2
            for parity in range(2):
                route.append((2 * low + parity, 2 * (high + turn) + parity))
                route.append((2 * high + parity, 2 * (low - turn) + parity))
        came = lax.ppermute(block, "seq", route)
        total = came if total is None else total + came
    return total


def states(kept, came, place):
    odd = place % 2
    level_count = (lax.axis_size("seq") // 2).bit_length() - 1
    kept, came = kept.astype(F32), came.astype(F32)
    pair = kept + came
    low = jnp.zeros_like(pair[:, 0])
    high = jnp.zeros_like(low)
    for level in range(level_count):
        upper = ((place // 2) >> level) % 2 == 1
        send = jnp.where(upper, pair[:, 1] + high, pair[:, 0] + low).astype(BF)
        got = spread(send, level).astype(F32)
        low = low + jnp.where(upper, got, 0.0)
        high = high + jnp.where(upper, 0.0, got)
    first = odd == 0
    mine = jnp.stack(
        [low + jnp.where(first, 0.0, came[:, 0]), high + jnp.where(first, came[:, 1], 0.0)], axis=1
    )
    others = jnp.stack(
        [low + jnp.where(first, kept[:, 0], 0.0), high + jnp.where(first, 0.0, kept[:, 1])], axis=1
    )
    return mine.astype(BF), others.astype(BF)


def half_of(block, which):
    size = block.shape[0] // 2
    return lax.dynamic_slice_in_dim(block, which * size, size, 0)


def joined(own, other, which):
    return jnp.where(
        which == 0, jnp.concatenate([own, other], 0), jnp.concatenate([other, own], 0)
    )


def map_sum(own, other, odd, total_tokens):
    core = lax.axis_index("dp") % 2
    far = lax.axis_index("dp") // 2
    own, other = own.reshape(2, 2, 2, HD, HD), other.reshape(2, 2, 2, HD, HD)

    def at(block, index):
        return lax.dynamic_index_in_dim(block, index, 0, False)

    both = jnp.stack([own, other], axis=1)
    swapped = flat_flipped(at(both, 1 - core), 0, 1)
    mine = (at(both, core).astype(F32) + swapped.astype(F32)).astype(BF)
    near, beyond = mine[0], mine[1]
    a = flat_flipped(at(beyond, far), 1, 0)
    b = flat_flipped(at(near, 1 - far), 0, 2)
    c = flat_flipped(at(beyond, 1 - far), 1, 2)
    total = at(near, far).astype(F32) + a.astype(F32) + b.astype(F32) + c.astype(F32)
    bit = 2
    while bit < lax.axis_size("seq"):
        sent = total.astype(BF)
        total = sent.astype(F32) + flat_flipped(sent, bit, 0).astype(F32)
        bit *= 2
    done = total.astype(BF)
    a = flat_flipped(done, 1, 0)
    b = flat_flipped(done, 0, 2)
    c = flat_flipped(done, 1, 2)
    quarter = jnp.stack([joined(done[None], b[None], far), joined(a[None], c[None], far)], axis=0)
    swapped = flat_flipped(quarter, 0, 1)
    halves = jnp.where(core == 0, jnp.stack([quarter, swapped], 1), jnp.stack([swapped, quarter], 1))
    whole = jnp.where(odd == 0, halves, halves[::-1])
    return whole.reshape(HEADS, HD, HD).astype(F32) * total_tokens ** (-0.5)


def on_device(
    linear_queries, linear_keys, window_queries, window_keys, values, cotangent, feature_map
):
    tokens = linear_queries.shape[1]
    length = tokens * lax.axis_size("seq")
    total_tokens = length * lax.axis_size("dp") * linear_queries.shape[0]
    place = lax.axis_index("seq")
    odd = place % 2
    lq, lk, wq, wk, v, g = (
        x[0]
        for x in (linear_queries, linear_keys, window_queries, window_keys, values, cotangent)
    )
    steps = HALF // GROUP
    scalar = jnp.int32(length)
    own = jnp.stack([odd * steps, scalar]).astype(jnp.int32)
    other = jnp.stack([(1 - odd) * steps, scalar]).astype(jnp.int32)
    fq, fk, sums_other = features(other, lq, lk, v, g, feature_map, ())
    came = flipped(sums_other, 1)
    fq, fk, sums_own = features(own, lq, lk, v, g, feature_map, (fq, fk))
    came, tail_in = lax.optimization_barrier(
        (came, (wk[tokens - WINDOW :], v[tokens - WINDOW :]))
    )
    rim_k, rim_v = (passed_along(x, 1) for x in tail_in)
    info = jnp.stack([place, scalar]).astype(jnp.int32)
    local = local_part(info, wq, wk, v, g, rim_k, rim_v, fq, fk)
    att_p, dv_p, dfq_p, dfk_p, dwq, dwk, tail_k, send_k, send_v = local
    parts = (att_p, dv_p, dfq_p, dfk_p)
    mine, others = states(sums_own, came, place)
    state_other = flipped(others, 1)
    outs = state_part(own, lq, lk, v, g, feature_map, fq, fk, mine, parts, ())
    state_other, sends = lax.optimization_barrier((state_other, (send_k, send_v)))
    back_k, back_v = (passed_along(x, -1) for x in sends)
    map_own = outs[5]
    outs = state_part(other, lq, lk, v, g, feature_map, fq, fk, state_other, parts, outs[:5])
    attended, dlq, dlk, dv, tail_v, map_other = outs
    map_grad = map_sum(map_own, map_other, odd, total_tokens)
    dwk, dv = finish(tail_k, back_k, tail_v, back_v, dwk, dv)
    return attended[None], dlq[None], dlk[None], dwq[None], dwk[None], dv[None], map_grad


def solution(mesh):
    row = P("dp", "seq", None)
    return jax.shard_map(
        on_device,
        mesh=mesh,
        in_specs=(row,) * 6 + (P(),),
        out_specs=(row,) * 6 + (P(),),
        check_vma=False,
    )
```

time: 376 us -> 147 us (0.39)
  waiting for transfers between devices: 212 us -> 62.5 us
  matrix products: 78.2 us -> 0 us
  Pallas kernels: 0 us -> 29.6 us
  local copies, waits for them, and re-layouts: 41.8 us -> 17.5 us
  starting transfers between devices: 7.03 us -> 26.9 us
  between operations: 14.3 us -> 1 us
  other arithmetic: 20.9 us -> 8.82 us
    psum x1 -> x0, waiting for transfers between devices: 133 us -> none  [on_device(): map_grad = lax.psum(map_terms, ('seq', 'dp')) * total_tokens ** (-0.5)]
    dot_general x24 -> x0, matrix products: 78.2 us -> none  [the longest x16 58.2 us: plain(): return jnp.einsum(form, left, right, preferred_element_type=jnp.float32)]
    all_gather x2 -> x0, waiting for transfers between devices: 69.1 us -> none  [entering(): gathered = lax.all_gather(shard.astype(jnp.bfloat16), axis)]
    ppermute x4 -> x19, waiting for transfers between devices: 10.1 us -> 62.5 us  [the longest x10 24 us: flat_flipped(): return lax.ppermute(block, ('seq', 'dp'), route)]
    pallas_call x0 -> x6, Pallas kernels: none -> 29.6 us  [the longest x1 14.5 us: local_part(): pl.pallas_call(local_kernel, grid_spec=pltpu.PrefetchScalarGridSpec(num_s...]
    ppermute x4 -> x19, starting transfers between devices: 6.91 us -> 26.9 us  [the longest x10 10.4 us: flat_flipped(): return lax.ppermute(block, ('seq', 'dp'), route)]
    another operation x9 -> x1, local copies, waits for them, and re-layouts: 8.96 us -> 0.04 us  [states(): jnp.stack([low + jnp.where(first, 0.0, came[:, 0]), high + jnp.where(firs...]
    add x8 -> x1, other arithmetic: 8.99 us -> 1.21 us  [states(): pair = kept + came]
  transfers between devices with their start and end apart: 7 -> 19, of which waited for: 4 -> 13; matrix products, arithmetic and copies ran while one was open for 26% -> 2% of each run, Pallas kernels for 0% -> 15%
where the time goes in v1:
time: 147 us; the launch traced here: 146 us
  waiting for transfers between devices  62.5 us (43%)
  Pallas kernels  29.6 us (20%)
  starting transfers between devices  26.9 us (18%)
  local copies, waits for them, and re-layouts  17.5 us (12%)
  other arithmetic  8.82 us (6%)
    ppermute x10, waiting for transfers between devices, flat_flipped(): return lax.ppermute(block, ('seq', 'dp'), route)  24 us
    ppermute x3, waiting for transfers between devices, spread(): came = lax.ppermute(block, 'seq', route)  17.3 us
    unnamed x66, local copies, waits for them, and re-layouts  14.6 us
    pallas_call x1, Pallas kernels, local_part(): pl.pallas_call(local_kernel, grid_spec=pltpu.PrefetchScalarGridSpec(num_s...  14.5 us
    ppermute x4, waiting for transfers between devices, passed_along(): return lax.ppermute(block, 'seq', route)  14 us
    ppermute x10, starting transfers between devices, flat_flipped(): return lax.ppermute(block, ('seq', 'dp'), route)  10.4 us
    pallas_call x2, Pallas kernels, state_part(): pl.pallas_call(state_kernel, grid_spec=pltpu.PrefetchScalarGridSpec(num_s...  8.65 us
    ppermute x4, starting transfers between devices, passed_along(): return lax.ppermute(block, 'seq', route)  8.24 us
  transfers between devices with their start and end apart: 19, of which 13 were waited for; matrix products, arithmetic and copies ran while one was open for 2% of the time, Pallas kernels for 15%

profile of v1, /device:TPU:0, one launch (start us, length us, event | category | flops | bytes accessed | tf_op | source)
XLA Modules:
  0.0 146.3 jit_solution(10703882448381264344)
XLA Ops:
  5.9 2.8 %features.2 = (bf16[128,2048]{1,0:T(8,128)(2,1)S(1)}, bf16[128,2048]{1,0:T(8,128)(2,1)S(1)}, bf16[8,2,128,128]{3,2,1,0:T(8,128)(2,1)S(1)}) custom-call(s32[2]{0:T(128)S(1)} %pad_add_fusion.2.off, bf16[128,2048]{1,0:T(8,128)(2,1)S(1)} %bitcast.104, bf16[128,2048]{1,0:T(8,128)(2,1)S(1)} %bitcast.108, bf16[128,2048]{1,0:T(8,128)(2,1)S(1)} %bitcast.99, ...), custom_call_target="tpu_custom_call" | custom-call | flops 134217728 | bytes 4000000 | tf_op jit(solution)/shard_map/features/pallas_call | solution.py:62
  9.7 2.9 %collective-permute-start = (bf16[8,2,128,128]{3,2,0,1:T(8,128)(2,1)}, bf16[8,2,128,128]{3,2,0,1:T(8,128)(2,1)}, u32[]{:S(2)}, u32[]{:S(2)}) collective-permute-start(bf16[8,2,128,128]{3,2,0,1:T(8,128)(2,1)} %copy.24), channel_id=1, source_target_pairs={{0,4},{4,0},{8,12},{12,8},{16,20},{20,16},{24,28},{28,24},{1,5},{5... | collective-permute-start | bytes 1572872 | tf_op jit(solution)/shard_map/ppermute | solution.py:226
  13.8 2.8 %features.3 = (bf16[128,2048]{1,0:T(8,128)(2,1)S(1)}, bf16[128,2048]{1,0:T(8,128)(2,1)S(1)}, bf16[8,2,128,128]{3,2,1,0:T(8,128)(2,1)S(1)}) custom-call(s32[2]{0:T(128)S(1)} %get-tuple-element.89.off, bf16[128,2048]{1,0:T(8,128)(2,1)S(1)} %bitcast.105, bf16[128,2048]{1,0:T(8,128)(2,1)S(1)} %bitcast.109, ...), custom_call_target="tpu_custom_call", output_to_operand_aliasing={{0}: (6, {}), {1}: (7, {})} | custom-call | flops 134217728 | bytes 4000000 | tf_op jit(solution)/shard_map/features/pallas_call | solution.py:62
  17.7 7.2 %collective-permute-done = bf16[8,2,128,128]{3,2,0,1:T(8,128)(2,1)} collective-permute-done((bf16[8,2,128,128]{3,2,0,1:T(8,128)(2,1)}, bf16[8,2,128,128]{3,2,0,1:T(8,128)(2,1)}, u32[]{:S(2)}, u32[]{:S(2)}) %collective-permute-start) | collective-permute-done | bytes 524320 | tf_op jit(solution)/shard_map/ppermute | solution.py:226
  27.9 1.8 %collective-permute-start.1 = (bf16[8,128,128]{2,1,0:T(8,128)(2,1)}, bf16[8,128,128]{2,1,0:T(8,128)(2,1)S(1)}, u32[]{:S(2)}, u32[]{:S(2)}) collective-permute-start(bf16[8,128,128]{2,1,0:T(8,128)(2,1)} %select_convert_fusion), channel_id=1, source_target_pairs={{0,8},{8,0},{4,12},{12,4},{16,24},{24,16},{20,28},{28,20},{1,9},{9... | collective-permute-start | bytes 786440 | tf_op jit(solution)/shard_map/ppermute | solution.py:256
  29.7 5.9 %collective-permute-done.1 = bf16[8,128,128]{2,1,0:T(8,128)(2,1)S(1)} collective-permute-done((bf16[8,128,128]{2,1,0:T(8,128)(2,1)}, bf16[8,128,128]{2,1,0:T(8,128)(2,1)S(1)}, u32[]{:S(2)}, u32[]{:S(2)}) %collective-permute-start.1) | collective-permute-done | bytes 262176 | tf_op jit(solution)/shard_map/ppermute | solution.py:256
  40.2 11.5 %collective-permute-done.3 = bf16[8,128,128]{2,1,0:T(8,128)(2,1)S(1)} collective-permute-done((bf16[8,128,128]{2,1,0:T(8,128)(2,1)S(1)}, bf16[8,128,128]{2,1,0:T(8,128)(2,1)S(1)}, u32[]{:S(2)}, u32[]{:S(2)}) %collective-permute-start.3) | collective-permute-done | bytes 262176 | tf_op jit(solution)/shard_map/ppermute | solution.py:256
  55.8 3.2 %collective-permute-start.5 = (bf16[64,2048]{1,0:T(8,128)(2,1)}, bf16[64,2048]{1,0:T(8,128)(2,1)}, u32[]{:S(2)}, u32[]{:S(2)}) collective-permute-start(bf16[64,2048]{1,0:T(8,128)(2,1)} %get-tuple-element.49), channel_id=1, source_target_pairs={{0,4},{4,8},{8,12},{12,16},{16,20},{20,24},{24,28},{1,5},{5,9},{9,... | collective-permute-start | bytes 786440 | tf_op jit(solution)/shard_map/ppermute | solution.py:242
  59.0 2.5 %collective-permute-start.6 = (bf16[64,2048]{1,0:T(8,128)(2,1)S(1)}, bf16[64,2048]{1,0:T(8,128)(2,1)}, u32[]{:S(2)}, u32[]{:S(2)}) collective-permute-start(bf16[64,2048]{1,0:T(8,128)(2,1)S(1)} %copy-done.32), channel_id=1, source_target_pairs={{0,4},{4,8},{8,12},{12,16},{16,20},{20,24},{24,28},{1,5},{5,9},{9,... | collective-permute-start | bytes 786440 | tf_op jit(solution)/shard_map/ppermute | solution.py:242
  61.5 11.2 %collective-permute-done.5.rim_k = bf16[64,2048]{1,0:T(8,128)(2,1)} collective-permute-done((bf16[64,2048]{1,0:T(8,128)(2,1)}, bf16[64,2048]{1,0:T(8,128)(2,1)}, u32[]{:S(2)}, u32[]{:S(2)}) %collective-permute-start.5) | collective-permute-done | bytes 262176 | tf_op jit(solution)/shard_map/ppermute | solution.py:242
  72.8 2.7 %collective-permute-done.6.rim_v = bf16[64,2048]{1,0:T(8,128)(2,1)} collective-permute-done((bf16[64,2048]{1,0:T(8,128)(2,1)S(1)}, bf16[64,2048]{1,0:T(8,128)(2,1)}, u32[]{:S(2)}, u32[]{:S(2)}) %collective-permute-start.6) | collective-permute-done | bytes 262176 | tf_op jit(solution)/shard_map/ppermute | solution.py:242
  78.6 14.5 %local_part.1 = (f32[128,2048]{1,0:T(8,128)S(1)}, f32[128,2048]{1,0:T(8,128)S(1)}, f32[128,2048]{1,0:T(8,128)S(1)}, f32[128,2048]{1,0:T(8,128)S(1)}, bf16[128,20...) custom-call(s32[2]{0:T(128)S(1)} %get-tuple-element.88.info, ...), custom_call_target="tpu_custom_call" | custom-call | flops 1006632960 | bytes 10000000 | tf_op jit(solution)/shard_map/local_part/pallas_call | solution.py:136
  94.7 4.0 %state_part.2 = (bf16[128,2048]{1,0:T(8,128)(2,1)}, bf16[128,2048]{1,0:T(8,128)(2,1)}, bf16[128,2048]{1,0:T(8,128)(2,1)}, bf16[128,2048]{1,0:T(8,128)(2,1)}, f32...) custom-call(s32[2]{0:T(128)S(1)} %get-tuple-element.89.off, bf16[128,2048]{1,0:T(8,128)(2,1)S(1)} %bitcast.106, ...), custom_call_target="tpu_custom_call" | custom-call | flops 268435456 | bytes 8000000 | tf_op jit(solution)/shard_map/state_part/pallas_call | solution.py:181
  98.7 4.6 %state_part.3 = (bf16[128,2048]{1,0:T(8,128)(2,1)}, bf16[128,2048]{1,0:T(8,128)(2,1)}, bf16[128,2048]{1,0:T(8,128)(2,1)}, bf16[128,2048]{1,0:T(8,128)(2,1)}, f32...) custom-call(s32[2]{0:T(128)S(1)} %pad_add_fusion.2.off, ...), custom_call_target="tpu_custom_call", output_to_operand_aliasing={{0}: (13, {}), {1}: (14, {}), {2}: (15, {}), {3}: (16, {}),... | custom-call | flops 268435456 | bytes 8000000 | tf_op jit(solution)/shard_map/state_part/pallas_call | solution.py:181
  104.9 1.5 %collective-permute-done.9 = bf16[2,2,2,128,128]{4,3,2,1,0:T(8,128)(2,1)S(1)} collective-permute-done((bf16[2,2,2,128,128]{4,3,2,1,0:T(8,128)(2,1)S(1)}, bf16[2,2,2,128,128]{4,3,2,1,0:T(8,128)(2,1)S(1)}, u32[]{:S(2)}, u32[]{:S(2)}) %collective-permute-start.9) | collective-permute-done | bytes 262176 | tf_op jit(solution)/shard_map/ppermute | solution.py:236
  107.4 1.6 %collective-permute-start.11 = (bf16[2,128,128]{2,1,0:T(8,128)(2,1)S(1)}, bf16[2,128,128]{2,1,0:T(8,128)(2,1)S(1)}, u32[]{:S(2)}, u32[]{:S(2)}) collective-permute-start(bf16[2,128,128]{2,1,0:T(8,128)(2,1)S(1)} %dynamic-slice_bitcast_fusion.1), channel_id=1, source_target_pairs={{0,2},{1,3},{2,0},{3,1},{4,6},{5,7},{6,4},{7,5},{8,10},{9,11},{10,... | collective-permute-start | bytes 196616 | tf_op jit(solution)/shard_map/ppermute | solution.py:236
  109.1 2.7 %collective-permute-start.10 = (bf16[2,128,128]{2,1,0:T(8,128)(2,1)S(1)}, bf16[2,128,128]{2,1,0:T(8,128)(2,1)S(1)}, u32[]{:S(2)}, u32[]{:S(2)}) collective-permute-start(bf16[2,128,128]{2,1,0:T(8,128)(2,1)S(1)} %get-tuple-element.86), channel_id=1, source_target_pairs={{0,4},{1,5},{2,6},{3,7},{4,0},{5,1},{6,2},{7,3},{8,12},{9,13},{10,... | collective-permute-start | bytes 196616 | tf_op jit(solution)/shard_map/ppermute | solution.py:236
  111.8 2.4 %collective-permute-done.10 = bf16[2,128,128]{2,1,0:T(8,128)(2,1)S(1)} collective-permute-done((bf16[2,128,128]{2,1,0:T(8,128)(2,1)S(1)}, bf16[2,128,128]{2,1,0:T(8,128)(2,1)S(1)}, u32[]{:S(2)}, u32[]{:S(2)}) %collective-permute-start.10) | collective-permute-done | bytes 65568 | tf_op jit(solution)/shard_map/ppermute | solution.py:236
  114.2 2.7 %collective-permute-done.12 = bf16[2,128,128]{2,1,0:T(8,128)(2,1)S(1)} collective-permute-done((bf16[2,128,128]{2,1,0:T(8,128)(2,1)S(1)}, bf16[2,128,128]{2,1,0:T(8,128)(2,1)S(1)}, u32[]{:S(2)}, u32[]{:S(2)}) %collective-permute-start.12) | collective-permute-done | bytes 65568 | tf_op jit(solution)/shard_map/ppermute | solution.py:236
  117.0 4.3 %collective-permute-done.13 = bf16[2,128,128]{2,1,0:T(8,128)(2,1)S(1)} collective-permute-done((bf16[2,128,128]{2,1,0:T(8,128)(2,1)S(1)}, bf16[2,128,128]{2,1,0:T(8,128)(2,1)S(1)}, u32[]{:S(2)}, u32[]{:S(2)}) %collective-permute-start.13) | collective-permute-done | bytes 65568 | tf_op jit(solution)/shard_map/ppermute | solution.py:236
  122.4 4.4 %collective-permute-done.14 = bf16[2,128,128]{2,1,0:T(8,128)(2,1)S(1)} collective-permute-done((bf16[2,128,128]{2,1,0:T(8,128)(2,1)S(1)}, bf16[2,128,128]{2,1,0:T(8,128)(2,1)S(1)}, u32[]{:S(2)}, u32[]{:S(2)}) %collective-permute-start.14) | collective-permute-done | bytes 65568 | tf_op jit(solution)/shard_map/ppermute | solution.py:236
  130.0 3.3 %collective-permute-start.16 = (bf16[2,128,128]{2,1,0:T(8,128)(2,1)S(1)}, bf16[2,128,128]{2,1,0:T(8,128)(2,1)S(1)}, u32[]{:S(2)}, u32[]{:S(2)}) collective-permute-start(bf16[2,128,128]{2,1,0:T(8,128)(2,1)S(1)} %add_convert_fusion), channel_id=1, source_target_pairs={{0,4},{1,5},{2,6},{3,7},{4,0},{5,1},{6,2},{7,3},{8,12},{9,13},{10,... | collective-permute-start | bytes 196616 | tf_op jit(solution)/shard_map/ppermute | solution.py:236
  134.3 7.1 %collective-permute-done.16 = bf16[2,128,128]{2,1,0:T(8,128)(2,1)S(1)} collective-permute-done((bf16[2,128,128]{2,1,0:T(8,128)(2,1)S(1)}, bf16[2,128,128]{2,1,0:T(8,128)(2,1)S(1)}, u32[]{:S(2)}, u32[]{:S(2)}) %collective-permute-start.16) | collective-permute-done | bytes 65568 | tf_op jit(solution)/shard_map/ppermute | solution.py:236
  141.4 1.5 %collective-permute-done.17 = bf16[2,128,128]{2,1,0:T(8,128)(2,1)S(1)} collective-permute-done((bf16[2,128,128]{2,1,0:T(8,128)(2,1)S(1)}, bf16[2,128,128]{2,1,0:T(8,128)(2,1)S(1)}, u32[]{:S(2)}, u32[]{:S(2)}) %collective-permute-start.17) | collective-permute-done | bytes 65568 | tf_op jit(solution)/shard_map/ppermute | solution.py:236
  (114 shorter events, 36.1 us)
Async XLA Ops:
  9.7 15.2 %collective-permute-start = (bf16[8,2,128,128]{3,2,0,1:T(8,128)(2,1)}, bf16[8,2,128,128]{3,2,0,1:T(8,128)(2,1)}, u32[]{:S(2)}, u32[]{:S(2)}) collective-permute-start(bf16[8,2,128,128]{3,2,0,1:T(8,128)(2,1)} %copy.24), channel_id=1, source_target_pairs={{0,4},{4,0},{8,12},{12,8},{16,20},{20,16},{24,28},{28,24},{1,5},{5... | collective-permute-start | bytes 1572872 | tf_op jit(solution)/shard_map/ppermute | solution.py:226
  27.9 7.7 %collective-permute-start.1 = (bf16[8,128,128]{2,1,0:T(8,128)(2,1)}, bf16[8,128,128]{2,1,0:T(8,128)(2,1)S(1)}, u32[]{:S(2)}, u32[]{:S(2)}) collective-permute-start(bf16[8,128,128]{2,1,0:T(8,128)(2,1)} %select_convert_fusion), channel_id=1, source_target_pairs={{0,8},{8,0},{4,12},{12,4},{16,24},{24,16},{20,28},{28,20},{1,9},{9... | collective-permute-start | bytes 786440 | tf_op jit(solution)/shard_map/ppermute | solution.py:256
  29.7 9.2 %copy-start.18 = (bf16[8,2,128,128]{3,2,1,0:T(8,128)(2,1)S(1)}, bf16[8,2,128,128]{3,2,1,0:T(8,128)(2,1)}, u32[]{:S(2)}) copy-start(bf16[8,2,128,128]{3,2,1,0:T(8,128)(2,1)} %copy-done.17) | copy-start | bytes 1572868
  36.9 3.2 %collective-permute-start.2 = (bf16[8,128,128]{2,1,0:T(8,128)(2,1)S(1)}, bf16[8,128,128]{2,1,0:T(8,128)(2,1)S(1)}, u32[]{:S(2)}, u32[]{:S(2)}) collective-permute-start(bf16[8,128,128]{2,1,0:T(8,128)(2,1)S(1)} %fusion.5), channel_id=1, source_target_pairs={{8,16},{16,8},{12,20},{20,12},{9,17},{17,9},{13,21},{21,13},{10,18... | collective-permute-start | bytes 786440 | tf_op jit(solution)/shard_map/ppermute | solution.py:256
  37.6 14.0 %collective-permute-start.3 = (bf16[8,128,128]{2,1,0:T(8,128)(2,1)S(1)}, bf16[8,128,128]{2,1,0:T(8,128)(2,1)S(1)}, u32[]{:S(2)}, u32[]{:S(2)}) collective-permute-start(bf16[8,128,128]{2,1,0:T(8,128)(2,1)S(1)} %fusion.5), channel_id=1, source_target_pairs={{8,24},{16,0},{12,28},{20,4},{9,25},{17,1},{13,29},{21,5},{10,26},... | collective-permute-start | bytes 786440 | tf_op jit(solution)/shard_map/ppermute | solution.py:256
  54.4 44.4 %collective-permute-start.4 = (bf16[8,2,128,128]{3,2,1,0:T(8,128)(2,1)}, bf16[8,2,128,128]{3,2,1,0:T(8,128)(2,1)}, u32[]{:S(2)}, u32[]{:S(2)}) collective-permute-start(bf16[8,2,128,128]{3,2,1,0:T(8,128)(2,1)} %pad_maximum_fusion), channel_id=1, source_target_pairs={{0,4},{4,0},{8,12},{12,8},{16,20},{20,16},{24,28},{28,24},{1,5},{5... | collective-permute-start | bytes 1572872 | tf_op jit(solution)/shard_map/ppermute | solution.py:226
  55.8 16.9 %collective-permute-start.5 = (bf16[64,2048]{1,0:T(8,128)(2,1)}, bf16[64,2048]{1,0:T(8,128)(2,1)}, u32[]{:S(2)}, u32[]{:S(2)}) collective-permute-start(bf16[64,2048]{1,0:T(8,128)(2,1)} %get-tuple-element.49), channel_id=1, source_target_pairs={{0,4},{4,8},{8,12},{12,16},{16,20},{20,24},{24,28},{1,5},{5,9},{9,... | collective-permute-start | bytes 786440 | tf_op jit(solution)/shard_map/ppermute | solution.py:242
  59.0 16.4 %collective-permute-start.6 = (bf16[64,2048]{1,0:T(8,128)(2,1)S(1)}, bf16[64,2048]{1,0:T(8,128)(2,1)}, u32[]{:S(2)}, u32[]{:S(2)}) collective-permute-start(bf16[64,2048]{1,0:T(8,128)(2,1)S(1)} %copy-done.32), channel_id=1, source_target_pairs={{0,4},{4,8},{8,12},{12,16},{16,20},{20,24},{24,28},{1,5},{5,9},{9,... | collective-permute-start | bytes 786440 | tf_op jit(solution)/shard_map/ppermute | solution.py:242
  78.6 15.3 %copy-start.30 = (bf16[8,1,128,128]{3,2,0,1:T(8,128)(2,1)S(1)}, bf16[8,1,128,128]{3,2,0,1:T(8,128)(2,1)}, u32[]{:S(2)}) copy-start(bf16[8,1,128,128]{3,2,0,1:T(8,128)(2,1)} %get-tuple-element.81) | copy-start | bytes 786436
  78.6 15.3 %copy-start.31 = (bf16[8,1,128,128]{3,2,0,1:T(8,128)(2,1)S(1)}, bf16[8,1,128,128]{3,2,0,1:T(8,128)(2,1)}, u32[]{:S(2)}) copy-start(bf16[8,1,128,128]{3,2,0,1:T(8,128)(2,1)} %get-tuple-element.77) | copy-start | bytes 786436
  104.9 1.5 %collective-permute-start.9 = (bf16[2,2,2,128,128]{4,3,2,1,0:T(8,128)(2,1)S(1)}, bf16[2,2,2,128,128]{4,3,2,1,0:T(8,128)(2,1)S(1)}, u32[]{:S(2)}, u32[]{:S(2)}) collective-permute-start(bf16[2,2,2,128,128]{4,3,2,1,0:T(8,128)(2,1)S(1)} %fusion.24), channel_id=1, source_target_pairs={{0,1},{1,0},{2,3},{3,2},{4,5},{5,4},{6,7},{7,6},{8,9},{9,8},{10,11... | collective-permute-start | bytes 786440 | tf_op jit(solution)/shard_map/ppermute | solution.py:236
  107.4 4.3 %collective-permute-start.11 = (bf16[2,128,128]{2,1,0:T(8,128)(2,1)S(1)}, bf16[2,128,128]{2,1,0:T(8,128)(2,1)S(1)}, u32[]{:S(2)}, u32[]{:S(2)}) collective-permute-start(bf16[2,128,128]{2,1,0:T(8,128)(2,1)S(1)} %dynamic-slice_bitcast_fusion.1), channel_id=1, source_target_pairs={{0,2},{1,3},{2,0},{3,1},{4,6},{5,7},{6,4},{7,5},{8,10},{9,11},{10,... | collective-permute-start | bytes 196616 | tf_op jit(solution)/shard_map/ppermute | solution.py:236
  109.1 5.1 %collective-permute-start.10 = (bf16[2,128,128]{2,1,0:T(8,128)(2,1)S(1)}, bf16[2,128,128]{2,1,0:T(8,128)(2,1)S(1)}, u32[]{:S(2)}, u32[]{:S(2)}) collective-permute-start(bf16[2,128,128]{2,1,0:T(8,128)(2,1)S(1)} %get-tuple-element.86), channel_id=1, source_target_pairs={{0,4},{1,5},{2,6},{3,7},{4,0},{5,1},{6,2},{7,3},{8,12},{9,13},{10,... | collective-permute-start | bytes 196616 | tf_op jit(solution)/shard_map/ppermute | solution.py:236
  111.7 5.2 %collective-permute-start.12 = (bf16[2,128,128]{2,1,0:T(8,128)(2,1)S(1)}, bf16[2,128,128]{2,1,0:T(8,128)(2,1)S(1)}, u32[]{:S(2)}, u32[]{:S(2)}) collective-permute-start(bf16[2,128,128]{2,1,0:T(8,128)(2,1)S(1)} %get-tuple-element.87), channel_id=1, source_target_pairs={{0,6},{1,7},{2,4},{3,5},{4,2},{5,3},{6,0},{7,1},{8,14},{9,15},{10,... | collective-permute-start | bytes 196616 | tf_op jit(solution)/shard_map/ppermute | solution.py:236
  116.9 10.5 %copy-start.28 = (bf16[64,2048]{1,0:T(8,128)(2,1)S(1)}, bf16[64,2048]{1,0:T(8,128)(2,1)}, u32[]{:S(2)}) copy-start(bf16[64,2048]{1,0:T(8,128)(2,1)} %copy-done.27) | copy-start | bytes 786436
  116.9 11.7 %copy-start.26 = (bf16[64,2048]{1,0:T(8,128)(2,1)S(1)}, bf16[64,2048]{1,0:T(8,128)(2,1)}, u32[]{:S(2)}) copy-start(bf16[64,2048]{1,0:T(8,128)(2,1)} %copy-done.25) | copy-start | bytes 786436
  116.9 4.3 %collective-permute-start.13 = (bf16[2,128,128]{2,1,0:T(8,128)(2,1)S(1)}, bf16[2,128,128]{2,1,0:T(8,128)(2,1)S(1)}, u32[]{:S(2)}, u32[]{:S(2)}) collective-permute-start(bf16[2,128,128]{2,1,0:T(8,128)(2,1)S(1)} %fusion.29), channel_id=1, source_target_pairs={{0,8},{1,9},{2,10},{3,11},{4,12},{5,13},{6,14},{7,15},{8,0},{9,1},... | collective-permute-start | bytes 196616 | tf_op jit(solution)/shard_map/ppermute | solution.py:236
  121.3 5.5 %collective-permute-start.14 = (bf16[2,128,128]{2,1,0:T(8,128)(2,1)S(1)}, bf16[2,128,128]{2,1,0:T(8,128)(2,1)S(1)}, u32[]{:S(2)}, u32[]{:S(2)}) collective-permute-start(bf16[2,128,128]{2,1,0:T(8,128)(2,1)S(1)} %add_convert_fusion.1), channel_id=1, source_target_pairs={{0,16},{1,17},{2,18},{3,19},{4,20},{5,21},{6,22},{7,23},{8,24},{9,... | collective-permute-start | bytes 196616 | tf_op jit(solution)/shard_map/ppermute | solution.py:236
  126.8 7.5 %collective-permute-start.15 = (bf16[2,128,128]{2,1,0:T(8,128)(2,1)S(1)}, bf16[2,128,128]{2,1,0:T(8,128)(2,1)S(1)}, u32[]{:S(2)}, u32[]{:S(2)}) collective-permute-start(bf16[2,128,128]{2,1,0:T(8,128)(2,1)S(1)} %add_convert_fusion), channel_id=1, source_target_pairs={{0,2},{1,3},{2,0},{3,1},{4,6},{5,7},{6,4},{7,5},{8,10},{9,11},{10,... | collective-permute-start | bytes 196616 | tf_op jit(solution)/shard_map/ppermute | solution.py:236
  127.4 15.8 %collective-permute-start.7 = (bf16[64,2048]{1,0:T(8,128)(2,1)S(1)}, bf16[64,2048]{1,0:T(8,128)(2,1)S(1)}, u32[]{:S(2)}, u32[]{:S(2)}) collective-permute-start(bf16[64,2048]{1,0:T(8,128)(2,1)S(1)} %copy-done.28), channel_id=1, source_target_pairs={{4,0},{8,4},{12,8},{16,12},{20,16},{24,20},{28,24},{5,1},{9,5},{13... | collective-permute-start | bytes 786440 | tf_op jit(solution)/shard_map/ppermute | solution.py:242
  128.7 14.5 %collective-permute-start.8 = (bf16[64,2048]{1,0:T(8,128)(2,1)S(1)}, bf16[64,2048]{1,0:T(8,128)(2,1)S(1)}, u32[]{:S(2)}, u32[]{:S(2)}) collective-permute-start(bf16[64,2048]{1,0:T(8,128)(2,1)S(1)} %copy-done.26), channel_id=1, source_target_pairs={{4,0},{8,4},{12,8},{16,12},{20,16},{24,20},{28,24},{5,1},{9,5},{13... | collective-permute-start | bytes 786440 | tf_op jit(solution)/shard_map/ppermute | solution.py:242
  130.0 11.5 %collective-permute-start.16 = (bf16[2,128,128]{2,1,0:T(8,128)(2,1)S(1)}, bf16[2,128,128]{2,1,0:T(8,128)(2,1)S(1)}, u32[]{:S(2)}, u32[]{:S(2)}) collective-permute-start(bf16[2,128,128]{2,1,0:T(8,128)(2,1)S(1)} %add_convert_fusion), channel_id=1, source_target_pairs={{0,4},{1,5},{2,6},{3,7},{4,0},{5,1},{6,2},{7,3},{8,12},{9,13},{10,... | collective-permute-start | bytes 196616 | tf_op jit(solution)/shard_map/ppermute | solution.py:236
  133.3 9.7 %collective-permute-start.17 = (bf16[2,128,128]{2,1,0:T(8,128)(2,1)S(1)}, bf16[2,128,128]{2,1,0:T(8,128)(2,1)S(1)}, u32[]{:S(2)}, u32[]{:S(2)}) collective-permute-start(bf16[2,128,128]{2,1,0:T(8,128)(2,1)S(1)} %add_convert_fusion), channel_id=1, source_target_pairs={{0,6},{1,7},{2,4},{3,5},{4,2},{5,3},{6,0},{7,1},{8,14},{9,15},{10,... | collective-permute-start | bytes 196616 | tf_op jit(solution)/shard_map/ppermute | solution.py:236
  143.0 2.0 %collective-permute-start.18 = (bf16[2,2,2,128,128]{4,3,2,1,0:T(8,128)(2,1)S(1)}, bf16[2,2,2,128,128]{4,3,2,1,0:T(8,128)(2,1)S(1)}, u32[]{:S(2)}, u32[]{:S(2)}) collective-permute-start(bf16[2,2,2,128,128]{4,3,2,1,0:T(8,128)(2,1)S(1)} %get-tuple-element.83), channel_id=1, source_target_pairs={{0,1},{1,0},{2,3},{3,2},{4,5},{5,4},{6,7},{7,6},{8,9},{9,8},{10,11... | collective-permute-start | bytes 786440 | tf_op jit(solution)/shard_map/ppermute | solution.py:236
  (28 other events, 67.4 us)

commit v2 on v1

v2 whole, which is shorter than its diff:
```python
import functools

import jax
import jax.numpy as jnp
from jax import lax
from jax.experimental import pallas as pl
from jax.experimental.pallas import tpu as pltpu
from jax.sharding import PartitionSpec as P

HEADS = 16
HD = 128
WINDOW = 64
HALF = HEADS // 2
CHUNKS = 2
CHUNK = HALF // CHUNKS
GROUP = 2
WIDE = HEADS * HD
VMEM = 8 * 1024 * 1024
BF = jnp.bfloat16
F32 = jnp.float32


def dot(left, right):
    return jnp.dot(left, right, preferred_element_type=F32)


def dot_nt(left, right):
    return lax.dot_general(left, right, (((1,), (1,)), ((), ())), preferred_element_type=F32)


def dot_tn(left, right):
    return lax.dot_general(left, right, (((0,), (0,)), ((), ())), preferred_element_type=F32)


def phi(before):
    return jnp.where(before > 0, before + 1.0, jnp.exp(jnp.minimum(before, 0.0)))


def col(head):
    return slice(head * HD, (head + 1) * HD)


def col_of(half, head):
    return pl.ds(pl.multiple_of(half * (HALF * HD) + head * HD, HD), HD)


def own_half():
    return lax.axis_index("seq") % 2


def lin_scale(tokens):
    return 1.0 / (HD * tokens * lax.axis_size("seq"))


def cost(microseconds):
    return pl.CostEstimate(
        flops=int(microseconds * 1000), bytes_accessed=1000, transcendentals=0
    )


def array(shape, kind):
    return jax.ShapeDtypeStruct(shape, kind)


def call(kernel, name, outs, operands, in_hbm=0, unread=0, microseconds=3, **more):
    whole = pl.BlockSpec(memory_space=pltpu.VMEM)
    return pl.pallas_call(
        kernel,
        in_specs=[pl.BlockSpec(memory_space=pltpu.HBM)] * in_hbm
        + [whole] * (len(operands) - in_hbm - unread)
        + [pl.BlockSpec(memory_space=pl.ANY)] * unread,
        out_specs=[whole] * len(outs),
        out_shape=outs,
        cost_estimate=cost(microseconds),
        compiler_params=pltpu.CompilerParams(vmem_limit_bytes=VMEM),
        name=name,
        **more,
    )(*operands)


def feature_kernel(first, lq, lk, v, g, fm, *rest):
    fq_out, fk_out, *t_out, rows, maps, arrived = rest[-5 - CHUNKS :]
    half = 1 - own_half() if first else own_half()

    def copies(step):
        head = half * HALF + step * GROUP
        wide = pl.ds(pl.multiple_of(head * HD, GROUP * HD), GROUP * HD)
        here = slice(step * GROUP * HD, (step + 1) * GROUP * HD)
        pairs = [(ref.at[:, wide], rows.at[n, :, here]) for n, ref in enumerate((lq, lk, v, g))]
        pairs.append((fm.at[pl.ds(head, GROUP)], maps.at[step * GROUP : (step + 1) * GROUP]))
        return [
            pltpu.make_async_copy(source, target, arrived.at[step, n])
            for n, (source, target) in enumerate(pairs)
        ]

    started = [copies(step) for step in range(HALF // GROUP)]
    for step in started:
        for copy in step:
            copy.start()
    for h in range(HALF):
        if h % GROUP == 0:
            for copy in started[h // GROUP]:
                copy.wait()
        c = col(h)
        w = maps[h]
        fq = phi(dot(rows[0, :, c], w)).astype(BF)
        fk = phi(dot(rows[1, :, c], w)).astype(BF)
        fq_out[:, c] = fq
        fk_out[:, c] = fk
        t_out[h // CHUNK][0, h % CHUNK] = dot_tn(fk, rows[2, :, c]).astype(BF)
        t_out[h // CHUNK][1, h % CHUNK] = dot_tn(fq, rows[3, :, c]).astype(BF)


def features(lq, lk, v, g, fm, follows):
    tokens = lq.shape[0]
    row = array((tokens, HALF * HD), BF)
    lq, lk, v, g, fm = (pltpu.with_memory_space_constraint(x, pltpu.HBM) for x in (lq, lk, v, g, fm))
    return call(
        functools.partial(feature_kernel, not follows),
        "features",
        [row, row] + [array((2, CHUNK, HD, HD), BF)] * CHUNKS,
        (lq, lk, v, g, fm, *follows),
        in_hbm=5,
        unread=len(follows),
        scratch_shapes=[
            pltpu.VMEM((4, tokens, HALF * HD), BF),
            pltpu.VMEM((HALF, HD, HD), BF),
            pltpu.SemaphoreType.DMA((HALF // GROUP, 5)),
        ],
    )


def causal_mask(tokens):
    rows = lax.broadcasted_iota(jnp.int32, (tokens, tokens), 0)
    cols = lax.broadcasted_iota(jnp.int32, (tokens, tokens), 1)
    return rows >= cols


def window_kernel(wq, wk, v, g, rims, *rest):
    att, dv, dwq, dwk, tail_k, send = rest[-6:]
    tokens = wq.shape[0]
    root = HD ** (-0.5)
    rows = lax.broadcasted_iota(jnp.int32, (tokens, 2 * WINDOW), 0)
    cols = lax.broadcasted_iota(jnp.int32, (tokens, 2 * WINDOW), 1)
    offset = cols - rows % WINDOW
    absent = (lax.axis_index("seq") == 0) & (rows < WINDOW) & (cols < WINDOW)
    band = (offset >= 1) & (offset <= WINDOW) & jnp.logical_not(absent)
    for h in range(HEADS):
        c = col(h)
        q, k, val, grad = wq[:, c], wk[:, c], v[:, c], g[:, c]
        kp = jnp.concatenate([rims[0, :, c], k[:WINDOW]], axis=0)
        vp = jnp.concatenate([rims[1, :, c], val[:WINDOW]], axis=0)
        score = jnp.concatenate([dot_nt(q[:WINDOW], kp), dot_nt(q[WINDOW:], k)], axis=0) * root
        score = jnp.where(band, score, -jnp.inf)
        expo = jnp.exp(score - jnp.max(score, axis=-1, keepdims=True))
        prob = expo / jnp.sum(expo, axis=-1, keepdims=True)
        prob_b = prob.astype(BF)
        dprob = jnp.concatenate([dot_nt(grad[:WINDOW], vp), dot_nt(grad[WINDOW:], val)], axis=0)
        delta = jnp.sum(prob * dprob, axis=-1, keepdims=True)
        dscore = (prob * (dprob - delta) * root).astype(BF)
        win = jnp.concatenate([dot(prob_b[:WINDOW], vp), dot(prob_b[WINDOW:], val)], axis=0)
        att[:, c] = win
        dwq[:, c] = jnp.concatenate(
            [dot(dscore[:WINDOW], kp), dot(dscore[WINDOW:], k)], axis=0
        ).astype(BF)
        dk0 = dot_tn(dscore[:WINDOW], q[:WINDOW])
        dk1 = dot_tn(dscore[WINDOW:], q[WINDOW:])
        dv0 = dot_tn(prob_b[:WINDOW], grad[:WINDOW])
        dv1 = dot_tn(prob_b[WINDOW:], grad[WINDOW:])
        send[0, :, c] = dk0[:WINDOW].astype(BF)
        send[1, :, c] = dv0[:WINDOW].astype(BF)
        dwk[:, c] = jnp.concatenate([dk0[WINDOW:] + dk1[:WINDOW], dk1[WINDOW:]], axis=0).astype(BF)
        tail_k[:, c] = dk1[WINDOW:]
        dv[:, c] = jnp.concatenate([dv0[WINDOW:] + dv1[:WINDOW], dv1[WINDOW:]], axis=0)


def window_part(*operands):
    tokens = operands[0].shape[0]
    wide, narrow = array((tokens, WIDE), F32), array((tokens, WIDE), BF)
    return call(
        window_kernel,
        "window_part",
        [wide, wide, narrow, narrow, array((WINDOW, WIDE), F32), array((2, WINDOW, WIDE), BF)],
        operands,
        unread=len(operands) - 5,
        microseconds=6,
    )


def state_kernel(first, count, lq, lk, v, g, fq, fk, *rest):
    states, (dpq_out, dpk_out, keep, send) = rest[:count], rest[-4:]
    core, far = lax.axis_index("dp") % 2, lax.axis_index("dp") // 2
    half = own_half() if count == CHUNKS else 1 - own_half()
    scale = lin_scale(lq.shape[0])
    causal = causal_mask(lq.shape[0])
    if 0 < first:
        keep[:, :first] = rest[count][...]
        send[:, :first] = rest[count + 1][...]
    for n in range(count):
        terms = []
        for h in range(CHUNK):
            head = (first + n) * CHUNK + h
            c, at, here = col(head), col_of(half, head), col(n * CHUNK + h)
            q_feat, k_feat, val, grad = fq[:, c], fk[:, c], v[:, at], g[:, at]
            mixed = jnp.where(causal, dot_nt(grad, val), 0.0).astype(BF)
            dfq = (dot(mixed, k_feat) + dot_nt(grad, states[n][0, h])) * scale
            dfk = (dot_tn(mixed, q_feat) + dot_nt(val, states[n][1, h])) * scale
            dpq = (dfq * jnp.minimum(q_feat.astype(F32), 1.0)).astype(BF)
            dpk = (dfk * jnp.minimum(k_feat.astype(F32), 1.0)).astype(BF)
            dpq_out[:, here], dpk_out[:, here] = dpq, dpk
            terms.append((dot_tn(lq[:, at], dpq) + dot_tn(lk[:, at], dpk)).astype(BF))
        for y in range(2):
            keep[y ^ far, first + n] = jnp.where(core == 0, terms[y], terms[2 + y])
            send[y ^ far, first + n] = jnp.where(core == 0, terms[2 + y], terms[y])


def state_part(first, count, arrays, states, earlier, follows=()):
    row = array((arrays[0].shape[0], count * CHUNK * HD), BF)
    part = array((2, first + count, HD, HD), BF)
    return call(
        functools.partial(state_kernel, first, count),
        "state_part",
        [row, row, part, part],
        (*arrays, *states, *earlier, *follows),
        unread=len(follows),
    )


def output_kernel(v, g, fm, win, dv_win, *rest):
    att, dlq, dlk, dv, tail_v = rest[-5:]
    scale = lin_scale(win.shape[0])
    own = own_half()
    causal = causal_mask(v.shape[0])
    for half, refs in ((own, rest[: 4 + CHUNKS]), (1 - own, rest[4 + CHUNKS : -5])):
        fq, fk = refs[:2]
        states, pairs = refs[2 : 2 + CHUNKS], refs[2 + CHUNKS :]
        for h in range(HALF):
            n, k = h // CHUNK, h % CHUNK
            c, at = col(h), col_of(half, h)
            w = fm[half * HALF + h]
            each = 2 * HALF // len(pairs)
            m, here = 2 * (h // each), col(h % each)
            dlq[:, at] = dot_nt(pairs[m][:, here], w).astype(BF)
            dlk[:, at] = dot_nt(pairs[m + 1][:, here], w).astype(BF)
            q_feat, k_feat = fq[:, c], fk[:, c]
            scores = jnp.where(causal, dot_nt(q_feat, k_feat), 0.0).astype(BF)
            lin = dot(scores, v[:, at]) + dot(q_feat, states[n][0, k])
            att[:, at] = (lin * scale + win[:, at]).astype(BF)
            grad_v = dot_tn(scores, g[:, at]) + dot(k_feat, states[n][1, k])
            grad_v = grad_v * scale + dv_win[:, at]
            dv[:, at] = grad_v.astype(BF)
            tail_v[:, at] = grad_v[WINDOW:]


def output_part(v, g, fm, win, dv_win, own, other):
    row = array(win.shape, BF)
    return call(
        output_kernel,
        "output_part",
        [row] * 4 + [array((WINDOW, WIDE), F32)],
        (v, g, fm, win, dv_win, *own, *other),
    )


def finish_kernel(tail_k, tail_v, rims, k_in, v_in, dk, dv):
    dk[...] = (tail_k[...] + rims[0].astype(F32)).astype(BF)
    dv[...] = (tail_v[...] + rims[1].astype(F32)).astype(BF)


def finish(tail_k, tail_v, back, dwk, dv):
    rims = pl.BlockSpec((WINDOW, WIDE), lambda i: (0, 0))
    last = pl.BlockSpec((WINDOW, WIDE), lambda i: (dwk.shape[0] // WINDOW - 1, 0))
    kept = pl.BlockSpec(memory_space=pl.ANY)
    row = jax.ShapeDtypeStruct(dwk.shape, BF)
    return pl.pallas_call(
        finish_kernel,
        grid=(1,),
        in_specs=[rims] * 2 + [pl.BlockSpec(back.shape, lambda i: (0, 0, 0))] + [kept] * 2,
        out_specs=[last, last],
        out_shape=[row, row],
        input_output_aliases={3: 0, 4: 1},
        cost_estimate=cost(1),
        compiler_params=pltpu.CompilerParams(vmem_limit_bytes=VMEM),
        name="finish",
    )(tail_k, tail_v, back, dwk, dv)


def flipped(block, bit):
    count = lax.axis_size("seq")
    return lax.ppermute(block, "seq", [(i, i ^ bit) for i in range(count)])


def flat_flipped(block, seq_bits, dp_bits):
    rows, width = lax.axis_size("seq"), lax.axis_size("dp")
    route = [
        (s * width + d, (s ^ seq_bits) * width + (d ^ dp_bits))
        for s in range(rows)
        for d in range(width)
    ]
    return lax.ppermute(block, ("seq", "dp"), route)


def passed_along(block, distance):
    devices = range(lax.axis_size("seq"))
    route = [(i - distance, i) for i in devices if i - distance in devices]
    return lax.ppermute(block, "seq", route)


def spread(block, level):
    count = lax.axis_size("seq")
    size = 2 << level
    total = None
    for turn in range(1 << level):
        route = []
        for base in range(0, count // 2, size):
            low, high = base + size // 2 - 1, base + size // 2
            for parity in range(2):
                route.append((2 * low + parity, 2 * (high + turn) + parity))
                route.append((2 * high + parity, 2 * (low - turn) + parity))
        came = lax.ppermute(block, "seq", route)
        total = came if total is None else total + came
    return total


def levels():
    return (lax.axis_size("seq") // 2).bit_length() - 1


def upper(level):
    return ((lax.axis_index("seq") // 2) >> level) % 2 == 1


def outgoing(pair, sums, level):
    total = pair if sums is None else pair.astype(F32) + sums.astype(F32)
    return jnp.where(upper(level), total[1], total[0]).astype(BF)


def taken(sums, got, level):
    side = lax.broadcasted_iota(jnp.int32, (2, 1, 1, 1), 0)
    here = jnp.where((side == 0) == upper(level), got[None], jnp.zeros_like(got)[None])
    return here if sums is None else (sums.astype(F32) + here.astype(F32)).astype(BF)


def entering(sums, kept, came):
    side = lax.broadcasted_iota(jnp.int32, (2, 1, 1, 1), 0)
    same = side == own_half()
    added = (jnp.where(same, jnp.zeros_like(came), came), jnp.where(same, kept, jnp.zeros_like(kept)))
    return [(sums.astype(F32) + x.astype(F32)).astype(BF) for x in added]


def near_sum(keep, send):
    return (keep.astype(F32) + flat_flipped(send, 0, 1).astype(F32)).astype(BF)


def assemble_kernel(norm, *refs):
    pieces, out = refs[:-1], refs[-1]
    core, far = lax.axis_index("dp") % 2, lax.axis_index("dp") // 2
    for side in range(2):
        half = own_half() ^ side
        for n in range(CHUNKS):
            for c in range(2):
                for y in range(2):
                    head = half * HALF + n * CHUNK + (c ^ core) * 2 + (y ^ far)
                    out[head] = pieces[side * 4 + c * 2 + y][n].astype(F32) * norm


def assemble(pieces, norm):
    return call(
        functools.partial(assemble_kernel, norm), "assemble", [array((HEADS, HD, HD), F32)], pieces
    )[0]


def on_device(
    linear_queries, linear_keys, window_queries, window_keys, values, cotangent, feature_map
):
    tokens = linear_queries.shape[1]
    total_tokens = tokens * lax.axis_size("seq") * lax.axis_size("dp") * linear_queries.shape[0]
    lq, lk, wq, wk, v, g = (
        x[0]
        for x in (linear_queries, linear_keys, window_queries, window_keys, values, cotangent)
    )
    fq_o, fk_o, *given = features(lq, lk, v, g, feature_map, ())
    came = [flipped(x, 1) for x in given]
    fq, fk, *kept = features(lq, lk, v, g, feature_map, (fq_o,))
    pair = [(a.astype(F32) + b.astype(F32)).astype(BF) for a, b in zip(kept, came)]
    sums = [None] * CHUNKS
    for level in range(levels()):
        sent = [outgoing(pair[n], sums[n], level) for n in range(CHUNKS)]
        if level == 0:
            tails = jnp.stack([wk[tokens - WINDOW :], v[tokens - WINDOW :]])
            sent[0], tails = lax.optimization_barrier((sent[0], tails))
            rims = passed_along(tails, 1)
        for n in range(CHUNKS):
            got = spread(sent[n], level)
            if level == levels() - 1 and n == CHUNKS - 1:
                got, rims = lax.optimization_barrier((got, rims))
            sums[n] = taken(sums[n], got, level)
    mine, others = zip(*(entering(sums[n], kept[n], came[n]) for n in range(CHUNKS)))
    rows = (lq, lk, v, g)
    back = [flipped(x, 1) for x in others]
    win, dv_win, dwq, dwk, tail_k, edge = window_part(wq, wk, v, g, rims, others[-1])
    dpq, dpk, *near = state_part(0, CHUNKS, (*rows, fq, fk), mine, (), (dwq,))
    own = (fq, fk, *mine, dpq, dpk)
    beyond, pairs = (), []
    for n in range(CHUNKS):
        dpq, dpk, *beyond = state_part(n, 1, (*rows, fq_o, fk_o), (back[n],), beyond, (dwq,))
        pairs += [dpq, dpk]
    other = (fq_o, fk_o, *back, *pairs)
    near, beyond = lax.optimization_barrier((near, beyond))
    near, beyond = near_sum(*near), near_sum(*beyond)
    a, c = flat_flipped(beyond[0], 1, 0), flat_flipped(beyond[1], 1, 2)
    b = flat_flipped(near[1], 0, 2)
    total = sum(x.astype(F32) for x in (near[0], a, b, c))
    sent, edge = lax.optimization_barrier((total.astype(BF), edge))
    total = sent.astype(F32)
    for bits in range(2, lax.axis_size("seq"), 2):
        total = total + flat_flipped(sent, bits, 0).astype(F32)
    edge = passed_along(edge, -1)
    done = total.astype(BF)
    a, b, c = flat_flipped(done, 1, 0), flat_flipped(done, 0, 2), flat_flipped(done, 1, 2)
    across = [flat_flipped(x, 0, 1) for x in (done, b, a, c)]
    map_grad = assemble(
        (done, b, *across[:2], a, c, *across[2:]), total_tokens ** (-0.5)
    )
    attended, dlq, dlk, dv, tail_v = output_part(v, g, feature_map, win, dv_win, own, other)
    dwk, dv = finish(tail_k, tail_v, edge, dwk, dv)
    return attended[None], dlq[None], dlk[None], dwq[None], dwk[None], dv[None], map_grad


def solution(mesh):
    row = P("dp", "seq", None)
    return jax.shard_map(
        on_device,
        mesh=mesh,
        in_specs=(row,) * 6 + (P(),),
        out_specs=(row,) * 6 + (P(),),
        check_vma=False,
    )
```

time: 147 us -> 112 us (0.76)
  waiting for transfers between devices: 62.5 us -> 36.3 us
  local copies, waits for them, and re-layouts: 17.5 us -> 2.06 us
  starting transfers between devices: 26.9 us -> 37.3 us
  Pallas kernels: 29.6 us -> 26.6 us
    ppermute x4 -> x2, waiting for transfers between devices: 14 us -> 0.01 us  [passed_along(): return lax.ppermute(block, 'seq', route)]
    unnamed x66 -> x16, local copies, waits for them, and re-layouts: 14.6 us -> 1.08 us
    ppermute x10 -> x15, starting transfers between devices: 10.4 us -> 18.6 us  [flat_flipped(): return lax.ppermute(block, ('seq', 'dp'), route)]
    ppermute x3 -> x6, waiting for transfers between devices: 17.3 us -> 10.3 us  [spread(): came = lax.ppermute(block, 'seq', route)]
    ppermute x3 -> x6, starting transfers between devices: 3.79 us -> 8.53 us  [spread(): came = lax.ppermute(block, 'seq', route)]
    ppermute x2 -> x4, waiting for transfers between devices: 7.24 us -> 3.62 us  [flipped(): return lax.ppermute(block, 'seq', [(i, i ^ bit) for i in range(count)])]
    ppermute x4 -> x2, starting transfers between devices: 8.24 us -> 4.89 us  [passed_along(): return lax.ppermute(block, 'seq', route)]
    pallas_call x6 -> x9, Pallas kernels: 29.6 us -> 26.6 us  [the longest x8 25.7 us: call(): pl.pallas_call(kernel, in_specs=[pl.BlockSpec(memory_space=pltpu.HBM)] *...]
  transfers between devices with their start and end apart: 19 -> 27, of which waited for: 13 -> 12; matrix products, arithmetic and copies ran while one was open for 2% -> 6% of each run, Pallas kernels for 15% -> 19%
where the time goes in v2:
time: 112 us; the launch traced here: 111 us
  starting transfers between devices  37.3 us (33%)
  waiting for transfers between devices  36.3 us (32%)
  Pallas kernels  26.6 us (24%)
  other arithmetic  7.87 us (7%)
  local copies, waits for them, and re-layouts  2.06 us (2%)
    pallas_call x8, Pallas kernels, call(): pl.pallas_call(kernel, in_specs=[pl.BlockSpec(memory_space=pltpu.HBM)] *...  25.7 us
    ppermute x15, waiting for transfers between devices, flat_flipped(): return lax.ppermute(block, ('seq', 'dp'), route)  22.4 us
    ppermute x15, starting transfers between devices, flat_flipped(): return lax.ppermute(block, ('seq', 'dp'), route)  18.6 us
    ppermute x6, waiting for transfers between devices, spread(): came = lax.ppermute(block, 'seq', route)  10.3 us
    ppermute x6, starting transfers between devices, spread(): came = lax.ppermute(block, 'seq', route)  8.53 us
    ppermute x4, starting transfers between devices, flipped(): return lax.ppermute(block, 'seq', [(i, i ^ bit) for i in range(count)])  5.32 us
    ppermute x2, starting transfers between devices, passed_along(): return lax.ppermute(block, 'seq', route)  4.89 us
    ppermute x4, waiting for transfers between devices, flipped(): return lax.ppermute(block, 'seq', [(i, i ^ bit) for i in range(count)])  3.62 us
  transfers between devices with their start and end apart: 27, of which 12 were waited for; matrix products, arithmetic and copies ran while one was open for 6% of the time, Pallas kernels for 19%

profile of v2, /device:TPU:0, one launch (start us, length us, event | category | flops | bytes accessed | tf_op | source)
XLA Modules:
  0.0 111.1 jit_solution(239681641433980708)
XLA Ops:
  0.6 3.5 %features.2 = (bf16[128,1024]{1,0:T(8,128)(2,1)S(1)}, bf16[128,1024]{1,0:T(8,128)(2,1)S(1)}, bf16[2,4,128,128]{3,2,1,0:T(8,128)(2,1)S(1)}, bf16[2,4,128,128]{3,2,1,0:T(8,128)(2,1)S(1)}) custom-call(bf16[128,2048]{1,0:T(8,128)(2,1)} %bitcast.45, bf16[128,2048]{1,0:T(8,128)(2,1)} %bitcast.50, bf16[128,2048]{1,0:T(8,128)(2,1)} %bitcast.31, ...), custom_call_target="tpu_custom_call" | custom-call | flops 3000 | bytes 1000 | tf_op jit(solution)/shard_map/features/pallas_call | solution.py:67
  4.2 3.0 %collective-permute-start = (bf16[2,4,128,128]{3,2,1,0:T(8,128)(2,1)S(1)}, bf16[2,4,128,128]{3,2,1,0:T(8,128)(2,1)S(1)}, u32[]{:S(2)}, u32[]{:S(2)}) collective-permute-start(bf16[2,4,128,128]{3,2,1,0:T(8,128)(2,1)S(1)} %get-tuple-element.52), channel_id=1, source_target_pairs={{0,4},{4,0},{8,12},{12,8},{16,20},{20,16},{24,28},{28,24},{1,5},{5... | collective-permute-start | bytes 786440 | tf_op jit(solution)/shard_map/ppermute | solution.py:290
  7.3 3.6 %features.3 = (bf16[128,1024]{1,0:T(8,128)(2,1)S(1)}, bf16[128,1024]{1,0:T(8,128)(2,1)S(1)}, bf16[2,4,128,128]{3,2,1,0:T(8,128)(2,1)S(1)}, bf16[2,4,128,128]{3,2,1,0:T(8,128)(2,1)S(1)}) custom-call(bf16[128,2048]{1,0:T(8,128)(2,1)} %bitcast.46, bf16[128,2048]{1,0:T(8,128)(2,1)} %bitcast.51, bf16[128,2048]{1,0:T(8,128)(2,1)} %bitcast.32, ...), custom_call_target="tpu_custom_call" | custom-call | flops 3000 | bytes 1000 | tf_op jit(solution)/shard_map/features/pallas_call | solution.py:67
  12.7 1.6 %collective-permute-done = bf16[2,4,128,128]{3,2,1,0:T(8,128)(2,1)S(1)} collective-permute-done((bf16[2,4,128,128]{3,2,1,0:T(8,128)(2,1)S(1)}, bf16[2,4,128,128]{3,2,1,0:T(8,128)(2,1)S(1)}, u32[]{:S(2)}, u32[]{:S(2)}) %collective-permute-start) | collective-permute-done | bytes 262176 | tf_op jit(solution)/shard_map/ppermute | solution.py:290
  15.1 2.1 %collective-permute-start.1 = (bf16[4,128,128]{2,1,0:T(8,128)(2,1)}, bf16[4,128,128]{2,1,0:T(8,128)(2,1)S(1)}, u32[]{:S(2)}, u32[]{:S(2)}) collective-permute-start(bf16[4,128,128]{2,1,0:T(8,128)(2,1)} %fusion.11), channel_id=1, source_target_pairs={{0,8},{8,0},{4,12},{12,4},{16,24},{24,16},{20,28},{28,20},{1,9},{9... | collective-permute-start | bytes 393224 | tf_op jit(solution)/shard_map/ppermute | solution.py:320
  17.2 2.0 %collective-permute-done.4 = bf16[2,4,128,128]{3,2,1,0:T(8,128)(2,1)} collective-permute-done((bf16[2,4,128,128]{3,2,1,0:T(8,128)(2,1)S(1)}, bf16[2,4,128,128]{3,2,1,0:T(8,128)(2,1)}, u32[]{:S(2)}, u32[]{:S(2)}) %collective-permute-start.4) | collective-permute-done | bytes 262176 | tf_op jit(solution)/shard_map/ppermute | solution.py:290
  20.9 1.8 %collective-permute-start.6 = (bf16[4,128,128]{2,1,0:T(8,128)(2,1)}, bf16[4,128,128]{2,1,0:T(8,128)(2,1)}, u32[]{:S(2)}, u32[]{:S(2)}) collective-permute-start(bf16[4,128,128]{2,1,0:T(8,128)(2,1)} %fusion.10), channel_id=1, source_target_pairs={{0,8},{8,0},{4,12},{12,4},{16,24},{24,16},{20,28},{28,20},{1,9},{9... | collective-permute-start | bytes 393224 | tf_op jit(solution)/shard_map/ppermute | solution.py:320
  22.7 3.4 %collective-permute-start.5 = (bf16[2,64,2048]{2,1,0:T(8,128)(2,1)}, bf16[2,64,2048]{2,1,0:T(8,128)(2,1)S(1)}, u32[]{:S(2)}, u32[]{:S(2)}) collective-permute-start(bf16[2,64,2048]{2,1,0:T(8,128)(2,1)} %pad_maximum_fusion), channel_id=1, source_target_pairs={{0,4},{4,8},{8,12},{12,16},{16,20},{20,24},{24,28},{1,5},{5,9},{9,... | collective-permute-start | bytes 1572872 | tf_op jit(solution)/shard_map/ppermute | solution.py:306
  32.6 2.5 %collective-permute-done.3 = bf16[4,128,128]{2,1,0:T(8,128)(2,1)S(1)} collective-permute-done((bf16[4,128,128]{2,1,0:T(8,128)(2,1)S(1)}, bf16[4,128,128]{2,1,0:T(8,128)(2,1)S(1)}, u32[]{:S(2)}, u32[]{:S(2)}) %collective-permute-start.3) | collective-permute-done | bytes 131104 | tf_op jit(solution)/shard_map/ppermute | solution.py:320
  35.2 7.8 %collective-permute-done.8 = bf16[4,128,128]{2,1,0:T(8,128)(2,1)S(1)} collective-permute-done((bf16[4,128,128]{2,1,0:T(8,128)(2,1)}, bf16[4,128,128]{2,1,0:T(8,128)(2,1)S(1)}, u32[]{:S(2)}, u32[]{:S(2)}) %collective-permute-start.8) | collective-permute-done | bytes 131104 | tf_op jit(solution)/shard_map/ppermute | solution.py:320
  43.9 1.6 %fusion.5 = (bf16[2,4,128,128]{3,2,1,0:T(8,128)(2,1)S(1)}, bf16[2,4,128,128]{3,2,1,0:T(8,128)(2,1)S(1)}, bf16[2,4,128,128]{3,2,1,0:T(8,128)(2,1)S(1)}, bf16[2,4,128,128]{3,2,1,0:T(8,128)(2,1)S(1)}) fusion(bf16[2,4,128,128]{3,2,1,0:T(8,128)(2,1)S(1)} %get-tuple-element.53, pred[2]{0:T(512)(128)(4,1)S(1)} %iota_compare_fusion, ...), kind=kLoop, calls=%fused_computation.13 | loop fusion | flops 3932160 | bytes 2621446 | tf_op jit(solution)/shard_map/convert_element_type | solution.py:348
  45.5 2.2 %collective-permute-start.9 = (bf16[2,4,128,128]{3,2,1,0:T(8,128)(2,1)S(1)}, bf16[2,4,128,128]{3,2,1,0:T(8,128)(2,1)S(1)}, u32[]{:S(2)}, u32[]{:S(2)}) collective-permute-start(bf16[2,4,128,128]{3,2,1,0:T(8,128)(2,1)S(1)} %get-tuple-element.93), channel_id=1, source_target_pairs={{0,4},{4,0},{8,12},{12,8},{16,20},{20,16},{24,28},{28,24},{1,5},{5... | collective-permute-start | bytes 786440 | tf_op jit(solution)/shard_map/ppermute | solution.py:290
  47.8 8.7 %window_part.1 = (f32[128,2048]{1,0:T(8,128)S(1)}, f32[128,2048]{1,0:T(8,128)S(1)}, bf16[128,2048]{1,0:T(8,128)(2,1)}, bf16[128,2048]{1,0:T(8,128)(2,1)}, f32[64...) custom-call(bf16[128,2048]{1,0:T(8,128)(2,1)S(1)} %bitcast.57, bf16[128,2048]{1,0:T(8,128)(2,1)S(1)} %bitcast.56, ...), custom_call_target="tpu_custom_call" | custom-call | flops 6000 | bytes 1000 | tf_op jit(solution)/shard_map/window_part/pallas_call | solution.py:67
  57.6 2.1 %state_part.3 = (bf16[128,1024]{1,0:T(8,128)(2,1)S(1)}, bf16[128,1024]{1,0:T(8,128)(2,1)S(1)}, bf16[2,2,128,128]{3,2,1,0:T(8,128)(2,1)S(1)}, bf16[2,2,128,128]{3,2,1,0:T(8,128)(2,1)S(1)}) custom-call(bf16[128,2048]{1,0:T(8,128)(2,1)S(1)} %bitcast.47, bf16[128,2048]{1,0:T(8,128)(2,1)S(1)} %bitcast.52, bf16[128,2048]{1,0:T(8,128)(2,1)S(1)} %bitcast.34, ...), custom_call_target="tpu_custom_call" | custom-call | flops 3000 | bytes 1000 | tf_op jit(solution)/shard_map/state_part/pallas_call | solution.py:67
  63.5 1.6 %collective-permute-start.14 = (bf16[2,128,128]{2,1,0:T(8,128)(2,1)S(1)}, bf16[2,128,128]{2,1,0:T(8,128)(2,1)S(1)}, u32[]{:S(2)}, u32[]{:S(2)}) collective-permute-start(bf16[2,128,128]{2,1,0:T(8,128)(2,1)S(1)} %slice_bitcast_fusion.1), channel_id=1, source_target_pairs={{0,2},{1,3},{2,0},{3,1},{4,6},{5,7},{6,4},{7,5},{8,10},{9,11},{10,... | collective-permute-start | bytes 196616 | tf_op jit(solution)/shard_map/ppermute | solution.py:300
  65.2 2.0 %collective-permute-start.13 = (bf16[2,128,128]{2,1,0:T(8,128)(2,1)S(1)}, bf16[2,128,128]{2,1,0:T(8,128)(2,1)S(1)}, u32[]{:S(2)}, u32[]{:S(2)}) collective-permute-start(bf16[2,128,128]{2,1,0:T(8,128)(2,1)S(1)} %get-tuple-element.97), channel_id=1, source_target_pairs={{0,4},{1,5},{2,6},{3,7},{4,0},{5,1},{6,2},{7,3},{8,12},{9,13},{10,... | collective-permute-start | bytes 196616 | tf_op jit(solution)/shard_map/ppermute | solution.py:300
  67.8 1.9 %collective-permute-done.13 = bf16[2,128,128]{2,1,0:T(8,128)(2,1)S(1)} collective-permute-done((bf16[2,128,128]{2,1,0:T(8,128)(2,1)S(1)}, bf16[2,128,128]{2,1,0:T(8,128)(2,1)S(1)}, u32[]{:S(2)}, u32[]{:S(2)}) %collective-permute-start.13) | collective-permute-done | bytes 65568 | tf_op jit(solution)/shard_map/ppermute | solution.py:300
  69.8 2.6 %collective-permute-done.15 = bf16[2,128,128]{2,1,0:T(8,128)(2,1)S(1)} collective-permute-done((bf16[2,128,128]{2,1,0:T(8,128)(2,1)S(1)}, bf16[2,128,128]{2,1,0:T(8,128)(2,1)S(1)}, u32[]{:S(2)}, u32[]{:S(2)}) %collective-permute-start.15) | collective-permute-done | bytes 65568 | tf_op jit(solution)/shard_map/ppermute | solution.py:300
  72.4 1.5 %collective-permute-start.16 = (bf16[2,64,2048]{2,1,0:T(8,128)(2,1)S(1)}, bf16[2,64,2048]{2,1,0:T(8,128)(2,1)S(1)}, u32[]{:S(2)}, u32[]{:S(2)}) collective-permute-start(bf16[2,64,2048]{2,1,0:T(8,128)(2,1)S(1)} %get-tuple-element.87), channel_id=1, source_target_pairs={{4,0},{8,4},{12,8},{16,12},{20,16},{24,20},{28,24},{5,1},{9,5},{13... | collective-permute-start | bytes 1572872 | tf_op jit(solution)/shard_map/ppermute | solution.py:306
  73.9 9.7 %collective-permute-start.19 = (bf16[2,128,128]{2,1,0:T(8,128)(2,1)S(1)}, bf16[2,128,128]{2,1,0:T(8,128)(2,1)S(1)}, u32[]{:S(2)}, u32[]{:S(2)}) collective-permute-start(bf16[2,128,128]{2,1,0:T(8,128)(2,1)S(1)} %fusion.14), channel_id=1, source_target_pairs={{0,24},{1,25},{2,26},{3,27},{4,28},{5,29},{6,30},{7,31},{8,16},{9,... | collective-permute-start | bytes 196616 | tf_op jit(solution)/shard_map/ppermute | solution.py:300
  84.2 12.9 %collective-permute-done.19 = bf16[2,128,128]{2,1,0:T(8,128)(2,1)S(1)} collective-permute-done((bf16[2,128,128]{2,1,0:T(8,128)(2,1)S(1)}, bf16[2,128,128]{2,1,0:T(8,128)(2,1)S(1)}, u32[]{:S(2)}, u32[]{:S(2)}) %collective-permute-start.19) | collective-permute-done | bytes 65568 | tf_op jit(solution)/shard_map/ppermute | solution.py:300
  98.3 2.2 %collective-permute-start.23 = (bf16[2,128,128]{2,1,0:T(8,128)(2,1)S(1)}, bf16[2,128,128]{2,1,0:T(8,128)(2,1)S(1)}, u32[]{:S(2)}, u32[]{:S(2)}) collective-permute-start(bf16[2,128,128]{2,1,0:T(8,128)(2,1)S(1)} %add_convert_fusion.4.refs_0_), channel_id=1, source_target_pairs={{0,4},{1,5},{2,6},{3,7},{4,0},{5,1},{6,2},{7,3},{8,12},{9,13},{10,... | collective-permute-start | bytes 196616 | tf_op jit(solution)/shard_map/ppermute | solution.py:300
  101.7 1.7 %collective-permute-done.24.refs_5_ = bf16[2,128,128]{2,1,0:T(8,128)(2,1)S(1)} collective-permute-done((bf16[2,128,128]{2,1,0:T(8,128)(2,1)S(1)}, bf16[2,128,128]{2,1,0:T(8,128)(2,1)S(1)}, u32[]{:S(2)}, u32[]{:S(2)}) %collective-permute-start.24) | collective-permute-done | bytes 65568 | tf_op jit(solution)/shard_map/ppermute | solution.py:300
  104.7 4.4 %output_part.1 = (bf16[128,2048]{1,0:T(8,128)(2,1)}, bf16[128,2048]{1,0:T(8,128)(2,1)}, bf16[128,2048]{1,0:T(8,128)(2,1)}, bf16[128,2048]{1,0:T(8,128)(2,1)}, f32[64,2048]{1,0:T(8,128)S(1)}) custom-call(bf16[128,2048]{1,0:T(8,128)(2,1)S(1)} %bitcast.37, bf16[128,2048]{1,0:T(8,128)(2,1)S(1)} %bitcast.44, bf16[16,128,128]{2,1,0:T(8,128)(2,1)S(1)} %copy-done.5, ...), custom_call_target="tpu_custom_call" | custom-call | flops 3000 | bytes 1000 | tf_op jit(solution)/shard_map/output_part/pallas_call | solution.py:67
  (78 shorter events, 23.9 us)
Async XLA Ops:
  4.2 10.1 %collective-permute-start = (bf16[2,4,128,128]{3,2,1,0:T(8,128)(2,1)S(1)}, bf16[2,4,128,128]{3,2,1,0:T(8,128)(2,1)S(1)}, u32[]{:S(2)}, u32[]{:S(2)}) collective-permute-start(bf16[2,4,128,128]{3,2,1,0:T(8,128)(2,1)S(1)} %get-tuple-element.52), channel_id=1, source_target_pairs={{0,4},{4,0},{8,12},{12,8},{16,20},{20,16},{24,28},{28,24},{1,5},{5... | collective-permute-start | bytes 786440 | tf_op jit(solution)/shard_map/ppermute | solution.py:290
  7.2 12.0 %collective-permute-start.4 = (bf16[2,4,128,128]{3,2,1,0:T(8,128)(2,1)S(1)}, bf16[2,4,128,128]{3,2,1,0:T(8,128)(2,1)}, u32[]{:S(2)}, u32[]{:S(2)}) collective-permute-start(bf16[2,4,128,128]{3,2,1,0:T(8,128)(2,1)S(1)} %get-tuple-element.54), channel_id=1, source_target_pairs={{0,4},{4,0},{8,12},{12,8},{16,20},{20,16},{24,28},{28,24},{1,5},{5... | collective-permute-start | bytes 786440 | tf_op jit(solution)/shard_map/ppermute | solution.py:290
  15.1 11.1 %collective-permute-start.1 = (bf16[4,128,128]{2,1,0:T(8,128)(2,1)}, bf16[4,128,128]{2,1,0:T(8,128)(2,1)S(1)}, u32[]{:S(2)}, u32[]{:S(2)}) collective-permute-start(bf16[4,128,128]{2,1,0:T(8,128)(2,1)} %fusion.11), channel_id=1, source_target_pairs={{0,8},{8,0},{4,12},{12,4},{16,24},{24,16},{20,28},{28,20},{1,9},{9... | collective-permute-start | bytes 393224 | tf_op jit(solution)/shard_map/ppermute | solution.py:320
  20.9 5.3 %collective-permute-start.6 = (bf16[4,128,128]{2,1,0:T(8,128)(2,1)}, bf16[4,128,128]{2,1,0:T(8,128)(2,1)}, u32[]{:S(2)}, u32[]{:S(2)}) collective-permute-start(bf16[4,128,128]{2,1,0:T(8,128)(2,1)} %fusion.10), channel_id=1, source_target_pairs={{0,8},{8,0},{4,12},{12,4},{16,24},{24,16},{20,28},{28,20},{1,9},{9... | collective-permute-start | bytes 393224 | tf_op jit(solution)/shard_map/ppermute | solution.py:320
  22.7 21.2 %collective-permute-start.5 = (bf16[2,64,2048]{2,1,0:T(8,128)(2,1)}, bf16[2,64,2048]{2,1,0:T(8,128)(2,1)S(1)}, u32[]{:S(2)}, u32[]{:S(2)}) collective-permute-start(bf16[2,64,2048]{2,1,0:T(8,128)(2,1)} %pad_maximum_fusion), channel_id=1, source_target_pairs={{0,4},{4,8},{8,12},{12,16},{16,20},{20,24},{24,28},{1,5},{5,9},{9,... | collective-permute-start | bytes 1572872 | tf_op jit(solution)/shard_map/ppermute | solution.py:306
  27.4 7.8 %collective-permute-start.3 = (bf16[4,128,128]{2,1,0:T(8,128)(2,1)S(1)}, bf16[4,128,128]{2,1,0:T(8,128)(2,1)S(1)}, u32[]{:S(2)}, u32[]{:S(2)}) collective-permute-start(bf16[4,128,128]{2,1,0:T(8,128)(2,1)S(1)} %fusion.8), channel_id=1, source_target_pairs={{8,24},{16,0},{12,28},{20,4},{9,25},{17,1},{13,29},{21,5},{10,26},... | collective-permute-start | bytes 393224 | tf_op jit(solution)/shard_map/ppermute | solution.py:320
  28.7 6.5 %collective-permute-start.2 = (bf16[4,128,128]{2,1,0:T(8,128)(2,1)S(1)}, bf16[4,128,128]{2,1,0:T(8,128)(2,1)S(1)}, u32[]{:S(2)}, u32[]{:S(2)}) collective-permute-start(bf16[4,128,128]{2,1,0:T(8,128)(2,1)S(1)} %fusion.8), channel_id=1, source_target_pairs={{8,16},{16,8},{12,20},{20,12},{9,17},{17,9},{13,21},{21,13},{10,18... | collective-permute-start | bytes 393224 | tf_op jit(solution)/shard_map/ppermute | solution.py:320
  30.0 12.9 %collective-permute-start.8 = (bf16[4,128,128]{2,1,0:T(8,128)(2,1)}, bf16[4,128,128]{2,1,0:T(8,128)(2,1)S(1)}, u32[]{:S(2)}, u32[]{:S(2)}) collective-permute-start(bf16[4,128,128]{2,1,0:T(8,128)(2,1)} %fusion.9), channel_id=1, source_target_pairs={{8,24},{16,0},{12,28},{20,4},{9,25},{17,1},{13,29},{21,5},{10,26},... | collective-permute-start | bytes 393224 | tf_op jit(solution)/shard_map/ppermute | solution.py:320
  31.3 11.6 %collective-permute-start.7 = (bf16[4,128,128]{2,1,0:T(8,128)(2,1)}, bf16[4,128,128]{2,1,0:T(8,128)(2,1)}, u32[]{:S(2)}, u32[]{:S(2)}) collective-permute-start(bf16[4,128,128]{2,1,0:T(8,128)(2,1)} %fusion.9), channel_id=1, source_target_pairs={{8,16},{16,8},{12,20},{20,12},{9,17},{17,9},{13,21},{21,13},{10,18... | collective-permute-start | bytes 393224 | tf_op jit(solution)/shard_map/ppermute | solution.py:320
  45.5 14.1 %collective-permute-start.9 = (bf16[2,4,128,128]{3,2,1,0:T(8,128)(2,1)S(1)}, bf16[2,4,128,128]{3,2,1,0:T(8,128)(2,1)S(1)}, u32[]{:S(2)}, u32[]{:S(2)}) collective-permute-start(bf16[2,4,128,128]{3,2,1,0:T(8,128)(2,1)S(1)} %get-tuple-element.93), channel_id=1, source_target_pairs={{0,4},{4,0},{8,12},{12,8},{16,20},{20,16},{24,28},{28,24},{1,5},{5... | collective-permute-start | bytes 786440 | tf_op jit(solution)/shard_map/ppermute | solution.py:290
  47.7 13.1 %collective-permute-start.10 = (bf16[2,4,128,128]{3,2,1,0:T(8,128)(2,1)S(1)}, bf16[2,4,128,128]{3,2,1,0:T(8,128)(2,1)S(1)}, u32[]{:S(2)}, u32[]{:S(2)}) collective-permute-start(bf16[2,4,128,128]{3,2,1,0:T(8,128)(2,1)S(1)} %get-tuple-element.99.rest_0_), channel_id=1, source_target_pairs={{0,4},{4,0},{8,12},{12,8},{16,20},{20,16},{24,28},{28,24},{1,5},{5... | collective-permute-start | bytes 786440 | tf_op jit(solution)/shard_map/ppermute | solution.py:290
  63.5 4.3 %collective-permute-start.14 = (bf16[2,128,128]{2,1,0:T(8,128)(2,1)S(1)}, bf16[2,128,128]{2,1,0:T(8,128)(2,1)S(1)}, u32[]{:S(2)}, u32[]{:S(2)}) collective-permute-start(bf16[2,128,128]{2,1,0:T(8,128)(2,1)S(1)} %slice_bitcast_fusion.1), channel_id=1, source_target_pairs={{0,2},{1,3},{2,0},{3,1},{4,6},{5,7},{6,4},{7,5},{8,10},{9,11},{10,... | collective-permute-start | bytes 196616 | tf_op jit(solution)/shard_map/ppermute | solution.py:300
  65.2 4.6 %collective-permute-start.13 = (bf16[2,128,128]{2,1,0:T(8,128)(2,1)S(1)}, bf16[2,128,128]{2,1,0:T(8,128)(2,1)S(1)}, u32[]{:S(2)}, u32[]{:S(2)}) collective-permute-start(bf16[2,128,128]{2,1,0:T(8,128)(2,1)S(1)} %get-tuple-element.97), channel_id=1, source_target_pairs={{0,4},{1,5},{2,6},{3,7},{4,0},{5,1},{6,2},{7,3},{8,12},{9,13},{10,... | collective-permute-start | bytes 196616 | tf_op jit(solution)/shard_map/ppermute | solution.py:300
  67.2 5.2 %collective-permute-start.15 = (bf16[2,128,128]{2,1,0:T(8,128)(2,1)S(1)}, bf16[2,128,128]{2,1,0:T(8,128)(2,1)S(1)}, u32[]{:S(2)}, u32[]{:S(2)}) collective-permute-start(bf16[2,128,128]{2,1,0:T(8,128)(2,1)S(1)} %get-tuple-element.98), channel_id=1, source_target_pairs={{0,6},{1,7},{2,4},{3,5},{4,2},{5,3},{6,0},{7,1},{8,14},{9,15},{10,... | collective-permute-start | bytes 196616 | tf_op jit(solution)/shard_map/ppermute | solution.py:300
  72.4 37.8 %collective-permute-start.16 = (bf16[2,64,2048]{2,1,0:T(8,128)(2,1)S(1)}, bf16[2,64,2048]{2,1,0:T(8,128)(2,1)S(1)}, u32[]{:S(2)}, u32[]{:S(2)}) collective-permute-start(bf16[2,64,2048]{2,1,0:T(8,128)(2,1)S(1)} %get-tuple-element.87), channel_id=1, source_target_pairs={{4,0},{8,4},{12,8},{16,12},{20,16},{24,20},{28,24},{5,1},{9,5},{13... | collective-permute-start | bytes 1572872 | tf_op jit(solution)/shard_map/ppermute | solution.py:306
  73.9 23.2 %collective-permute-start.19 = (bf16[2,128,128]{2,1,0:T(8,128)(2,1)S(1)}, bf16[2,128,128]{2,1,0:T(8,128)(2,1)S(1)}, u32[]{:S(2)}, u32[]{:S(2)}) collective-permute-start(bf16[2,128,128]{2,1,0:T(8,128)(2,1)S(1)} %fusion.14), channel_id=1, source_target_pairs={{0,24},{1,25},{2,26},{3,27},{4,28},{5,29},{6,30},{7,31},{8,16},{9,... | collective-permute-start | bytes 196616 | tf_op jit(solution)/shard_map/ppermute | solution.py:300
  83.5 14.6 %collective-permute-start.18 = (bf16[2,128,128]{2,1,0:T(8,128)(2,1)S(1)}, bf16[2,128,128]{2,1,0:T(8,128)(2,1)S(1)}, u32[]{:S(2)}, u32[]{:S(2)}) collective-permute-start(bf16[2,128,128]{2,1,0:T(8,128)(2,1)S(1)} %fusion.14), channel_id=1, source_target_pairs={{0,16},{1,17},{2,18},{3,19},{4,20},{5,21},{6,22},{7,23},{8,24},{9,... | collective-permute-start | bytes 196616 | tf_op jit(solution)/shard_map/ppermute | solution.py:300
  83.5 14.6 %collective-permute-start.17 = (bf16[2,128,128]{2,1,0:T(8,128)(2,1)S(1)}, bf16[2,128,128]{2,1,0:T(8,128)(2,1)S(1)}, u32[]{:S(2)}, u32[]{:S(2)}) collective-permute-start(bf16[2,128,128]{2,1,0:T(8,128)(2,1)S(1)} %fusion.14), channel_id=1, source_target_pairs={{0,8},{1,9},{2,10},{3,11},{4,12},{5,13},{6,14},{7,15},{8,0},{9,1},... | collective-permute-start | bytes 196616 | tf_op jit(solution)/shard_map/ppermute | solution.py:300
  98.2 5.2 %collective-permute-start.24 = (bf16[2,128,128]{2,1,0:T(8,128)(2,1)S(1)}, bf16[2,128,128]{2,1,0:T(8,128)(2,1)S(1)}, u32[]{:S(2)}, u32[]{:S(2)}) collective-permute-start(bf16[2,128,128]{2,1,0:T(8,128)(2,1)S(1)} %add_convert_fusion.4.refs_0_), channel_id=1, source_target_pairs={{0,6},{1,7},{2,4},{3,5},{4,2},{5,3},{6,0},{7,1},{8,14},{9,15},{10,... | collective-permute-start | bytes 196616 | tf_op jit(solution)/shard_map/ppermute | solution.py:300
  98.3 5.2 %collective-permute-start.23 = (bf16[2,128,128]{2,1,0:T(8,128)(2,1)S(1)}, bf16[2,128,128]{2,1,0:T(8,128)(2,1)S(1)}, u32[]{:S(2)}, u32[]{:S(2)}) collective-permute-start(bf16[2,128,128]{2,1,0:T(8,128)(2,1)S(1)} %add_convert_fusion.4.refs_0_), channel_id=1, source_target_pairs={{0,4},{1,5},{2,6},{3,7},{4,0},{5,1},{6,2},{7,3},{8,12},{9,13},{10,... | collective-permute-start | bytes 196616 | tf_op jit(solution)/shard_map/ppermute | solution.py:300
  101.7 7.4 %collective-permute-start.21 = (bf16[2,128,128]{2,1,0:T(8,128)(2,1)S(1)}, bf16[2,128,128]{2,1,0:T(8,128)(2,1)S(1)}, u32[]{:S(2)}, u32[]{:S(2)}) collective-permute-start(bf16[2,128,128]{2,1,0:T(8,128)(2,1)S(1)} %add_convert_fusion.4.refs_0_), channel_id=1, source_target_pairs={{0,1},{1,0},{2,3},{3,2},{4,5},{5,4},{6,7},{7,6},{8,9},{9,8},{10,11... | collective-permute-start | bytes 196616 | tf_op jit(solution)/shard_map/ppermute | solution.py:300
  103.4 5.7 %collective-permute-start.26 = (bf16[2,128,128]{2,1,0:T(8,128)(2,1)S(1)}, bf16[2,128,128]{2,1,0:T(8,128)(2,1)S(1)}, u32[]{:S(2)}, u32[]{:S(2)}) collective-permute-start(bf16[2,128,128]{2,1,0:T(8,128)(2,1)S(1)} %collective-permute-done.24.refs_5_), channel_id=1, source_target_pairs={{0,1},{1,0},{2,3},{3,2},{4,5},{5,4},{6,7},{7,6},{8,9},{9,8},{10,11... | collective-permute-start | bytes 196616 | tf_op jit(solution)/shard_map/ppermute | solution.py:300
  103.4 5.7 %collective-permute-start.25 = (bf16[2,128,128]{2,1,0:T(8,128)(2,1)S(1)}, bf16[2,128,128]{2,1,0:T(8,128)(2,1)S(1)}, u32[]{:S(2)}, u32[]{:S(2)}) collective-permute-start(bf16[2,128,128]{2,1,0:T(8,128)(2,1)S(1)} %collective-permute-done.23.refs_4_), channel_id=1, source_target_pairs={{0,1},{1,0},{2,3},{3,2},{4,5},{5,4},{6,7},{7,6},{8,9},{9,8},{10,11... | collective-permute-start | bytes 196616 | tf_op jit(solution)/shard_map/ppermute | solution.py:300
  104.7 4.5 %collective-permute-start.22 = (bf16[2,128,128]{2,1,0:T(8,128)(2,1)S(1)}, bf16[2,128,128]{2,1,0:T(8,128)(2,1)S(1)}, u32[]{:S(2)}, u32[]{:S(2)}) collective-permute-start(bf16[2,128,128]{2,1,0:T(8,128)(2,1)S(1)} %collective-permute-done.20.refs_1_), channel_id=1, source_target_pairs={{0,1},{1,0},{2,3},{3,2},{4,5},{5,4},{6,7},{7,6},{8,9},{9,8},{10,11... | collective-permute-start | bytes 196616 | tf_op jit(solution)/shard_map/ppermute | solution.py:300
  (12 other events, 83.0 us)

commit v3 on v2

v3 whole, which is shorter than its diff:
```python
import functools

import jax
import jax.numpy as jnp
from jax import lax
from jax.experimental import pallas as pl
from jax.experimental.pallas import tpu as pltpu
from jax.sharding import PartitionSpec as P

HEADS = 16
HD = 128
WINDOW = 64
HALF = HEADS // 2
CHUNKS = 2
CHUNK = HALF // CHUNKS
GROUP = 2
WINDOW_GROUP = 4
WIDE = HEADS * HD
VMEM = 8 * 1024 * 1024
BF = jnp.bfloat16
F32 = jnp.float32


def dot(left, right):
    return jnp.dot(left, right, preferred_element_type=F32)


def dot_nt(left, right):
    return lax.dot_general(left, right, (((1,), (1,)), ((), ())), preferred_element_type=F32)


def dot_tn(left, right):
    return lax.dot_general(left, right, (((0,), (0,)), ((), ())), preferred_element_type=F32)


def phi(before):
    return jnp.where(before > 0, before + 1.0, jnp.exp(jnp.minimum(before, 0.0)))


def col(head):
    return slice(head * HD, (head + 1) * HD)


def col_of(half, head):
    return pl.ds(pl.multiple_of(half * (HALF * HD) + head * HD, HD), HD)


def own_half():
    return lax.axis_index("seq") % 2


def lin_scale(tokens):
    return 1.0 / (HD * tokens * lax.axis_size("seq"))


def cost(microseconds):
    return pl.CostEstimate(
        flops=int(microseconds * 1000), bytes_accessed=1000, transcendentals=0
    )


def array(shape, kind):
    return jax.ShapeDtypeStruct(shape, kind)


def call(kernel, name, outs, operands, in_hbm=0, unread=0, microseconds=3, **more):
    whole = pl.BlockSpec(memory_space=pltpu.VMEM)
    return pl.pallas_call(
        kernel,
        in_specs=[pl.BlockSpec(memory_space=pltpu.HBM)] * in_hbm
        + [whole] * (len(operands) - in_hbm - unread)
        + [pl.BlockSpec(memory_space=pl.ANY)] * unread,
        out_specs=[whole] * len(outs),
        out_shape=outs,
        cost_estimate=cost(microseconds),
        compiler_params=pltpu.CompilerParams(vmem_limit_bytes=VMEM),
        name=name,
        **more,
    )(*operands)


def feature_kernel(first, lq, lk, v, g, fm, *rest):
    fq_out, fk_out, *t_out, rows, maps, arrived = rest[-5 - CHUNKS :]
    half = 1 - own_half() if first else own_half()

    def copies(step):
        head = half * HALF + step * GROUP
        wide = pl.ds(pl.multiple_of(head * HD, GROUP * HD), GROUP * HD)
        here = slice(step * GROUP * HD, (step + 1) * GROUP * HD)
        pairs = [(ref.at[:, wide], rows.at[n, :, here]) for n, ref in enumerate((lq, lk, v, g))]
        pairs.append((fm.at[pl.ds(head, GROUP)], maps.at[step * GROUP : (step + 1) * GROUP]))
        return [
            pltpu.make_async_copy(source, target, arrived.at[step, n])
            for n, (source, target) in enumerate(pairs)
        ]

    started = [copies(step) for step in range(HALF // GROUP)]
    for step in started:
        for copy in step:
            copy.start()
    for step, arriving in enumerate(started):
        for copy in arriving:
            copy.wait()
        heads = range(step * GROUP, (step + 1) * GROUP)
        pre = [(dot(rows[0, :, col(h)], maps[h]), dot(rows[1, :, col(h)], maps[h])) for h in heads]
        feats = [(phi(q).astype(BF), phi(k).astype(BF)) for q, k in pre]
        for h, (fq, fk) in zip(heads, feats):
            fq_out[:, col(h)], fk_out[:, col(h)] = fq, fk
        sums = [
            (dot_tn(fk, rows[2, :, col(h)]), dot_tn(fq, rows[3, :, col(h)]))
            for h, (fq, fk) in zip(heads, feats)
        ]
        for h, (forward, backward) in zip(heads, sums):
            t_out[h // CHUNK][0, h % CHUNK] = forward.astype(BF)
            t_out[h // CHUNK][1, h % CHUNK] = backward.astype(BF)


def features(lq, lk, v, g, fm, follows):
    tokens = lq.shape[0]
    row = array((tokens, HALF * HD), BF)
    lq, lk, v, g, fm = (pltpu.with_memory_space_constraint(x, pltpu.HBM) for x in (lq, lk, v, g, fm))
    return call(
        functools.partial(feature_kernel, not follows),
        "features",
        [row, row] + [array((2, CHUNK, HD, HD), BF)] * CHUNKS,
        (lq, lk, v, g, fm, *follows),
        in_hbm=5,
        unread=len(follows),
        scratch_shapes=[
            pltpu.VMEM((4, tokens, HALF * HD), BF),
            pltpu.VMEM((HALF, HD, HD), BF),
            pltpu.SemaphoreType.DMA((HALF // GROUP, 5)),
        ],
    )


def causal_mask(tokens):
    rows = lax.broadcasted_iota(jnp.int32, (tokens, tokens), 0)
    cols = lax.broadcasted_iota(jnp.int32, (tokens, tokens), 1)
    return rows >= cols


def window_kernel(wq, wk, v, g, rims, *rest):
    win, dv, dwq, dwk, edge = rest[-5:]
    tokens = wq.shape[0]
    root = HD ** (-0.5)
    rows = lax.broadcasted_iota(jnp.int32, (tokens, 2 * WINDOW), 0)
    cols = lax.broadcasted_iota(jnp.int32, (tokens, 2 * WINDOW), 1)
    offset = cols - rows % WINDOW
    absent = (lax.axis_index("seq") == 0) & (rows < WINDOW) & (cols < WINDOW)
    band = (offset >= 1) & (offset <= WINDOW) & jnp.logical_not(absent)
    blocks = range(tokens // WINDOW)

    def rows_of(block):
        return slice(block * WINDOW, (block + 1) * WINDOW)

    def pairs(ref, rim, c):
        first = jnp.concatenate([rims[rim, :, c], ref[:WINDOW, c]], axis=0)
        return [first] + [ref[(n - 1) * WINDOW : (n + 1) * WINDOW, c] for n in blocks[1:]]

    def by_block(form, lefts, rights):
        return jnp.concatenate([form(a, b) for a, b in zip(lefts, rights)], axis=0)

    for start in range(0, HEADS, WINDOW_GROUP):
        at = [col(h) for h in range(start, start + WINDOW_GROUP)]
        q = [[wq[rows_of(n), c] for n in blocks] for c in at]
        grad = [[g[rows_of(n), c] for n in blocks] for c in at]
        keys, vals = [pairs(wk, 0, c) for c in at], [pairs(v, 1, c) for c in at]
        score = [by_block(dot_nt, a, b) for a, b in zip(q, keys)]
        dprob = [by_block(dot_nt, a, b) for a, b in zip(grad, vals)]
        score = [jnp.where(band, x * root, -jnp.inf) for x in score]
        top = [jnp.max(x, axis=-1, keepdims=True) for x in score]
        expo = [jnp.exp(x - y) for x, y in zip(score, top)]
        prob = [x / jnp.sum(x, axis=-1, keepdims=True) for x in expo]
        delta = [jnp.sum(x * y, axis=-1, keepdims=True) for x, y in zip(prob, dprob)]
        dscore = [
            (x * (y - z) * root).astype(BF) for x, y, z in zip(prob, dprob, delta)
        ]
        prob = [x.astype(BF) for x in prob]
        prob = [[x[rows_of(n)] for n in blocks] for x in prob]
        dscore = [[x[rows_of(n)] for n in blocks] for x in dscore]
        for i, c in enumerate(at):
            win[:, c] = by_block(dot, prob[i], vals[i])
            dwq[:, c] = by_block(dot, dscore[i], keys[i]).astype(BF)
        for i, c in enumerate(at):
            dk = [dot_tn(x, y) for x, y in zip(dscore[i], q[i])]
            dval = [dot_tn(x, y) for x, y in zip(prob[i], grad[i])]
            edge[0, :, c], edge[1, :, c] = dk[0][:WINDOW].astype(BF), dval[0][:WINDOW].astype(BF)
            for n in blocks:
                more = n + 1 < len(blocks)
                a, b = dk[n][WINDOW:], dval[n][WINDOW:]
                dwk[rows_of(n), c] = a + dk[n + 1][:WINDOW] if more else a
                dv[rows_of(n), c] = b + dval[n + 1][:WINDOW] if more else b


def window_part(*operands):
    wide = array(operands[0].shape, F32)
    return call(
        window_kernel,
        "window_part",
        [wide, wide, array(wide.shape, BF), wide, array((2, WINDOW, WIDE), BF)],
        operands,
        unread=len(operands) - 5,
    )


def state_kernel(first, count, lq, lk, v, g, fq, fk, *rest):
    states, (dpq_out, dpk_out, keep, send) = rest[:count], rest[-4:]
    core, far = lax.axis_index("dp") % 2, lax.axis_index("dp") // 2
    side = 0 if count == CHUNKS else 1
    half = own_half() if side == 0 else 1 - own_half()
    scale = lin_scale(lq.shape[0])
    causal = causal_mask(lq.shape[0])
    if side == 1:
        keep[0], send[0] = rest[count][0], rest[count + 1][0]
        if first > 0:
            keep[1, :, :first] = rest[count][1, :, :first]
            send[1, :, :first] = rest[count + 1][1, :, :first]
    for n in range(count):
        heads = [(first + n) * CHUNK + h for h in range(CHUNK)]
        at = [col_of(half, head) for head in heads]
        q_feat, k_feat = [fq[:, col(x)] for x in heads], [fk[:, col(x)] for x in heads]
        val, grad = [v[:, x] for x in at], [g[:, x] for x in at]
        mixed = [jnp.where(causal, dot_nt(a, b), 0.0).astype(BF) for a, b in zip(grad, val)]
        dfq = [dot_nt(a, states[n][0, h]) for h, a in enumerate(grad)]
        dfk = [dot_nt(a, states[n][1, h]) for h, a in enumerate(val)]
        dfq = [(a + dot(b, c)) * scale for a, b, c in zip(dfq, mixed, k_feat)]
        dfk = [(a + dot_tn(b, c)) * scale for a, b, c in zip(dfk, mixed, q_feat)]
        dpq = [(a * jnp.minimum(b.astype(F32), 1.0)).astype(BF) for a, b in zip(dfq, q_feat)]
        dpk = [(a * jnp.minimum(b.astype(F32), 1.0)).astype(BF) for a, b in zip(dfk, k_feat)]
        terms = [
            (dot_tn(lq[:, x], a) + dot_tn(lk[:, x], b)).astype(BF)
            for x, a, b in zip(at, dpq, dpk)
        ]
        for h in range(CHUNK):
            here = col(n * CHUNK + h)
            dpq_out[:, here], dpk_out[:, here] = dpq[h], dpk[h]
        for y in range(2):
            keep[side, y ^ far, first + n] = jnp.where(core == 0, terms[y], terms[2 + y])
            send[side, y ^ far, first + n] = jnp.where(core == 0, terms[2 + y], terms[y])


def state_part(first, count, arrays, states, earlier, follows=()):
    row = array((arrays[0].shape[0], count * CHUNK * HD), BF)
    part = array((2, 2, CHUNKS, HD, HD), BF)
    return call(
        functools.partial(state_kernel, first, count),
        "state_part",
        [row, row, part, part],
        (*arrays, *states, *earlier, *follows),
        unread=len(follows),
    )


def output_kernel(v, g, fm, win, dv_win, dq, dk, edge, *rest):
    att, dlq, dlk, dv, dwq, dwk, token = rest[-7:]
    token[...] = jnp.zeros_like(token)
    scale = lin_scale(v.shape[0])
    causal = causal_mask(v.shape[0])
    tail = v.shape[0] - WINDOW
    dwq[...] = dq[...]
    dwk[:tail] = dk[:tail].astype(BF)
    dwk[tail:] = (dk[tail:] + edge[0].astype(F32)).astype(BF)
    for side in range(2):
        half = own_half() ^ side
        refs = rest[: 2 + CHUNKS + 2] if side == 0 else rest[2 + CHUNKS + 2 : -7]
        fq, fk = refs[:2]
        states, pairs = refs[2 : 2 + CHUNKS], refs[2 + CHUNKS :]
        each = 2 * HALF // len(pairs)
        for n in range(CHUNKS):
            heads = [n * CHUNK + k for k in range(CHUNK)]
            cols = [(col(h), col_of(half, h)) for h in heads]
            scores = [
                jnp.where(causal, dot_nt(fq[:, c], fk[:, c]), 0.0).astype(BF) for c, _ in cols
            ]
            for h, (_, at) in zip(heads, cols):
                m, here, w = 2 * (h // each), col(h % each), fm[half * HALF + h]
                dlq[:, at] = dot_nt(pairs[m][:, here], w).astype(BF)
                dlk[:, at] = dot_nt(pairs[m + 1][:, here], w).astype(BF)
            lin = [dot(fq[:, c], states[n][0, k]) for k, (c, _) in enumerate(cols)]
            grad_v = [dot(fk[:, c], states[n][1, k]) for k, (c, _) in enumerate(cols)]
            for k, (_, at) in enumerate(cols):
                out = (lin[k] + dot(scores[k], v[:, at])) * scale
                att[:, at] = (out + win[:, at]).astype(BF)
                out = (grad_v[k] + dot_tn(scores[k], g[:, at])) * scale + dv_win[:, at]
                dv[:tail, at] = out[:tail].astype(BF)
                dv[tail:, at] = (out[tail:] + edge[1, :, at].astype(F32)).astype(BF)


def output_part(v, g, fm, windows, own, other):
    row = array(v.shape, BF)
    return call(
        output_kernel, "output_part", [row] * 6 + [array((8, HD), F32)], (v, g, fm, *windows, *own, *other)
    )


def flipped(block, bit):
    count = lax.axis_size("seq")
    return lax.ppermute(block, "seq", [(i, i ^ bit) for i in range(count)])


def flat_flipped(block, seq_bits, dp_bits):
    rows, width = lax.axis_size("seq"), lax.axis_size("dp")
    route = [
        (s * width + d, (s ^ seq_bits) * width + (d ^ dp_bits))
        for s in range(rows)
        for d in range(width)
    ]
    return lax.ppermute(block, ("seq", "dp"), route)


def passed_along(block, distance):
    devices = range(lax.axis_size("seq"))
    route = [(i - distance, i) for i in devices if i - distance in devices]
    return lax.ppermute(block, "seq", route)


def spread(block, level):
    count = lax.axis_size("seq")
    size = 2 << level
    arrived = []
    for turn in range(1 << level):
        route = []
        for base in range(0, count // 2, size):
            low, high = base + size // 2 - 1, base + size // 2
            for parity in range(2):
                route.append((2 * low + parity, 2 * (high + turn) + parity))
                route.append((2 * high + parity, 2 * (low - turn) + parity))
        arrived.append(lax.ppermute(block, "seq", route))
    return arrived


def levels():
    return (lax.axis_size("seq") // 2).bit_length() - 1


def upper(level):
    return ((lax.axis_index("seq") // 2) >> level) % 2 == 1


def sides(gots):
    low = high = None
    for level, arrived in enumerate(gots):
        got = sum(x[...].astype(F32) for x in arrived)
        above = upper(level)
        a, b = jnp.where(above, got, 0.0), jnp.where(above, 0.0, got)
        low, high = (a, b) if low is None else (low + a, high + b)
    return low, high


def by_level(refs):
    gots, at = [], 0
    while at < len(refs):
        count = 1 << len(gots)
        gots.append(refs[at : at + count])
        at += count
    return gots


def pair_kernel(kept, came, pair, send):
    total = kept[...].astype(F32) + came[...].astype(F32)
    pair[...] = total.astype(BF)
    send[...] = jnp.where(upper(0), total[1], total[0]).astype(BF)


def pair_sum(kept, came):
    return call(
        pair_kernel, "pair_sum", [array(kept.shape, BF), array(kept.shape[1:], BF)], (kept, came)
    )


def level_kernel(pair, *refs):
    *gots, send = refs
    gots = by_level(gots)
    low, high = sides(gots)
    above = upper(len(gots))
    send[...] = jnp.where(
        above, pair[1].astype(F32) + high, pair[0].astype(F32) + low
    ).astype(BF)


def level_sum(pair, gots):
    return call(level_kernel, "level_sum", [array(pair.shape[1:], BF)], (pair, *gots))[0]


def entering_kernel(kept, came, *refs):
    *gots, mine, others = refs
    low, high = sides(by_level(gots))
    zero = jnp.zeros_like(low)
    low, high = (zero, zero) if low is None else (low, high)
    first = own_half() == 0
    mine[0] = (low + jnp.where(first, zero, came[0].astype(F32))).astype(BF)
    mine[1] = (high + jnp.where(first, came[1].astype(F32), zero)).astype(BF)
    others[0] = (low + jnp.where(first, kept[0].astype(F32), zero)).astype(BF)
    others[1] = (high + jnp.where(first, zero, kept[1].astype(F32))).astype(BF)


def entering(kept, came, gots):
    return call(
        entering_kernel, "entering", [array(kept.shape, BF)] * 2, (kept, came, *gots)
    )


def near_kernel(keep, came, mine, a, b, c):
    def total(side, y):
        return keep[side, y].astype(F32) + came[side, y].astype(F32)

    mine[...] = total(0, 0)
    a[...], b[...], c[...] = (total(*at).astype(BF) for at in ((1, 0), (0, 1), (1, 1)))


def near_sum(keep, came):
    part = array(keep.shape[2:], BF)
    return call(
        near_kernel, "near_sum", [array(part.shape, F32), part, part, part], (keep, came)
    )


def total_kernel(count, *refs):
    refs[-1][...] = sum(x[...].astype(F32) for x in refs[:count]).astype(BF)


def total_of(arrays, follows=()):
    return call(
        functools.partial(total_kernel, len(arrays)),
        "total",
        [array(arrays[0].shape, BF)],
        (*arrays, *follows),
        unread=len(follows),
    )[0]


def assemble_kernel(norm, *refs):
    pieces, out = refs[:-1], refs[-1]
    core, far = lax.axis_index("dp") % 2, lax.axis_index("dp") // 2
    for side in range(2):
        half = own_half() ^ side
        for n in range(CHUNKS):
            for c in range(2):
                for y in range(2):
                    head = half * HALF + n * CHUNK + (c ^ core) * 2 + (y ^ far)
                    out[head] = pieces[side * 4 + c * 2 + y][n].astype(F32) * norm


def assemble(pieces, norm):
    return call(
        functools.partial(assemble_kernel, norm), "assemble", [array((HEADS, HD, HD), F32)], pieces
    )[0]


def on_device(
    linear_queries, linear_keys, window_queries, window_keys, values, cotangent, feature_map
):
    tokens = linear_queries.shape[1]
    total_tokens = tokens * lax.axis_size("seq") * lax.axis_size("dp") * linear_queries.shape[0]
    lq, lk, wq, wk, v, g = (
        x[0]
        for x in (linear_queries, linear_keys, window_queries, window_keys, values, cotangent)
    )
    fq_o, fk_o, *given = features(lq, lk, v, g, feature_map, ())
    came = [flipped(x, 1) for x in given]
    ends = jnp.stack([wk[tokens - WINDOW :], v[tokens - WINDOW :]])
    fq, fk, *kept = features(lq, lk, v, g, feature_map, (fq_o,))
    pair, sent = zip(*(pair_sum(a, b) for a, b in zip(kept, came)))
    pair, sent = list(pair), list(sent)
    gots = [[] for _ in range(CHUNKS)]
    for level in range(levels()):
        if level > 0:
            sent = [level_sum(pair[n], gots[n]) for n in range(CHUNKS)]
        for n in range(CHUNKS):
            gots[n] += spread(sent[n], level)
            if level == 0 and n == CHUNKS - 1:
                gots[n], ends = lax.optimization_barrier((gots[n], ends))
                rims = passed_along(ends, 1)
    mine, others = zip(*(entering(kept[n], came[n], gots[n]) for n in range(CHUNKS)))
    back = [flipped(x, 1) for x in others]
    *windows, edge = window_part(wq, wk, v, g, rims, others[-1])
    back[-1], edge = lax.optimization_barrier((back[-1], edge))
    edge = passed_along(edge, -1)
    rows = (lq, lk, v, g)
    dpq, dpk, *terms = state_part(0, CHUNKS, (*rows, fq, fk), mine, (), (others[-1],))
    own = (fq, fk, *mine, dpq, dpk)
    pairs = []
    for n in range(CHUNKS):
        dpq, dpk, *terms = state_part(n, 1, (*rows, fq_o, fk_o), (back[n],), terms)
        pairs += [dpq, dpk]
    other = (fq_o, fk_o, *back, *pairs)
    keep, send = terms
    near, a, b, c = near_sum(keep, flat_flipped(send, 0, 1))
    a, b, c = flat_flipped(a, 1, 0), flat_flipped(b, 0, 2), flat_flipped(c, 1, 2)
    sent = total_of((near, a, b, c))
    came = [flat_flipped(sent, bits, 0) for bits in range(2, lax.axis_size("seq"), 2)]
    attended, dlq, dlk, dv, dwq, dwk, token = output_part(
        v, g, feature_map, (*windows, edge), own, other
    )
    done = total_of((sent, *came), (token,))
    a, b, c = flat_flipped(done, 1, 0), flat_flipped(done, 0, 2), flat_flipped(done, 1, 2)
    across = [flat_flipped(x, 0, 1) for x in (done, b, a, c)]
    map_grad = assemble(
        (done, b, *across[:2], a, c, *across[2:]), total_tokens ** (-0.5)
    )
    return attended[None], dlq[None], dlk[None], dwq[None], dwk[None], dv[None], map_grad


def solution(mesh):
    row = P("dp", "seq", None)
    return jax.shard_map(
        on_device,
        mesh=mesh,
        in_specs=(row,) * 6 + (P(),),
        out_specs=(row,) * 6 + (P(),),
        check_vma=False,
    )
```

time: 112 us -> 90 us (0.80)
  waiting for transfers between devices: 36.3 us -> 26.6 us
  Pallas kernels: 26.6 us -> 17.4 us
  other arithmetic: 7.87 us -> 0.05 us
  starting transfers between devices: 37.3 us -> 44.8 us
  local copies, waits for them, and re-layouts: 2.06 us -> 0.06 us
    ppermute x4, starting transfers between devices: 5.32 us -> 15.2 us  [flipped(): return lax.ppermute(block, 'seq', [(i, i ^ bit) for i in range(count)])]
    ppermute x15 -> x14, waiting for transfers between devices: 22.4 us -> 13.1 us  [flat_flipped(): return lax.ppermute(block, ('seq', 'dp'), route)]
    pallas_call x8 -> x17, Pallas kernels: 25.7 us -> 17.4 us  [call(): pl.pallas_call(kernel, in_specs=[pl.BlockSpec(memory_space=pltpu.HBM)] *...]
    convert_element_type x9 -> x0, other arithmetic: 3.55 us -> none  [the longest x1 1.61 us: entering(): return [(sums.astype(F32) + x.astype(F32)).astype(BF) for x in added]]
    add x3 -> x0, other arithmetic: 2.12 us -> none  [the longest x1 1.14 us: outgoing(): total = pair if sums is None else pair.astype(F32) + sums.astype(F32)]
    ppermute x6, waiting for transfers between devices: 10.3 us -> 8.19 us  [spread(): arrived.append(lax.ppermute(block, 'seq', route))]
    ppermute x15 -> x14, starting transfers between devices: 18.6 us -> 16.7 us  [flat_flipped(): return lax.ppermute(block, ('seq', 'dp'), route)]
    ppermute x4, waiting for transfers between devices: 3.62 us -> 5.23 us  [flipped(): return lax.ppermute(block, 'seq', [(i, i ^ bit) for i in range(count)])]
  transfers between devices with their start and end apart: 27 -> 26, of which waited for: 12 -> 15; matrix products, arithmetic and copies ran while one was open for 6% -> 0% of each run, Pallas kernels for 19% -> 15%
where the time goes in v3:
time: 90 us; the launch traced here: 89.7 us
  starting transfers between devices  44.8 us (50%)
  waiting for transfers between devices  26.6 us (30%)
  Pallas kernels  17.4 us (19%)
    pallas_call x17, Pallas kernels, call(): pl.pallas_call(kernel, in_specs=[pl.BlockSpec(memory_space=pltpu.HBM)] *...  17.4 us
    ppermute x14, starting transfers between devices, flat_flipped(): return lax.ppermute(block, ('seq', 'dp'), route)  16.7 us
    ppermute x4, starting transfers between devices, flipped(): return lax.ppermute(block, 'seq', [(i, i ^ bit) for i in range(count)])  15.2 us
    ppermute x14, waiting for transfers between devices, flat_flipped(): return lax.ppermute(block, ('seq', 'dp'), route)  13.1 us
    ppermute x6, waiting for transfers between devices, spread(): arrived.append(lax.ppermute(block, 'seq', route))  8.19 us
    ppermute x6, starting transfers between devices, spread(): arrived.append(lax.ppermute(block, 'seq', route))  7.75 us
    ppermute x4, waiting for transfers between devices, flipped(): return lax.ppermute(block, 'seq', [(i, i ^ bit) for i in range(count)])  5.23 us
    ppermute x2, starting transfers between devices, passed_along(): return lax.ppermute(block, 'seq', route)  5.15 us
  transfers between devices with their start and end apart: 26, of which 15 were waited for; matrix products, arithmetic and copies ran while one was open for 0% of the time, Pallas kernels for 15%

profile of v3, /device:TPU:0, one launch (start us, length us, event | category | flops | bytes accessed | tf_op | source)
XLA Modules:
  0.0 89.7 jit_solution(8075627224352797459)
XLA Ops:
  0.6 2.8 %features.2 = (bf16[128,1024]{1,0:T(8,128)(2,1)S(1)}, bf16[128,1024]{1,0:T(8,128)(2,1)S(1)}, bf16[2,4,128,128]{3,2,1,0:T(8,128)(2,1)S(1)}, bf16[2,4,128,128]{3,2,1,0:T(8,128)(2,1)S(1)}) custom-call(bf16[128,2048]{1,0:T(8,128)(2,1)} %bitcast.26, bf16[128,2048]{1,0:T(8,128)(2,1)} %bitcast.31, bf16[128,2048]{1,0:T(8,128)(2,1)} %bitcast.12, ...), custom_call_target="tpu_custom_call" | custom-call | flops 3000 | bytes 1000 | tf_op jit(solution)/shard_map/features/pallas_call | solution.py:68
  3.4 3.0 %collective-permute-start = (bf16[2,4,128,128]{3,2,1,0:T(8,128)(2,1)S(1)}, bf16[2,4,128,128]{3,2,1,0:T(8,128)(2,1)S(1)}, u32[]{:S(2)}, u32[]{:S(2)}) collective-permute-start(bf16[2,4,128,128]{3,2,1,0:T(8,128)(2,1)S(1)} %get-tuple-element.57), channel_id=1, source_target_pairs={{0,4},{4,0},{8,12},{12,8},{16,20},{20,16},{24,28},{28,24},{1,5},{5... | collective-permute-start | bytes 786440 | tf_op jit(solution)/shard_map/ppermute | solution.py:299
  6.5 2.8 %features.3 = (bf16[128,1024]{1,0:T(8,128)(2,1)S(1)}, bf16[128,1024]{1,0:T(8,128)(2,1)S(1)}, bf16[2,4,128,128]{3,2,1,0:T(8,128)(2,1)S(1)}, bf16[2,4,128,128]{3,2,1,0:T(8,128)(2,1)S(1)}) custom-call(bf16[128,2048]{1,0:T(8,128)(2,1)} %bitcast.27, bf16[128,2048]{1,0:T(8,128)(2,1)} %bitcast.32, bf16[128,2048]{1,0:T(8,128)(2,1)} %bitcast.13, ...), custom_call_target="tpu_custom_call" | custom-call | flops 3000 | bytes 1000 | tf_op jit(solution)/shard_map/features/pallas_call | solution.py:68
  9.3 4.2 %collective-permute-done.came = bf16[2,4,128,128]{3,2,1,0:T(8,128)(2,1)S(1)} collective-permute-done((bf16[2,4,128,128]{3,2,1,0:T(8,128)(2,1)S(1)}, bf16[2,4,128,128]{3,2,1,0:T(8,128)(2,1)S(1)}, u32[]{:S(2)}, u32[]{:S(2)}) %collective-permute-start) | collective-permute-done | bytes 262176 | tf_op jit(solution)/shard_map/ppermute | solution.py:299
  13.6 2.2 %collective-permute-start.1 = (bf16[4,128,128]{2,1,0:T(8,128)(2,1)S(1)}, bf16[4,128,128]{2,1,0:T(8,128)(2,1)S(1)}, u32[]{:S(2)}, u32[]{:S(2)}) collective-permute-start(bf16[4,128,128]{2,1,0:T(8,128)(2,1)S(1)} %get-tuple-element.58), channel_id=1, source_target_pairs={{0,8},{8,0},{4,12},{12,4},{16,24},{24,16},{20,28},{28,20},{1,9},{9... | collective-permute-start | bytes 393224 | tf_op jit(solution)/shard_map/ppermute | solution.py:329
  15.9 2.9 %collective-permute-done.1.refs_0_ = bf16[4,128,128]{2,1,0:T(8,128)(2,1)S(1)} collective-permute-done((bf16[4,128,128]{2,1,0:T(8,128)(2,1)S(1)}, bf16[4,128,128]{2,1,0:T(8,128)(2,1)S(1)}, u32[]{:S(2)}, u32[]{:S(2)}) %collective-permute-start.1) | collective-permute-done | bytes 131104 | tf_op jit(solution)/shard_map/ppermute | solution.py:329
  18.8 3.9 %collective-permute-start.2 = (bf16[2,64,2048]{2,1,0:T(8,128)(2,1)S(1)}, bf16[2,64,2048]{2,1,0:T(8,128)(2,1)S(1)}, u32[]{:S(2)}, u32[]{:S(2)}) collective-permute-start(bf16[2,64,2048]{2,1,0:T(8,128)(2,1)S(1)} %pad_maximum_fusion), channel_id=1, source_target_pairs={{0,4},{4,8},{8,12},{12,16},{16,20},{20,24},{24,28},{1,5},{5,9},{9,... | collective-permute-start | bytes 1572872 | tf_op jit(solution)/shard_map/ppermute | solution.py:315
  22.7 1.6 %collective-permute-start.8 = (bf16[4,128,128]{2,1,0:T(8,128)(2,1)S(1)}, bf16[4,128,128]{2,1,0:T(8,128)(2,1)S(1)}, u32[]{:S(2)}, u32[]{:S(2)}) collective-permute-start(bf16[4,128,128]{2,1,0:T(8,128)(2,1)S(1)} %get-tuple-element.73), channel_id=1, source_target_pairs={{0,8},{8,0},{4,12},{12,4},{16,24},{24,16},{20,28},{28,20},{1,9},{9... | collective-permute-start | bytes 393224 | tf_op jit(solution)/shard_map/ppermute | solution.py:329
  26.5 2.6 %collective-permute-done.8.refs_0_ = bf16[4,128,128]{2,1,0:T(8,128)(2,1)S(1)} collective-permute-done((bf16[4,128,128]{2,1,0:T(8,128)(2,1)S(1)}, bf16[4,128,128]{2,1,0:T(8,128)(2,1)S(1)}, u32[]{:S(2)}, u32[]{:S(2)}) %collective-permute-start.8) | collective-permute-done | bytes 131104 | tf_op jit(solution)/shard_map/ppermute | solution.py:329
  31.1 2.5 %collective-permute-done.4.refs_2_ = bf16[4,128,128]{2,1,0:T(8,128)(2,1)S(1)} collective-permute-done((bf16[4,128,128]{2,1,0:T(8,128)(2,1)S(1)}, bf16[4,128,128]{2,1,0:T(8,128)(2,1)S(1)}, u32[]{:S(2)}, u32[]{:S(2)}) %collective-permute-start.4) | collective-permute-done | bytes 131104 | tf_op jit(solution)/shard_map/ppermute | solution.py:329
  33.9 3.8 %collective-permute-start.5 = (bf16[2,4,128,128]{3,2,1,0:T(8,128)(2,1)S(1)}, bf16[2,4,128,128]{3,2,1,0:T(8,128)(2,1)S(1)}, u32[]{:S(2)}, u32[]{:S(2)}) collective-permute-start(bf16[2,4,128,128]{3,2,1,0:T(8,128)(2,1)S(1)} %get-tuple-element.62.rest_0_.rest_2_), channel_id=1, source_target_pairs={{0,4},{4,0},{8,12},{12,8},{16,20},{20,16},{24,28},{28,24},{1,5},{5... | collective-permute-start | bytes 786440 | tf_op jit(solution)/shard_map/ppermute | solution.py:299
  38.1 8.3 %collective-permute-start.11 = (bf16[2,4,128,128]{3,2,1,0:T(8,128)(2,1)S(1)}, bf16[2,4,128,128]{3,2,1,0:T(8,128)(2,1)S(1)}, u32[]{:S(2)}, u32[]{:S(2)}) collective-permute-start(bf16[2,4,128,128]{3,2,1,0:T(8,128)(2,1)S(1)} %get-tuple-element.80), channel_id=1, source_target_pairs={{0,4},{4,0},{8,12},{12,8},{16,20},{20,16},{24,28},{28,24},{1,5},{5... | collective-permute-start | bytes 786440 | tf_op jit(solution)/shard_map/ppermute | solution.py:299
  46.5 3.4 %window_part.1 = (f32[128,2048]{1,0:T(8,128)S(1)}, f32[128,2048]{1,0:T(8,128)S(1)}, bf16[128,2048]{1,0:T(8,128)(2,1)S(1)}, f32[128,2048]{1,0:T(8,128)S(1)}, bf16[2,64,2048]{2,1,0:T(8,128)(2,1)S(1)}) custom-call(bf16[128,2048]{1,0:T(8,128)(2,1)S(1)} %bitcast.37, bf16[128,2048]{1,0:T(8,128)(2,1)S(1)} %bitcast.36, bf16[128,2048]{1,0:T(8,128)(2,1)S(1)} %bitcast.14, ...), custom_call_target="tpu_custom_call" | custom-call | flops 3000 | bytes 1000 | tf_op jit(solution)/shard_map/window_part/pallas_call | solution.py:68
  51.2 1.4 %state_part.3 = (bf16[128,1024]{1,0:T(8,128)(2,1)S(1)}, bf16[128,1024]{1,0:T(8,128)(2,1)S(1)}, bf16[2,2,2,128,128]{4,3,2,1,0:T(8,128)(2,1)S(1)}, bf16[2,2,2,128,128]{4,3,2,1,0:T(8,128)(2,1)S(1)}) custom-call(bf16[128,2048]{1,0:T(8,128)(2,1)S(1)} %bitcast.28, bf16[128,2048]{1,0:T(8,128)(2,1)S(1)} %bitcast.33, bf16[128,2048]{1,0:T(8,128)(2,1)S(1)} %bitcast.15, ...), custom_call_target="tpu_custom_call" | custom-call | flops 3000 | bytes 1000 | tf_op jit(solution)/shard_map/state_part/pallas_call | solution.py:68
  55.3 1.5 %collective-permute-done.12.came = bf16[2,2,2,128,128]{4,3,2,1,0:T(8,128)(2,1)S(1)} collective-permute-done((bf16[2,2,2,128,128]{4,3,2,1,0:T(8,128)(2,1)S(1)}, bf16[2,2,2,128,128]{4,3,2,1,0:T(8,128)(2,1)S(1)}, u32[]{:S(2)}, u32[]{:S(2)}) %collective-permute-start.12) | collective-permute-done | bytes 262176 | tf_op jit(solution)/shard_map/ppermute | solution.py:309
  56.9 1.7 %collective-permute-start.13 = (bf16[2,128,128]{2,1,0:T(8,128)(2,1)S(1)}, bf16[2,128,128]{2,1,0:T(8,128)(2,1)S(1)}, u32[]{:S(2)}, u32[]{:S(2)}) collective-permute-start(bf16[2,128,128]{2,1,0:T(8,128)(2,1)S(1)} %get-tuple-element.99), channel_id=1, source_target_pairs={{0,4},{1,5},{2,6},{3,7},{4,0},{5,1},{6,2},{7,3},{8,12},{9,13},{10,... | collective-permute-start | bytes 196616 | tf_op jit(solution)/shard_map/ppermute | solution.py:309
  58.6 1.5 %collective-permute-start.14 = (bf16[2,128,128]{2,1,0:T(8,128)(2,1)S(1)}, bf16[2,128,128]{2,1,0:T(8,128)(2,1)S(1)}, u32[]{:S(2)}, u32[]{:S(2)}) collective-permute-start(bf16[2,128,128]{2,1,0:T(8,128)(2,1)S(1)} %get-tuple-element.100), channel_id=1, source_target_pairs={{0,2},{1,3},{2,0},{3,1},{4,6},{5,7},{6,4},{7,5},{8,10},{9,11},{10,... | collective-permute-start | bytes 196616 | tf_op jit(solution)/shard_map/ppermute | solution.py:309
  60.4 4.9 %collective-permute-done.13.refs_1_ = bf16[2,128,128]{2,1,0:T(8,128)(2,1)S(1)} collective-permute-done((bf16[2,128,128]{2,1,0:T(8,128)(2,1)S(1)}, bf16[2,128,128]{2,1,0:T(8,128)(2,1)S(1)}, u32[]{:S(2)}, u32[]{:S(2)}) %collective-permute-start.13) | collective-permute-done | bytes 65568 | tf_op jit(solution)/shard_map/ppermute | solution.py:309
  65.3 1.3 %collective-permute-done.15.refs_3_ = bf16[2,128,128]{2,1,0:T(8,128)(2,1)S(1)} collective-permute-done((bf16[2,128,128]{2,1,0:T(8,128)(2,1)S(1)}, bf16[2,128,128]{2,1,0:T(8,128)(2,1)S(1)}, u32[]{:S(2)}, u32[]{:S(2)}) %collective-permute-start.15) | collective-permute-done | bytes 65568 | tf_op jit(solution)/shard_map/ppermute | solution.py:309
  66.7 8.6 %collective-permute-start.18 = (bf16[2,128,128]{2,1,0:T(8,128)(2,1)S(1)}, bf16[2,128,128]{2,1,0:T(8,128)(2,1)S(1)}, u32[]{:S(2)}, u32[]{:S(2)}) collective-permute-start(bf16[2,128,128]{2,1,0:T(8,128)(2,1)S(1)} %total.2.refs_0_), channel_id=1, source_target_pairs={{0,24},{1,25},{2,26},{3,27},{4,28},{5,29},{6,30},{7,31},{8,16},{9,... | collective-permute-start | bytes 196616 | tf_op jit(solution)/shard_map/ppermute | solution.py:309
  75.9 3.5 %output_part.1 = (bf16[128,2048]{1,0:T(8,128)(2,1)}, bf16[128,2048]{1,0:T(8,128)(2,1)}, bf16[128,2048]{1,0:T(8,128)(2,1)}, bf16[128,2048]{1,0:T(8,128)(2,1)}, bf...) custom-call(bf16[128,2048]{1,0:T(8,128)(2,1)S(1)} %bitcast.18, ...), custom_call_target="tpu_custom_call" | custom-call | flops 3000 | bytes 1000 | tf_op jit(solution)/shard_map/output_part/pallas_call | solution.py:68
  79.4 1.3 %collective-permute-done.17.refs_2_ = bf16[2,128,128]{2,1,0:T(8,128)(2,1)S(1)} collective-permute-done((bf16[2,128,128]{2,1,0:T(8,128)(2,1)S(1)}, bf16[2,128,128]{2,1,0:T(8,128)(2,1)S(1)}, u32[]{:S(2)}, u32[]{:S(2)}) %collective-permute-start.17) | collective-permute-done | bytes 65568 | tf_op jit(solution)/shard_map/ppermute | solution.py:309
  80.8 2.0 %collective-permute-start.23 = (bf16[2,128,128]{2,1,0:T(8,128)(2,1)S(1)}, bf16[2,128,128]{2,1,0:T(8,128)(2,1)S(1)}, u32[]{:S(2)}, u32[]{:S(2)}) collective-permute-start(bf16[2,128,128]{2,1,0:T(8,128)(2,1)S(1)} %total.3.refs_0_), channel_id=1, source_target_pairs={{0,6},{1,7},{2,4},{3,5},{4,2},{5,3},{6,0},{7,1},{8,14},{9,15},{10,... | collective-permute-start | bytes 196616 | tf_op jit(solution)/shard_map/ppermute | solution.py:309
  84.4 1.7 %collective-permute-done.23.refs_5_ = bf16[2,128,128]{2,1,0:T(8,128)(2,1)S(1)} collective-permute-done((bf16[2,128,128]{2,1,0:T(8,128)(2,1)S(1)}, bf16[2,128,128]{2,1,0:T(8,128)(2,1)S(1)}, u32[]{:S(2)}, u32[]{:S(2)}) %collective-permute-start.23) | collective-permute-done | bytes 65568 | tf_op jit(solution)/shard_map/ppermute | solution.py:309
  (63 shorter events, 15.4 us)
Async XLA Ops:
  3.4 10.1 %collective-permute-start = (bf16[2,4,128,128]{3,2,1,0:T(8,128)(2,1)S(1)}, bf16[2,4,128,128]{3,2,1,0:T(8,128)(2,1)S(1)}, u32[]{:S(2)}, u32[]{:S(2)}) collective-permute-start(bf16[2,4,128,128]{3,2,1,0:T(8,128)(2,1)S(1)} %get-tuple-element.57), channel_id=1, source_target_pairs={{0,4},{4,0},{8,12},{12,8},{16,20},{20,16},{24,28},{28,24},{1,5},{5... | collective-permute-start | bytes 786440 | tf_op jit(solution)/shard_map/ppermute | solution.py:299
  6.4 16.2 %collective-permute-start.7 = (bf16[2,4,128,128]{3,2,1,0:T(8,128)(2,1)S(1)}, bf16[2,4,128,128]{3,2,1,0:T(8,128)(2,1)S(1)}, u32[]{:S(2)}, u32[]{:S(2)}) collective-permute-start(bf16[2,4,128,128]{3,2,1,0:T(8,128)(2,1)S(1)} %get-tuple-element.72), channel_id=1, source_target_pairs={{0,4},{4,0},{8,12},{12,8},{16,20},{20,16},{24,28},{28,24},{1,5},{5... | collective-permute-start | bytes 786440 | tf_op jit(solution)/shard_map/ppermute | solution.py:299
  13.6 5.2 %collective-permute-start.1 = (bf16[4,128,128]{2,1,0:T(8,128)(2,1)S(1)}, bf16[4,128,128]{2,1,0:T(8,128)(2,1)S(1)}, u32[]{:S(2)}, u32[]{:S(2)}) collective-permute-start(bf16[4,128,128]{2,1,0:T(8,128)(2,1)S(1)} %get-tuple-element.58), channel_id=1, source_target_pairs={{0,8},{8,0},{4,12},{12,4},{16,24},{24,16},{20,28},{28,20},{1,9},{9... | collective-permute-start | bytes 393224 | tf_op jit(solution)/shard_map/ppermute | solution.py:329
  18.8 27.7 %collective-permute-start.2 = (bf16[2,64,2048]{2,1,0:T(8,128)(2,1)S(1)}, bf16[2,64,2048]{2,1,0:T(8,128)(2,1)S(1)}, u32[]{:S(2)}, u32[]{:S(2)}) collective-permute-start(bf16[2,64,2048]{2,1,0:T(8,128)(2,1)S(1)} %pad_maximum_fusion), channel_id=1, source_target_pairs={{0,4},{4,8},{8,12},{12,16},{16,20},{20,24},{24,28},{1,5},{5,9},{9,... | collective-permute-start | bytes 1572872 | tf_op jit(solution)/shard_map/ppermute | solution.py:315
  22.7 6.3 %collective-permute-start.8 = (bf16[4,128,128]{2,1,0:T(8,128)(2,1)S(1)}, bf16[4,128,128]{2,1,0:T(8,128)(2,1)S(1)}, u32[]{:S(2)}, u32[]{:S(2)}) collective-permute-start(bf16[4,128,128]{2,1,0:T(8,128)(2,1)S(1)} %get-tuple-element.73), channel_id=1, source_target_pairs={{0,8},{8,0},{4,12},{12,4},{16,24},{24,16},{20,28},{28,20},{1,9},{9... | collective-permute-start | bytes 393224 | tf_op jit(solution)/shard_map/ppermute | solution.py:329
  24.5 9.2 %collective-permute-start.4 = (bf16[4,128,128]{2,1,0:T(8,128)(2,1)S(1)}, bf16[4,128,128]{2,1,0:T(8,128)(2,1)S(1)}, u32[]{:S(2)}, u32[]{:S(2)}) collective-permute-start(bf16[4,128,128]{2,1,0:T(8,128)(2,1)S(1)} %level_sum.2), channel_id=1, source_target_pairs={{8,24},{16,0},{12,28},{20,4},{9,25},{17,1},{13,29},{21,5},{10,26},... | collective-permute-start | bytes 393224 | tf_op jit(solution)/shard_map/ppermute | solution.py:329
  25.8 7.9 %collective-permute-start.3 = (bf16[4,128,128]{2,1,0:T(8,128)(2,1)S(1)}, bf16[4,128,128]{2,1,0:T(8,128)(2,1)S(1)}, u32[]{:S(2)}, u32[]{:S(2)}) collective-permute-start(bf16[4,128,128]{2,1,0:T(8,128)(2,1)S(1)} %level_sum.2), channel_id=1, source_target_pairs={{8,16},{16,8},{12,20},{20,12},{9,17},{17,9},{13,21},{21,13},{10,18... | collective-permute-start | bytes 393224 | tf_op jit(solution)/shard_map/ppermute | solution.py:329
  29.2 8.7 %collective-permute-start.10 = (bf16[4,128,128]{2,1,0:T(8,128)(2,1)S(1)}, bf16[4,128,128]{2,1,0:T(8,128)(2,1)S(1)}, u32[]{:S(2)}, u32[]{:S(2)}) collective-permute-start(bf16[4,128,128]{2,1,0:T(8,128)(2,1)S(1)} %level_sum.3), channel_id=1, source_target_pairs={{8,24},{16,0},{12,28},{20,4},{9,25},{17,1},{13,29},{21,5},{10,26},... | collective-permute-start | bytes 393224 | tf_op jit(solution)/shard_map/ppermute | solution.py:329
  30.5 7.4 %collective-permute-start.9 = (bf16[4,128,128]{2,1,0:T(8,128)(2,1)S(1)}, bf16[4,128,128]{2,1,0:T(8,128)(2,1)S(1)}, u32[]{:S(2)}, u32[]{:S(2)}) collective-permute-start(bf16[4,128,128]{2,1,0:T(8,128)(2,1)S(1)} %level_sum.3), channel_id=1, source_target_pairs={{8,16},{16,8},{12,20},{20,12},{9,17},{17,9},{13,21},{21,13},{10,18... | collective-permute-start | bytes 393224 | tf_op jit(solution)/shard_map/ppermute | solution.py:329
  33.9 16.0 %collective-permute-start.5 = (bf16[2,4,128,128]{3,2,1,0:T(8,128)(2,1)S(1)}, bf16[2,4,128,128]{3,2,1,0:T(8,128)(2,1)S(1)}, u32[]{:S(2)}, u32[]{:S(2)}) collective-permute-start(bf16[2,4,128,128]{3,2,1,0:T(8,128)(2,1)S(1)} %get-tuple-element.62.rest_0_.rest_2_), channel_id=1, source_target_pairs={{0,4},{4,0},{8,12},{12,8},{16,20},{20,16},{24,28},{28,24},{1,5},{5... | collective-permute-start | bytes 786440 | tf_op jit(solution)/shard_map/ppermute | solution.py:299
  38.1 15.5 %collective-permute-start.11 = (bf16[2,4,128,128]{3,2,1,0:T(8,128)(2,1)S(1)}, bf16[2,4,128,128]{3,2,1,0:T(8,128)(2,1)S(1)}, u32[]{:S(2)}, u32[]{:S(2)}) collective-permute-start(bf16[2,4,128,128]{3,2,1,0:T(8,128)(2,1)S(1)} %get-tuple-element.80), channel_id=1, source_target_pairs={{0,4},{4,0},{8,12},{12,8},{16,20},{20,16},{24,28},{28,24},{1,5},{5... | collective-permute-start | bytes 786440 | tf_op jit(solution)/shard_map/ppermute | solution.py:299
  49.9 26.0 %collective-permute-start.6 = (bf16[2,64,2048]{2,1,0:T(8,128)(2,1)S(1)}, bf16[2,64,2048]{2,1,0:T(8,128)(2,1)S(1)}, u32[]{:S(2)}, u32[]{:S(2)}) collective-permute-start(bf16[2,64,2048]{2,1,0:T(8,128)(2,1)S(1)} %get-tuple-element.68), channel_id=1, source_target_pairs={{4,0},{8,4},{12,8},{16,12},{20,16},{24,20},{28,24},{5,1},{9,5},{13... | collective-permute-start | bytes 1572872 | tf_op jit(solution)/shard_map/ppermute | solution.py:315
  55.2 1.6 %collective-permute-start.12 = (bf16[2,2,2,128,128]{4,3,2,1,0:T(8,128)(2,1)S(1)}, bf16[2,2,2,128,128]{4,3,2,1,0:T(8,128)(2,1)S(1)}, u32[]{:S(2)}, u32[]{:S(2)}) collective-permute-start(bf16[2,2,2,128,128]{4,3,2,1,0:T(8,128)(2,1)S(1)} %get-tuple-element.97), channel_id=1, source_target_pairs={{0,1},{1,0},{2,3},{3,2},{4,5},{5,4},{6,7},{7,6},{8,9},{9,8},{10,11... | collective-permute-start | bytes 786440 | tf_op jit(solution)/shard_map/ppermute | solution.py:309
  56.9 8.4 %collective-permute-start.13 = (bf16[2,128,128]{2,1,0:T(8,128)(2,1)S(1)}, bf16[2,128,128]{2,1,0:T(8,128)(2,1)S(1)}, u32[]{:S(2)}, u32[]{:S(2)}) collective-permute-start(bf16[2,128,128]{2,1,0:T(8,128)(2,1)S(1)} %get-tuple-element.99), channel_id=1, source_target_pairs={{0,4},{1,5},{2,6},{3,7},{4,0},{5,1},{6,2},{7,3},{8,12},{9,13},{10,... | collective-permute-start | bytes 196616 | tf_op jit(solution)/shard_map/ppermute | solution.py:309
  58.6 6.7 %collective-permute-start.14 = (bf16[2,128,128]{2,1,0:T(8,128)(2,1)S(1)}, bf16[2,128,128]{2,1,0:T(8,128)(2,1)S(1)}, u32[]{:S(2)}, u32[]{:S(2)}) collective-permute-start(bf16[2,128,128]{2,1,0:T(8,128)(2,1)S(1)} %get-tuple-element.100), channel_id=1, source_target_pairs={{0,2},{1,3},{2,0},{3,1},{4,6},{5,7},{6,4},{7,5},{8,10},{9,11},{10,... | collective-permute-start | bytes 196616 | tf_op jit(solution)/shard_map/ppermute | solution.py:309
  60.1 6.6 %collective-permute-start.15 = (bf16[2,128,128]{2,1,0:T(8,128)(2,1)S(1)}, bf16[2,128,128]{2,1,0:T(8,128)(2,1)S(1)}, u32[]{:S(2)}, u32[]{:S(2)}) collective-permute-start(bf16[2,128,128]{2,1,0:T(8,128)(2,1)S(1)} %get-tuple-element.101), channel_id=1, source_target_pairs={{0,6},{1,7},{2,4},{3,5},{4,2},{5,3},{6,0},{7,1},{8,14},{9,15},{10,... | collective-permute-start | bytes 196616 | tf_op jit(solution)/shard_map/ppermute | solution.py:309
  66.7 12.8 %collective-permute-start.18 = (bf16[2,128,128]{2,1,0:T(8,128)(2,1)S(1)}, bf16[2,128,128]{2,1,0:T(8,128)(2,1)S(1)}, u32[]{:S(2)}, u32[]{:S(2)}) collective-permute-start(bf16[2,128,128]{2,1,0:T(8,128)(2,1)S(1)} %total.2.refs_0_), channel_id=1, source_target_pairs={{0,24},{1,25},{2,26},{3,27},{4,28},{5,29},{6,30},{7,31},{8,16},{9,... | collective-permute-start | bytes 196616 | tf_op jit(solution)/shard_map/ppermute | solution.py:309
  75.3 5.5 %collective-permute-start.17 = (bf16[2,128,128]{2,1,0:T(8,128)(2,1)S(1)}, bf16[2,128,128]{2,1,0:T(8,128)(2,1)S(1)}, u32[]{:S(2)}, u32[]{:S(2)}) collective-permute-start(bf16[2,128,128]{2,1,0:T(8,128)(2,1)S(1)} %total.2.refs_0_), channel_id=1, source_target_pairs={{0,16},{1,17},{2,18},{3,19},{4,20},{5,21},{6,22},{7,23},{8,24},{9,... | collective-permute-start | bytes 196616 | tf_op jit(solution)/shard_map/ppermute | solution.py:309
  75.4 5.3 %collective-permute-start.16 = (bf16[2,128,128]{2,1,0:T(8,128)(2,1)S(1)}, bf16[2,128,128]{2,1,0:T(8,128)(2,1)S(1)}, u32[]{:S(2)}, u32[]{:S(2)}) collective-permute-start(bf16[2,128,128]{2,1,0:T(8,128)(2,1)S(1)} %total.2.refs_0_), channel_id=1, source_target_pairs={{0,8},{1,9},{2,10},{3,11},{4,12},{5,13},{6,14},{7,15},{8,0},{9,1},... | collective-permute-start | bytes 196616 | tf_op jit(solution)/shard_map/ppermute | solution.py:309
  80.8 5.2 %collective-permute-start.23 = (bf16[2,128,128]{2,1,0:T(8,128)(2,1)S(1)}, bf16[2,128,128]{2,1,0:T(8,128)(2,1)S(1)}, u32[]{:S(2)}, u32[]{:S(2)}) collective-permute-start(bf16[2,128,128]{2,1,0:T(8,128)(2,1)S(1)} %total.3.refs_0_), channel_id=1, source_target_pairs={{0,6},{1,7},{2,4},{3,5},{4,2},{5,3},{6,0},{7,1},{8,14},{9,15},{10,... | collective-permute-start | bytes 196616 | tf_op jit(solution)/shard_map/ppermute | solution.py:309
  82.8 4.3 %collective-permute-start.22 = (bf16[2,128,128]{2,1,0:T(8,128)(2,1)S(1)}, bf16[2,128,128]{2,1,0:T(8,128)(2,1)S(1)}, u32[]{:S(2)}, u32[]{:S(2)}) collective-permute-start(bf16[2,128,128]{2,1,0:T(8,128)(2,1)S(1)} %total.3.refs_0_), channel_id=1, source_target_pairs={{0,4},{1,5},{2,6},{3,7},{4,0},{5,1},{6,2},{7,3},{8,12},{9,13},{10,... | collective-permute-start | bytes 196616 | tf_op jit(solution)/shard_map/ppermute | solution.py:309
  83.1 4.3 %collective-permute-start.19 = (bf16[2,128,128]{2,1,0:T(8,128)(2,1)S(1)}, bf16[2,128,128]{2,1,0:T(8,128)(2,1)S(1)}, u32[]{:S(2)}, u32[]{:S(2)}) collective-permute-start(bf16[2,128,128]{2,1,0:T(8,128)(2,1)S(1)} %total.3.refs_0_), channel_id=1, source_target_pairs={{0,2},{1,3},{2,0},{3,1},{4,6},{5,7},{6,4},{7,5},{8,10},{9,11},{10,... | collective-permute-start | bytes 196616 | tf_op jit(solution)/shard_map/ppermute | solution.py:309
  84.4 3.3 %collective-permute-start.20 = (bf16[2,128,128]{2,1,0:T(8,128)(2,1)S(1)}, bf16[2,128,128]{2,1,0:T(8,128)(2,1)S(1)}, u32[]{:S(2)}, u32[]{:S(2)}) collective-permute-start(bf16[2,128,128]{2,1,0:T(8,128)(2,1)S(1)} %total.3.refs_0_), channel_id=1, source_target_pairs={{0,1},{1,0},{2,3},{3,2},{4,5},{5,4},{6,7},{7,6},{8,9},{9,8},{10,11... | collective-permute-start | bytes 196616 | tf_op jit(solution)/shard_map/ppermute | solution.py:309
  86.0 1.6 %collective-permute-start.25 = (bf16[2,128,128]{2,1,0:T(8,128)(2,1)S(1)}, bf16[2,128,128]{2,1,0:T(8,128)(2,1)S(1)}, u32[]{:S(2)}, u32[]{:S(2)}) collective-permute-start(bf16[2,128,128]{2,1,0:T(8,128)(2,1)S(1)} %collective-permute-done.23.refs_5_), channel_id=1, source_target_pairs={{0,1},{1,0},{2,3},{3,2},{4,5},{5,4},{6,7},{7,6},{8,9},{9,8},{10,11... | collective-permute-start | bytes 196616 | tf_op jit(solution)/shard_map/ppermute | solution.py:309
  (10 other events, 76.0 us)

commit v4 on v3

--- a/solution.py
+++ b/solution.py
@@ -79,12 +79,15 @@
     )(*operands)
 
 
-def feature_kernel(first, lq, lk, v, g, fm, *rest):
-    fq_out, fk_out, *t_out, rows, maps, arrived = rest[-5 - CHUNKS :]
-    half = 1 - own_half() if first else own_half()
+def feature_kernel(first, count, ends_too, lq, lk, v, g, fm, wk, *rest):
+    fq_out, fk_out, *t_out, rows, maps, arrived = rest
+    t_out = t_out[-count - ends_too :]
+    ends = t_out.pop() if ends_too else None
+    half = own_half() if count == CHUNKS else 1 - own_half()
+    steps = count * CHUNK // GROUP
 
     def copies(step):
-        head = half * HALF + step * GROUP
+        head = half * HALF + first * CHUNK + step * GROUP
         wide = pl.ds(pl.multiple_of(head * HD, GROUP * HD), GROUP * HD)
         here = slice(step * GROUP * HD, (step + 1) * GROUP * HD)
         pairs = [(ref.at[:, wide], rows.at[n, :, here]) for n, ref in enumerate((lq, lk, v, g))]
@@ -94,10 +97,15 @@
             for n, (source, target) in enumerate(pairs)
         ]
 
-    started = [copies(step) for step in range(HALF // GROUP)]
-    for step in started:
-        for copy in step:
-            copy.start()
+    started = [copies(step) for step in range(steps)]
+    tails = [
+        pltpu.make_async_copy(
+            ref.at[pl.ds(ref.shape[0] - WINDOW, WINDOW)], ends.at[n], arrived.at[n, 5]
+        )
+        for n, ref in enumerate((wk, v) if ends_too else ())
+    ]
+    for copy in [copy for step in started for copy in step] + tails:
+        copy.start()
     for step, arriving in enumerate(started):
         for copy in arriving:
             copy.wait()
@@ -113,23 +121,34 @@
         for h, (forward, backward) in zip(heads, sums):
             t_out[h // CHUNK][0, h % CHUNK] = forward.astype(BF)
             t_out[h // CHUNK][1, h % CHUNK] = backward.astype(BF)
-
-
-def features(lq, lk, v, g, fm, follows):
+    for copy in tails:
+        copy.wait()
+
+
+def dropped(kernel, at, *refs):
+    kernel(*refs[:at], *refs[at + 1 :])
+
+
+def features(first, count, ends_too, lq, lk, v, g, fm, wk, follows):
     tokens = lq.shape[0]
-    row = array((tokens, HALF * HD), BF)
-    lq, lk, v, g, fm = (pltpu.with_memory_space_constraint(x, pltpu.HBM) for x in (lq, lk, v, g, fm))
-    return call(
-        functools.partial(feature_kernel, not follows),
+    row = array((tokens, count * CHUNK * HD), BF)
+    outs = [row, row] + [array((2, CHUNK, HD, HD), BF)] * count
+    operands = [pltpu.with_memory_space_constraint(x, pltpu.HBM) for x in (lq, lk, v, g, fm, wk)]
+    kernel = functools.partial(feature_kernel, first, count, ends_too)
+    if follows is not None:
+        kernel = functools.partial(dropped, kernel, len(operands))
+        operands.append(follows)
+    return call(
+        kernel,
         "features",
-        [row, row] + [array((2, CHUNK, HD, HD), BF)] * CHUNKS,
-        (lq, lk, v, g, fm, *follows),
-        in_hbm=5,
-        unread=len(follows),
+        outs + [array((2, WINDOW, WIDE), BF)] * ends_too,
+        operands,
+        in_hbm=6,
+        unread=len(operands) - 6,
         scratch_shapes=[
-            pltpu.VMEM((4, tokens, HALF * HD), BF),
-            pltpu.VMEM((HALF, HD, HD), BF),
-            pltpu.SemaphoreType.DMA((HALF // GROUP, 5)),
+            pltpu.VMEM((4, tokens, count * CHUNK * HD), BF),
+            pltpu.VMEM((count * CHUNK, HD, HD), BF),
+            pltpu.SemaphoreType.DMA((count * CHUNK // GROUP, 6)),
         ],
     )
 
@@ -219,7 +238,8 @@
     for n in range(count):
         heads = [(first + n) * CHUNK + h for h in range(CHUNK)]
         at = [col_of(half, head) for head in heads]
-        q_feat, k_feat = [fq[:, col(x)] for x in heads], [fk[:, col(x)] for x in heads]
+        local = [col(n * CHUNK + h) for h in range(CHUNK)]
+        q_feat, k_feat = [fq[:, x] for x in local], [fk[:, x] for x in local]
         val, grad = [v[:, x] for x in at], [g[:, x] for x in at]
         mixed = [jnp.where(causal, dot_nt(a, b), 0.0).astype(BF) for a, b in zip(grad, val)]
         dfq = [dot_nt(a, states[n][0, h]) for h, a in enumerate(grad)]
@@ -263,20 +283,20 @@
     dwk[tail:] = (dk[tail:] + edge[0].astype(F32)).astype(BF)
     for side in range(2):
         half = own_half() ^ side
-        refs = rest[: 2 + CHUNKS + 2] if side == 0 else rest[2 + CHUNKS + 2 : -7]
-        fq, fk = refs[:2]
-        states, pairs = refs[2 : 2 + CHUNKS], refs[2 + CHUNKS :]
-        each = 2 * HALF // len(pairs)
+        refs = rest[: 4 + CHUNKS] if side == 0 else rest[4 + CHUNKS : -7]
+        states, pairs = refs[:CHUNKS], refs[CHUNKS:]
+        each = 4 * HALF // len(pairs)
         for n in range(CHUNKS):
             heads = [n * CHUNK + k for k in range(CHUNK)]
-            cols = [(col(h), col_of(half, h)) for h in heads]
+            cols = [(col(h % each), col_of(half, h)) for h in heads]
+            fq, fk, dpq, dpk = pairs[4 * (n * CHUNK // each) :][:4]
             scores = [
                 jnp.where(causal, dot_nt(fq[:, c], fk[:, c]), 0.0).astype(BF) for c, _ in cols
             ]
             for h, (_, at) in zip(heads, cols):
-                m, here, w = 2 * (h // each), col(h % each), fm[half * HALF + h]
-                dlq[:, at] = dot_nt(pairs[m][:, here], w).astype(BF)
-                dlk[:, at] = dot_nt(pairs[m + 1][:, here], w).astype(BF)
+                here, w = col(h % each), fm[half * HALF + h]
+                dlq[:, at] = dot_nt(dpq[:, here], w).astype(BF)
+                dlk[:, at] = dot_nt(dpk[:, here], w).astype(BF)
             lin = [dot(fq[:, c], states[n][0, k]) for k, (c, _) in enumerate(cols)]
             grad_v = [dot(fk[:, c], states[n][1, k]) for k, (c, _) in enumerate(cols)]
             for k, (_, at) in enumerate(cols):
@@ -307,6 +327,19 @@
         for d in range(width)
     ]
     return lax.ppermute(block, ("seq", "dp"), route)
+
+
+def relayed(block):
+    devices = range(1, lax.axis_size("seq") - 2, 2)
+    return lax.ppermute(block, "seq", [(i, i + 2) for i in devices])
+
+
+def relay_kernel(own, came, out):
+    out[...] = jnp.where(own_half() == 1, came[...], own[...])
+
+
+def relay(own, came):
+    return call(relay_kernel, "relay", [array(own.shape, own.dtype)], (own, came))[0]
 
 
 def passed_along(block, distance):
@@ -457,10 +490,18 @@
         x[0]
         for x in (linear_queries, linear_keys, window_queries, window_keys, values, cotangent)
     )
-    fq_o, fk_o, *given = features(lq, lk, v, g, feature_map, ())
-    came = [flipped(x, 1) for x in given]
-    ends = jnp.stack([wk[tokens - WINDOW :], v[tokens - WINDOW :]])
-    fq, fk, *kept = features(lq, lk, v, g, feature_map, (fq_o,))
+    rows = (lq, lk, v, g)
+    inputs = (*rows, feature_map, wk)
+    feats, came, last = [], [], None
+    for n in range(CHUNKS):
+        fq, fk, sums, *ends = features(n, 1, n == CHUNKS - 1, *inputs, last)
+        last = fq
+        feats.append((fq, fk))
+        came.append(flipped(sums, 1))
+    far_ends = relayed(ends[0])
+    fq, fk, *kept = features(0, CHUNKS, False, *inputs, last)
+    came[-1], far_ends = lax.optimization_barrier((came[-1], far_ends))
+    rims = flipped(relay(ends[0], far_ends), 1)
     pair, sent = zip(*(pair_sum(a, b) for a, b in zip(kept, came)))
     pair, sent = list(pair), list(sent)
     gots = [[] for _ in range(CHUNKS)]
@@ -469,22 +510,18 @@
             sent = [level_sum(pair[n], gots[n]) for n in range(CHUNKS)]
         for n in range(CHUNKS):
             gots[n] += spread(sent[n], level)
-            if level == 0 and n == CHUNKS - 1:
-                gots[n], ends = lax.optimization_barrier((gots[n], ends))
-                rims = passed_along(ends, 1)
     mine, others = zip(*(entering(kept[n], came[n], gots[n]) for n in range(CHUNKS)))
     back = [flipped(x, 1) for x in others]
     *windows, edge = window_part(wq, wk, v, g, rims, others[-1])
-    back[-1], edge = lax.optimization_barrier((back[-1], edge))
+    back, edge = lax.optimization_barrier((back, edge))
     edge = passed_along(edge, -1)
-    rows = (lq, lk, v, g)
     dpq, dpk, *terms = state_part(0, CHUNKS, (*rows, fq, fk), mine, (), (others[-1],))
-    own = (fq, fk, *mine, dpq, dpk)
+    own = (*mine, fq, fk, dpq, dpk)
     pairs = []
     for n in range(CHUNKS):
-        dpq, dpk, *terms = state_part(n, 1, (*rows, fq_o, fk_o), (back[n],), terms)
-        pairs += [dpq, dpk]
-    other = (fq_o, fk_o, *back, *pairs)
+        dpq, dpk, *terms = state_part(n, 1, (*rows, *feats[n]), (back[n],), terms)
+        pairs += [*feats[n], dpq, dpk]
+    other = (*back, *pairs)
     keep, send = terms
     near, a, b, c = near_sum(keep, flat_flipped(send, 0, 1))
     a, b, c = flat_flipped(a, 1, 0), flat_flipped(b, 0, 2), flat_flipped(c, 1, 2)

time: 90 us -> 85.4 us (0.949)
  starting transfers between devices: 44.8 us -> 31.2 us
  waiting for transfers between devices: 26.6 us -> 34.5 us
  Pallas kernels: 17.4 us -> 18.4 us
    ppermute x4 -> x5, starting transfers between devices: 15.2 us -> 9.46 us  [flipped(): return lax.ppermute(block, 'seq', [(i, i ^ bit) for i in range(count)])]
    ppermute x4 -> x5, waiting for transfers between devices: 5.23 us -> 9.89 us  [flipped(): return lax.ppermute(block, 'seq', [(i, i ^ bit) for i in range(count)])]
    ppermute x14, starting transfers between devices: 16.7 us -> 12.5 us  [flat_flipped(): return lax.ppermute(block, ('seq', 'dp'), route)]
    ppermute x2 -> x1, starting transfers between devices: 5.15 us -> 1.28 us  [passed_along(): return lax.ppermute(block, 'seq', route)]
    ppermute x14, waiting for transfers between devices: 13.1 us -> 15.4 us  [flat_flipped(): return lax.ppermute(block, ('seq', 'dp'), route)]
    ppermute x6, waiting for transfers between devices: 8.19 us -> 9.18 us  [spread(): arrived.append(lax.ppermute(block, 'seq', route))]
    pallas_call x17 -> x19, Pallas kernels: 17.4 us -> 18.4 us  [call(): pl.pallas_call(kernel, in_specs=[pl.BlockSpec(memory_space=pltpu.HBM)] *...]
  transfers between devices with their start and end apart: 26 -> 27, of which waited for: 15 -> 13; matrix products, arithmetic and copies ran while one was open for 0% -> 0% of each run, Pallas kernels for 15% -> 16%
where the time goes in v4:
time: 85.4 us; the launch traced here: 85 us
  waiting for transfers between devices  34.5 us (40%)
  starting transfers between devices  31.2 us (37%)
  Pallas kernels  18.4 us (22%)
  between operations  0.92 us (1%)
    pallas_call x19, Pallas kernels, call(): pl.pallas_call(kernel, in_specs=[pl.BlockSpec(memory_space=pltpu.HBM)] *...  18.4 us
    ppermute x14, waiting for transfers between devices, flat_flipped(): return lax.ppermute(block, ('seq', 'dp'), route)  15.4 us
    ppermute x14, starting transfers between devices, flat_flipped(): return lax.ppermute(block, ('seq', 'dp'), route)  12.5 us
    ppermute x5, waiting for transfers between devices, flipped(): return lax.ppermute(block, 'seq', [(i, i ^ bit) for i in range(count)])  9.89 us
    ppermute x5, starting transfers between devices, flipped(): return lax.ppermute(block, 'seq', [(i, i ^ bit) for i in range(count)])  9.46 us
    ppermute x6, waiting for transfers between devices, spread(): arrived.append(lax.ppermute(block, 'seq', route))  9.18 us
    ppermute x6, starting transfers between devices, spread(): arrived.append(lax.ppermute(block, 'seq', route))  7.28 us
  transfers between devices with their start and end apart: 27, of which 13 were waited for; matrix products, arithmetic and copies ran while one was open for 0% of the time, Pallas kernels for 16%

profile of v4, /device:TPU:0, one launch (start us, length us, event | category | flops | bytes accessed | tf_op | source)
XLA Modules:
  0.0 85.0 jit_solution(15156705931542039818)
XLA Ops:
  0.6 1.9 %features.3 = (bf16[128,512]{1,0:T(8,128)(2,1)S(1)}, bf16[128,512]{1,0:T(8,128)(2,1)S(1)}, bf16[2,4,128,128]{3,2,1,0:T(8,128)(2,1)S(1)}) custom-call(bf16[128,2048]{1,0:T(8,128)(2,1)} %bitcast.28, bf16[128,2048]{1,0:T(8,128)(2,1)} %bitcast.34, bf16[128,2048]{1,0:T(8,128)(2,1)} %bitcast.12, bf16[128,2048]{1,0:T(8,128)(2,1)} %bitcast.20, ...), custom_call_target="tpu_custom_call" | custom-call | flops 3000 | bytes 1000 | tf_op jit(solution)/shard_map/features/pallas_call | solution.py:68
  2.5 1.9 %features.4 = (bf16[128,512]{1,0:T(8,128)(2,1)S(1)}, bf16[128,512]{1,0:T(8,128)(2,1)S(1)}, bf16[2,4,128,128]{3,2,1,0:T(8,128)(2,1)S(1)}, bf16[2,64,2048]{2,1,0:T(8,128)(2,1)S(1)}) custom-call(bf16[128,2048]{1,0:T(8,128)(2,1)} %bitcast.29, bf16[128,2048]{1,0:T(8,128)(2,1)} %bitcast.35, bf16[128,2048]{1,0:T(8,128)(2,1)} %bitcast.13, ...), custom_call_target="tpu_custom_call" | custom-call | flops 3000 | bytes 1000 | tf_op jit(solution)/shard_map/features/pallas_call | solution.py:68
  5.1 5.8 %collective-permute-start.6 = (bf16[2,4,128,128]{3,2,1,0:T(8,128)(2,1)S(1)}, bf16[2,4,128,128]{3,2,1,0:T(8,128)(2,1)S(1)}, u32[]{:S(2)}, u32[]{:S(2)}) collective-permute-start(bf16[2,4,128,128]{3,2,1,0:T(8,128)(2,1)S(1)} %get-tuple-element.74), channel_id=1, source_target_pairs={{0,4},{4,0},{8,12},{12,8},{16,20},{20,16},{24,28},{28,24},{1,5},{5... | collective-permute-start | bytes 786440 | tf_op jit(solution)/shard_map/ppermute | solution.py:319
  11.0 2.8 %features.5 = (bf16[128,1024]{1,0:T(8,128)(2,1)S(1)}, bf16[128,1024]{1,0:T(8,128)(2,1)S(1)}, bf16[2,4,128,128]{3,2,1,0:T(8,128)(2,1)S(1)}, bf16[2,4,128,128]{3,2,1,0:T(8,128)(2,1)S(1)}) custom-call(bf16[128,2048]{1,0:T(8,128)(2,1)} %bitcast.30, bf16[128,2048]{1,0:T(8,128)(2,1)} %bitcast.36, bf16[128,2048]{1,0:T(8,128)(2,1)} %bitcast.14, ...), custom_call_target="tpu_custom_call" | custom-call | flops 3000 | bytes 1000 | tf_op jit(solution)/shard_map/features/pallas_call | solution.py:68
  13.8 4.3 %collective-permute-done.6.came = bf16[2,4,128,128]{3,2,1,0:T(8,128)(2,1)S(1)} collective-permute-done((bf16[2,4,128,128]{3,2,1,0:T(8,128)(2,1)S(1)}, bf16[2,4,128,128]{3,2,1,0:T(8,128)(2,1)S(1)}, u32[]{:S(2)}, u32[]{:S(2)}) %collective-permute-start.6) | collective-permute-done | bytes 262176 | tf_op jit(solution)/shard_map/ppermute | solution.py:319
  18.2 1.6 %collective-permute-start.7 = (bf16[4,128,128]{2,1,0:T(8,128)(2,1)S(1)}, bf16[4,128,128]{2,1,0:T(8,128)(2,1)S(1)}, u32[]{:S(2)}, u32[]{:S(2)}) collective-permute-start(bf16[4,128,128]{2,1,0:T(8,128)(2,1)S(1)} %get-tuple-element.75), channel_id=1, source_target_pairs={{0,8},{8,0},{4,12},{12,4},{16,24},{24,16},{20,28},{28,20},{1,9},{9... | collective-permute-start | bytes 393224 | tf_op jit(solution)/shard_map/ppermute | solution.py:362
  19.8 2.8 %collective-permute-done.came = bf16[2,4,128,128]{3,2,1,0:T(8,128)(2,1)S(1)} collective-permute-done((bf16[2,4,128,128]{3,2,1,0:T(8,128)(2,1)S(1)}, bf16[2,4,128,128]{3,2,1,0:T(8,128)(2,1)S(1)}, u32[]{:S(2)}, u32[]{:S(2)}) %collective-permute-start) | collective-permute-done | bytes 262176 | tf_op jit(solution)/shard_map/ppermute | solution.py:319
  22.7 1.6 %collective-permute-start.3 = (bf16[4,128,128]{2,1,0:T(8,128)(2,1)S(1)}, bf16[4,128,128]{2,1,0:T(8,128)(2,1)S(1)}, u32[]{:S(2)}, u32[]{:S(2)}) collective-permute-start(bf16[4,128,128]{2,1,0:T(8,128)(2,1)S(1)} %get-tuple-element.66), channel_id=1, source_target_pairs={{0,8},{8,0},{4,12},{12,4},{16,24},{24,16},{20,28},{28,20},{1,9},{9... | collective-permute-start | bytes 393224 | tf_op jit(solution)/shard_map/ppermute | solution.py:362
  24.3 1.8 %collective-permute-start.2 = (bf16[2,64,2048]{2,1,0:T(8,128)(2,1)S(1)}, bf16[2,64,2048]{2,1,0:T(8,128)(2,1)S(1)}, u32[]{:S(2)}, u32[]{:S(2)}) collective-permute-start(bf16[2,64,2048]{2,1,0:T(8,128)(2,1)S(1)} %relay.1), channel_id=1, source_target_pairs={{0,4},{4,0},{8,12},{12,8},{16,20},{20,16},{24,28},{28,24},{1,5},{5... | collective-permute-start | bytes 1572872 | tf_op jit(solution)/shard_map/ppermute | solution.py:319
  30.5 5.3 %collective-permute-done.9.refs_2_ = bf16[4,128,128]{2,1,0:T(8,128)(2,1)S(1)} collective-permute-done((bf16[4,128,128]{2,1,0:T(8,128)(2,1)S(1)}, bf16[4,128,128]{2,1,0:T(8,128)(2,1)S(1)}, u32[]{:S(2)}, u32[]{:S(2)}) %collective-permute-start.9) | collective-permute-done | bytes 131104 | tf_op jit(solution)/shard_map/ppermute | solution.py:362
  36.6 3.9 %collective-permute-done.5.refs_2_ = bf16[4,128,128]{2,1,0:T(8,128)(2,1)S(1)} collective-permute-done((bf16[4,128,128]{2,1,0:T(8,128)(2,1)S(1)}, bf16[4,128,128]{2,1,0:T(8,128)(2,1)S(1)}, u32[]{:S(2)}, u32[]{:S(2)}) %collective-permute-start.5) | collective-permute-done | bytes 131104 | tf_op jit(solution)/shard_map/ppermute | solution.py:362
  41.9 3.4 %window_part.1 = (f32[128,2048]{1,0:T(8,128)S(1)}, f32[128,2048]{1,0:T(8,128)S(1)}, bf16[128,2048]{1,0:T(8,128)(2,1)S(1)}, f32[128,2048]{1,0:T(8,128)S(1)}, bf16[2,64,2048]{2,1,0:T(8,128)(2,1)S(1)}) custom-call(bf16[128,2048]{1,0:T(8,128)(2,1)S(1)} %bitcast.44, bf16[128,2048]{1,0:T(8,128)(2,1)S(1)} %bitcast.43, bf16[128,2048]{1,0:T(8,128)(2,1)S(1)} %bitcast.15, ...), custom_call_target="tpu_custom_call" | custom-call | flops 3000 | bytes 1000 | tf_op jit(solution)/shard_map/window_part/pallas_call | solution.py:68
  45.4 2.8 %collective-permute-done.11.rest_0_.rest_7_ = bf16[2,4,128,128]{3,2,1,0:T(8,128)(2,1)S(1)} collective-permute-done((bf16[2,4,128,128]{3,2,1,0:T(8,128)(2,1)S(1)}, bf16[2,4,128,128]{3,2,1,0:T(8,128)(2,1)S(1)}, u32[]{:S(2)}, u32[]{:S(2)}) %collective-permute-start.11) | collective-permute-done | bytes 262176 | tf_op jit(solution)/shard_map/ppermute | solution.py:319
  52.5 1.5 %collective-permute-done.13.came = bf16[2,2,2,128,128]{4,3,2,1,0:T(8,128)(2,1)S(1)} collective-permute-done((bf16[2,2,2,128,128]{4,3,2,1,0:T(8,128)(2,1)S(1)}, bf16[2,2,2,128,128]{4,3,2,1,0:T(8,128)(2,1)S(1)}, u32[]{:S(2)}, u32[]{:S(2)}) %collective-permute-start.13) | collective-permute-done | bytes 262176 | tf_op jit(solution)/shard_map/ppermute | solution.py:329
  54.1 2.7 %collective-permute-start.14 = (bf16[2,128,128]{2,1,0:T(8,128)(2,1)S(1)}, bf16[2,128,128]{2,1,0:T(8,128)(2,1)S(1)}, u32[]{:S(2)}, u32[]{:S(2)}) collective-permute-start(bf16[2,128,128]{2,1,0:T(8,128)(2,1)S(1)} %get-tuple-element.107), channel_id=1, source_target_pairs={{0,4},{1,5},{2,6},{3,7},{4,0},{5,1},{6,2},{7,3},{8,12},{9,13},{10,... | collective-permute-start | bytes 196616 | tf_op jit(solution)/shard_map/ppermute | solution.py:329
  56.8 1.5 %collective-permute-start.15 = (bf16[2,128,128]{2,1,0:T(8,128)(2,1)S(1)}, bf16[2,128,128]{2,1,0:T(8,128)(2,1)S(1)}, u32[]{:S(2)}, u32[]{:S(2)}) collective-permute-start(bf16[2,128,128]{2,1,0:T(8,128)(2,1)S(1)} %get-tuple-element.108), channel_id=1, source_target_pairs={{0,2},{1,3},{2,0},{3,1},{4,6},{5,7},{6,4},{7,5},{8,10},{9,11},{10,... | collective-permute-start | bytes 196616 | tf_op jit(solution)/shard_map/ppermute | solution.py:329
  58.3 5.6 %collective-permute-done.14.refs_1_ = bf16[2,128,128]{2,1,0:T(8,128)(2,1)S(1)} collective-permute-done((bf16[2,128,128]{2,1,0:T(8,128)(2,1)S(1)}, bf16[2,128,128]{2,1,0:T(8,128)(2,1)S(1)}, u32[]{:S(2)}, u32[]{:S(2)}) %collective-permute-start.14) | collective-permute-done | bytes 65568 | tf_op jit(solution)/shard_map/ppermute | solution.py:329
  63.9 1.7 %collective-permute-done.16.refs_3_ = bf16[2,128,128]{2,1,0:T(8,128)(2,1)S(1)} collective-permute-done((bf16[2,128,128]{2,1,0:T(8,128)(2,1)S(1)}, bf16[2,128,128]{2,1,0:T(8,128)(2,1)S(1)}, u32[]{:S(2)}, u32[]{:S(2)}) %collective-permute-start.16) | collective-permute-done | bytes 65568 | tf_op jit(solution)/shard_map/ppermute | solution.py:329
  66.2 2.7 %collective-permute-start.18 = (bf16[2,128,128]{2,1,0:T(8,128)(2,1)S(1)}, bf16[2,128,128]{2,1,0:T(8,128)(2,1)S(1)}, u32[]{:S(2)}, u32[]{:S(2)}) collective-permute-start(bf16[2,128,128]{2,1,0:T(8,128)(2,1)S(1)} %total.2.refs_0_), channel_id=1, source_target_pairs={{0,16},{1,17},{2,18},{3,19},{4,20},{5,21},{6,22},{7,23},{8,24},{9,... | collective-permute-start | bytes 196616 | tf_op jit(solution)/shard_map/ppermute | solution.py:329
  70.1 3.4 %output_part.1 = (bf16[128,2048]{1,0:T(8,128)(2,1)}, bf16[128,2048]{1,0:T(8,128)(2,1)}, bf16[128,2048]{1,0:T(8,128)(2,1)}, bf16[128,2048]{1,0:T(8,128)(2,1)}, bf...) custom-call(bf16[128,2048]{1,0:T(8,128)(2,1)S(1)} %bitcast.19, ...), custom_call_target="tpu_custom_call" | custom-call | flops 3000 | bytes 1000 | tf_op jit(solution)/shard_map/output_part/pallas_call | solution.py:68
  73.5 1.4 %collective-permute-done.19.refs_3_ = bf16[2,128,128]{2,1,0:T(8,128)(2,1)S(1)} collective-permute-done((bf16[2,128,128]{2,1,0:T(8,128)(2,1)S(1)}, bf16[2,128,128]{2,1,0:T(8,128)(2,1)S(1)}, u32[]{:S(2)}, u32[]{:S(2)}) %collective-permute-start.19) | collective-permute-done | bytes 65568 | tf_op jit(solution)/shard_map/ppermute | solution.py:329
  75.6 1.9 %collective-permute-start.23 = (bf16[2,128,128]{2,1,0:T(8,128)(2,1)S(1)}, bf16[2,128,128]{2,1,0:T(8,128)(2,1)S(1)}, u32[]{:S(2)}, u32[]{:S(2)}) collective-permute-start(bf16[2,128,128]{2,1,0:T(8,128)(2,1)S(1)} %total.3.refs_0_), channel_id=1, source_target_pairs={{0,4},{1,5},{2,6},{3,7},{4,0},{5,1},{6,2},{7,3},{8,12},{9,13},{10,... | collective-permute-start | bytes 196616 | tf_op jit(solution)/shard_map/ppermute | solution.py:329
  78.5 1.5 %collective-permute-done.20.refs_1_ = bf16[2,128,128]{2,1,0:T(8,128)(2,1)S(1)} collective-permute-done((bf16[2,128,128]{2,1,0:T(8,128)(2,1)S(1)}, bf16[2,128,128]{2,1,0:T(8,128)(2,1)S(1)}, u32[]{:S(2)}, u32[]{:S(2)}) %collective-permute-start.20) | collective-permute-done | bytes 65568 | tf_op jit(solution)/shard_map/ppermute | solution.py:329
  80.5 2.2 %collective-permute-done.24.refs_5_ = bf16[2,128,128]{2,1,0:T(8,128)(2,1)S(1)} collective-permute-done((bf16[2,128,128]{2,1,0:T(8,128)(2,1)S(1)}, bf16[2,128,128]{2,1,0:T(8,128)(2,1)S(1)}, u32[]{:S(2)}, u32[]{:S(2)}) %collective-permute-start.24) | collective-permute-done | bytes 65568 | tf_op jit(solution)/shard_map/ppermute | solution.py:329
  (63 shorter events, 18.1 us)
Async XLA Ops:
  4.4 18.2 %collective-permute-start.1 = (bf16[2,64,2048]{2,1,0:T(8,128)(2,1)S(1)}, bf16[2,64,2048]{2,1,0:T(8,128)(2,1)S(1)}, u32[]{:S(2)}, u32[]{:S(2)}) collective-permute-start(bf16[2,64,2048]{2,1,0:T(8,128)(2,1)S(1)} %get-tuple-element.60.own), channel_id=1, source_target_pairs={{4,12},{12,20},{20,28},{5,13},{13,21},{21,29},{6,14},{14,22},{22,3... | collective-permute-start | bytes 1572872 | tf_op jit(solution)/shard_map/ppermute | solution.py:334
  5.1 13.0 %collective-permute-start.6 = (bf16[2,4,128,128]{3,2,1,0:T(8,128)(2,1)S(1)}, bf16[2,4,128,128]{3,2,1,0:T(8,128)(2,1)S(1)}, u32[]{:S(2)}, u32[]{:S(2)}) collective-permute-start(bf16[2,4,128,128]{3,2,1,0:T(8,128)(2,1)S(1)} %get-tuple-element.74), channel_id=1, source_target_pairs={{0,4},{4,0},{8,12},{12,8},{16,20},{20,16},{24,28},{28,24},{1,5},{5... | collective-permute-start | bytes 786440 | tf_op jit(solution)/shard_map/ppermute | solution.py:319
  10.9 11.6 %collective-permute-start = (bf16[2,4,128,128]{3,2,1,0:T(8,128)(2,1)S(1)}, bf16[2,4,128,128]{3,2,1,0:T(8,128)(2,1)S(1)}, u32[]{:S(2)}, u32[]{:S(2)}) collective-permute-start(bf16[2,4,128,128]{3,2,1,0:T(8,128)(2,1)S(1)} %get-tuple-element.61), channel_id=1, source_target_pairs={{0,4},{4,0},{8,12},{12,8},{16,20},{20,16},{24,28},{28,24},{1,5},{5... | collective-permute-start | bytes 786440 | tf_op jit(solution)/shard_map/ppermute | solution.py:319
  18.2 8.0 %collective-permute-start.7 = (bf16[4,128,128]{2,1,0:T(8,128)(2,1)S(1)}, bf16[4,128,128]{2,1,0:T(8,128)(2,1)S(1)}, u32[]{:S(2)}, u32[]{:S(2)}) collective-permute-start(bf16[4,128,128]{2,1,0:T(8,128)(2,1)S(1)} %get-tuple-element.75), channel_id=1, source_target_pairs={{0,8},{8,0},{4,12},{12,4},{16,24},{24,16},{20,28},{28,20},{1,9},{9... | collective-permute-start | bytes 393224 | tf_op jit(solution)/shard_map/ppermute | solution.py:362
  22.7 5.6 %collective-permute-start.3 = (bf16[4,128,128]{2,1,0:T(8,128)(2,1)S(1)}, bf16[4,128,128]{2,1,0:T(8,128)(2,1)S(1)}, u32[]{:S(2)}, u32[]{:S(2)}) collective-permute-start(bf16[4,128,128]{2,1,0:T(8,128)(2,1)S(1)} %get-tuple-element.66), channel_id=1, source_target_pairs={{0,8},{8,0},{4,12},{12,4},{16,24},{24,16},{20,28},{28,20},{1,9},{9... | collective-permute-start | bytes 393224 | tf_op jit(solution)/shard_map/ppermute | solution.py:362
  24.3 17.5 %collective-permute-start.2 = (bf16[2,64,2048]{2,1,0:T(8,128)(2,1)S(1)}, bf16[2,64,2048]{2,1,0:T(8,128)(2,1)S(1)}, u32[]{:S(2)}, u32[]{:S(2)}) collective-permute-start(bf16[2,64,2048]{2,1,0:T(8,128)(2,1)S(1)} %relay.1), channel_id=1, source_target_pairs={{0,4},{4,0},{8,12},{12,8},{16,20},{20,16},{24,28},{28,24},{1,5},{5... | collective-permute-start | bytes 1572872 | tf_op jit(solution)/shard_map/ppermute | solution.py:319
  26.3 4.2 %collective-permute-start.8 = (bf16[4,128,128]{2,1,0:T(8,128)(2,1)S(1)}, bf16[4,128,128]{2,1,0:T(8,128)(2,1)S(1)}, u32[]{:S(2)}, u32[]{:S(2)}) collective-permute-start(bf16[4,128,128]{2,1,0:T(8,128)(2,1)S(1)} %level_sum.3), channel_id=1, source_target_pairs={{8,16},{16,8},{12,20},{20,12},{9,17},{17,9},{13,21},{21,13},{10,18... | collective-permute-start | bytes 393224 | tf_op jit(solution)/shard_map/ppermute | solution.py:362
  26.9 8.8 %collective-permute-start.9 = (bf16[4,128,128]{2,1,0:T(8,128)(2,1)S(1)}, bf16[4,128,128]{2,1,0:T(8,128)(2,1)S(1)}, u32[]{:S(2)}, u32[]{:S(2)}) collective-permute-start(bf16[4,128,128]{2,1,0:T(8,128)(2,1)S(1)} %level_sum.3), channel_id=1, source_target_pairs={{8,24},{16,0},{12,28},{20,4},{9,25},{17,1},{13,29},{21,5},{10,26},... | collective-permute-start | bytes 393224 | tf_op jit(solution)/shard_map/ppermute | solution.py:362
  28.4 8.2 %collective-permute-start.4 = (bf16[4,128,128]{2,1,0:T(8,128)(2,1)S(1)}, bf16[4,128,128]{2,1,0:T(8,128)(2,1)S(1)}, u32[]{:S(2)}, u32[]{:S(2)}) collective-permute-start(bf16[4,128,128]{2,1,0:T(8,128)(2,1)S(1)} %level_sum.2), channel_id=1, source_target_pairs={{8,16},{16,8},{12,20},{20,12},{9,17},{17,9},{13,21},{21,13},{10,18... | collective-permute-start | bytes 393224 | tf_op jit(solution)/shard_map/ppermute | solution.py:362
  29.2 11.3 %collective-permute-start.5 = (bf16[4,128,128]{2,1,0:T(8,128)(2,1)S(1)}, bf16[4,128,128]{2,1,0:T(8,128)(2,1)S(1)}, u32[]{:S(2)}, u32[]{:S(2)}) collective-permute-start(bf16[4,128,128]{2,1,0:T(8,128)(2,1)S(1)} %level_sum.2), channel_id=1, source_target_pairs={{8,24},{16,0},{12,28},{20,4},{9,25},{17,1},{13,29},{21,5},{10,26},... | collective-permute-start | bytes 393224 | tf_op jit(solution)/shard_map/ppermute | solution.py:362
  36.0 9.3 %collective-permute-start.10 = (bf16[2,4,128,128]{3,2,1,0:T(8,128)(2,1)S(1)}, bf16[2,4,128,128]{3,2,1,0:T(8,128)(2,1)S(1)}, u32[]{:S(2)}, u32[]{:S(2)}) collective-permute-start(bf16[2,4,128,128]{3,2,1,0:T(8,128)(2,1)S(1)} %get-tuple-element.77), channel_id=1, source_target_pairs={{0,4},{4,0},{8,12},{12,8},{16,20},{20,16},{24,28},{28,24},{1,5},{5... | collective-permute-start | bytes 786440 | tf_op jit(solution)/shard_map/ppermute | solution.py:319
  40.7 7.5 %collective-permute-start.11 = (bf16[2,4,128,128]{3,2,1,0:T(8,128)(2,1)S(1)}, bf16[2,4,128,128]{3,2,1,0:T(8,128)(2,1)S(1)}, u32[]{:S(2)}, u32[]{:S(2)}) collective-permute-start(bf16[2,4,128,128]{3,2,1,0:T(8,128)(2,1)S(1)} %get-tuple-element.68.rest_0_.rest_2_), channel_id=1, source_target_pairs={{0,4},{4,0},{8,12},{12,8},{16,20},{20,16},{24,28},{28,24},{1,5},{5... | collective-permute-start | bytes 786440 | tf_op jit(solution)/shard_map/ppermute | solution.py:319
  48.2 21.9 %collective-permute-start.12 = (bf16[2,64,2048]{2,1,0:T(8,128)(2,1)S(1)}, bf16[2,64,2048]{2,1,0:T(8,128)(2,1)S(1)}, u32[]{:S(2)}, u32[]{:S(2)}) collective-permute-start(bf16[2,64,2048]{2,1,0:T(8,128)(2,1)S(1)} %get-tuple-element.79), channel_id=1, source_target_pairs={{4,0},{8,4},{12,8},{16,12},{20,16},{24,20},{28,24},{5,1},{9,5},{13... | collective-permute-start | bytes 1572872 | tf_op jit(solution)/shard_map/ppermute | solution.py:348
  54.1 9.8 %collective-permute-start.14 = (bf16[2,128,128]{2,1,0:T(8,128)(2,1)S(1)}, bf16[2,128,128]{2,1,0:T(8,128)(2,1)S(1)}, u32[]{:S(2)}, u32[]{:S(2)}) collective-permute-start(bf16[2,128,128]{2,1,0:T(8,128)(2,1)S(1)} %get-tuple-element.107), channel_id=1, source_target_pairs={{0,4},{1,5},{2,6},{3,7},{4,0},{5,1},{6,2},{7,3},{8,12},{9,13},{10,... | collective-permute-start | bytes 196616 | tf_op jit(solution)/shard_map/ppermute | solution.py:329
  56.8 7.1 %collective-permute-start.15 = (bf16[2,128,128]{2,1,0:T(8,128)(2,1)S(1)}, bf16[2,128,128]{2,1,0:T(8,128)(2,1)S(1)}, u32[]{:S(2)}, u32[]{:S(2)}) collective-permute-start(bf16[2,128,128]{2,1,0:T(8,128)(2,1)S(1)} %get-tuple-element.108), channel_id=1, source_target_pairs={{0,2},{1,3},{2,0},{3,1},{4,6},{5,7},{6,4},{7,5},{8,10},{9,11},{10,... | collective-permute-start | bytes 196616 | tf_op jit(solution)/shard_map/ppermute | solution.py:329
  58.3 7.3 %collective-permute-start.16 = (bf16[2,128,128]{2,1,0:T(8,128)(2,1)S(1)}, bf16[2,128,128]{2,1,0:T(8,128)(2,1)S(1)}, u32[]{:S(2)}, u32[]{:S(2)}) collective-permute-start(bf16[2,128,128]{2,1,0:T(8,128)(2,1)S(1)} %get-tuple-element.109), channel_id=1, source_target_pairs={{0,6},{1,7},{2,4},{3,5},{4,2},{5,3},{6,0},{7,1},{8,14},{9,15},{10,... | collective-permute-start | bytes 196616 | tf_op jit(solution)/shard_map/ppermute | solution.py:329
  65.6 7.9 %collective-permute-start.17 = (bf16[2,128,128]{2,1,0:T(8,128)(2,1)S(1)}, bf16[2,128,128]{2,1,0:T(8,128)(2,1)S(1)}, u32[]{:S(2)}, u32[]{:S(2)}) collective-permute-start(bf16[2,128,128]{2,1,0:T(8,128)(2,1)S(1)} %total.2.refs_0_), channel_id=1, source_target_pairs={{0,8},{1,9},{2,10},{3,11},{4,12},{5,13},{6,14},{7,15},{8,0},{9,1},... | collective-permute-start | bytes 196616 | tf_op jit(solution)/shard_map/ppermute | solution.py:329
  66.2 7.4 %collective-permute-start.18 = (bf16[2,128,128]{2,1,0:T(8,128)(2,1)S(1)}, bf16[2,128,128]{2,1,0:T(8,128)(2,1)S(1)}, u32[]{:S(2)}, u32[]{:S(2)}) collective-permute-start(bf16[2,128,128]{2,1,0:T(8,128)(2,1)S(1)} %total.2.refs_0_), channel_id=1, source_target_pairs={{0,16},{1,17},{2,18},{3,19},{4,20},{5,21},{6,22},{7,23},{8,24},{9,... | collective-permute-start | bytes 196616 | tf_op jit(solution)/shard_map/ppermute | solution.py:329
  68.9 6.1 %collective-permute-start.19 = (bf16[2,128,128]{2,1,0:T(8,128)(2,1)S(1)}, bf16[2,128,128]{2,1,0:T(8,128)(2,1)S(1)}, u32[]{:S(2)}, u32[]{:S(2)}) collective-permute-start(bf16[2,128,128]{2,1,0:T(8,128)(2,1)S(1)} %total.2.refs_0_), channel_id=1, source_target_pairs={{0,24},{1,25},{2,26},{3,27},{4,28},{5,29},{6,30},{7,31},{8,16},{9,... | collective-permute-start | bytes 196616 | tf_op jit(solution)/shard_map/ppermute | solution.py:329
  75.0 5.0 %collective-permute-start.20 = (bf16[2,128,128]{2,1,0:T(8,128)(2,1)S(1)}, bf16[2,128,128]{2,1,0:T(8,128)(2,1)S(1)}, u32[]{:S(2)}, u32[]{:S(2)}) collective-permute-start(bf16[2,128,128]{2,1,0:T(8,128)(2,1)S(1)} %total.3.refs_0_), channel_id=1, source_target_pairs={{0,2},{1,3},{2,0},{3,1},{4,6},{5,7},{6,4},{7,5},{8,10},{9,11},{10,... | collective-permute-start | bytes 196616 | tf_op jit(solution)/shard_map/ppermute | solution.py:329
  75.6 4.7 %collective-permute-start.23 = (bf16[2,128,128]{2,1,0:T(8,128)(2,1)S(1)}, bf16[2,128,128]{2,1,0:T(8,128)(2,1)S(1)}, u32[]{:S(2)}, u32[]{:S(2)}) collective-permute-start(bf16[2,128,128]{2,1,0:T(8,128)(2,1)S(1)} %total.3.refs_0_), channel_id=1, source_target_pairs={{0,4},{1,5},{2,6},{3,7},{4,0},{5,1},{6,2},{7,3},{8,12},{9,13},{10,... | collective-permute-start | bytes 196616 | tf_op jit(solution)/shard_map/ppermute | solution.py:329
  77.6 5.2 %collective-permute-start.24 = (bf16[2,128,128]{2,1,0:T(8,128)(2,1)S(1)}, bf16[2,128,128]{2,1,0:T(8,128)(2,1)S(1)}, u32[]{:S(2)}, u32[]{:S(2)}) collective-permute-start(bf16[2,128,128]{2,1,0:T(8,128)(2,1)S(1)} %total.3.refs_0_), channel_id=1, source_target_pairs={{0,6},{1,7},{2,4},{3,5},{4,2},{5,3},{6,0},{7,1},{8,14},{9,15},{10,... | collective-permute-start | bytes 196616 | tf_op jit(solution)/shard_map/ppermute | solution.py:329
  78.5 4.2 %collective-permute-start.21 = (bf16[2,128,128]{2,1,0:T(8,128)(2,1)S(1)}, bf16[2,128,128]{2,1,0:T(8,128)(2,1)S(1)}, u32[]{:S(2)}, u32[]{:S(2)}) collective-permute-start(bf16[2,128,128]{2,1,0:T(8,128)(2,1)S(1)} %total.3.refs_0_), channel_id=1, source_target_pairs={{0,1},{1,0},{2,3},{3,2},{4,5},{5,4},{6,7},{7,6},{8,9},{9,8},{10,11... | collective-permute-start | bytes 196616 | tf_op jit(solution)/shard_map/ppermute | solution.py:329
  80.0 2.7 %collective-permute-start.22 = (bf16[2,128,128]{2,1,0:T(8,128)(2,1)S(1)}, bf16[2,128,128]{2,1,0:T(8,128)(2,1)S(1)}, u32[]{:S(2)}, u32[]{:S(2)}) collective-permute-start(bf16[2,128,128]{2,1,0:T(8,128)(2,1)S(1)} %collective-permute-done.20.refs_1_), channel_id=1, source_target_pairs={{0,1},{1,0},{2,3},{3,2},{4,5},{5,4},{6,7},{7,6},{8,9},{9,8},{10,11... | collective-permute-start | bytes 196616 | tf_op jit(solution)/shard_map/ppermute | solution.py:329
  (10 other events, 69.8 us)

commit v5 on v4

--- a/solution.py
+++ b/solution.py
@@ -79,15 +79,14 @@
     )(*operands)
 
 
-def feature_kernel(first, count, ends_too, lq, lk, v, g, fm, wk, *rest):
+def feature_kernel(partner, lq, lk, v, g, fm, wk, *rest):
     fq_out, fk_out, *t_out, rows, maps, arrived = rest
-    t_out = t_out[-count - ends_too :]
-    ends = t_out.pop() if ends_too else None
-    half = own_half() if count == CHUNKS else 1 - own_half()
-    steps = count * CHUNK // GROUP
+    ends = t_out.pop() if partner else None
+    half = 1 - own_half() if partner else own_half()
+    steps = HALF // GROUP
 
     def copies(step):
-        head = half * HALF + first * CHUNK + step * GROUP
+        head = half * HALF + step * GROUP
         wide = pl.ds(pl.multiple_of(head * HD, GROUP * HD), GROUP * HD)
         here = slice(step * GROUP * HD, (step + 1) * GROUP * HD)
         pairs = [(ref.at[:, wide], rows.at[n, :, here]) for n, ref in enumerate((lq, lk, v, g))]
@@ -102,7 +101,7 @@
         pltpu.make_async_copy(
             ref.at[pl.ds(ref.shape[0] - WINDOW, WINDOW)], ends.at[n], arrived.at[n, 5]
         )
-        for n, ref in enumerate((wk, v) if ends_too else ())
+        for n, ref in enumerate((wk, v) if partner else ())
     ]
     for copy in [copy for step in started for copy in step] + tails:
         copy.start()
@@ -129,26 +128,27 @@
     kernel(*refs[:at], *refs[at + 1 :])
 
 
-def features(first, count, ends_too, lq, lk, v, g, fm, wk, follows):
+def features(lq, lk, v, g, fm, wk, follows):
     tokens = lq.shape[0]
-    row = array((tokens, count * CHUNK * HD), BF)
-    outs = [row, row] + [array((2, CHUNK, HD, HD), BF)] * count
+    partner = follows is None
+    row = array((tokens, HALF * HD), BF)
+    outs = [row, row] + [array((2, CHUNK, HD, HD), BF)] * CHUNKS
     operands = [pltpu.with_memory_space_constraint(x, pltpu.HBM) for x in (lq, lk, v, g, fm, wk)]
-    kernel = functools.partial(feature_kernel, first, count, ends_too)
-    if follows is not None:
+    kernel = functools.partial(feature_kernel, partner)
+    if not partner:
         kernel = functools.partial(dropped, kernel, len(operands))
         operands.append(follows)
     return call(
         kernel,
         "features",
-        outs + [array((2, WINDOW, WIDE), BF)] * ends_too,
+        outs + [array((2, WINDOW, WIDE), BF)] * partner,
         operands,
         in_hbm=6,
         unread=len(operands) - 6,
         scratch_shapes=[
-            pltpu.VMEM((4, tokens, count * CHUNK * HD), BF),
-            pltpu.VMEM((count * CHUNK, HD, HD), BF),
-            pltpu.SemaphoreType.DMA((count * CHUNK // GROUP, 6)),
+            pltpu.VMEM((4, tokens, HALF * HD), BF),
+            pltpu.VMEM((HALF, HD, HD), BF),
+            pltpu.SemaphoreType.DMA((HALF // GROUP, 6)),
         ],
     )
 
@@ -231,15 +231,11 @@
     scale = lin_scale(lq.shape[0])
     causal = causal_mask(lq.shape[0])
     if side == 1:
-        keep[0], send[0] = rest[count][0], rest[count + 1][0]
-        if first > 0:
-            keep[1, :, :first] = rest[count][1, :, :first]
-            send[1, :, :first] = rest[count + 1][1, :, :first]
+        keep[...], send[...] = rest[count][...], rest[count + 1][...]
     for n in range(count):
         heads = [(first + n) * CHUNK + h for h in range(CHUNK)]
         at = [col_of(half, head) for head in heads]
-        local = [col(n * CHUNK + h) for h in range(CHUNK)]
-        q_feat, k_feat = [fq[:, x] for x in local], [fk[:, x] for x in local]
+        q_feat, k_feat = [fq[:, col(x)] for x in heads], [fk[:, col(x)] for x in heads]
         val, grad = [v[:, x] for x in at], [g[:, x] for x in at]
         mixed = [jnp.where(causal, dot_nt(a, b), 0.0).astype(BF) for a, b in zip(grad, val)]
         dfq = [dot_nt(a, states[n][0, h]) for h, a in enumerate(grad)]
@@ -284,12 +280,12 @@
     for side in range(2):
         half = own_half() ^ side
         refs = rest[: 4 + CHUNKS] if side == 0 else rest[4 + CHUNKS : -7]
-        states, pairs = refs[:CHUNKS], refs[CHUNKS:]
-        each = 4 * HALF // len(pairs)
+        states, (fq, fk, *pairs) = refs[:CHUNKS], refs[CHUNKS:]
+        each = 2 * HALF // len(pairs)
         for n in range(CHUNKS):
             heads = [n * CHUNK + k for k in range(CHUNK)]
-            cols = [(col(h % each), col_of(half, h)) for h in heads]
-            fq, fk, dpq, dpk = pairs[4 * (n * CHUNK // each) :][:4]
+            cols = [(col(h), col_of(half, h)) for h in heads]
+            dpq, dpk = pairs[2 * (n * CHUNK // each) :][:2]
             scores = [
                 jnp.where(causal, dot_nt(fq[:, c], fk[:, c]), 0.0).astype(BF) for c, _ in cols
             ]
@@ -492,16 +488,12 @@
     )
     rows = (lq, lk, v, g)
     inputs = (*rows, feature_map, wk)
-    feats, came, last = [], [], None
-    for n in range(CHUNKS):
-        fq, fk, sums, *ends = features(n, 1, n == CHUNKS - 1, *inputs, last)
-        last = fq
-        feats.append((fq, fk))
-        came.append(flipped(sums, 1))
-    far_ends = relayed(ends[0])
-    fq, fk, *kept = features(0, CHUNKS, False, *inputs, last)
+    fq_o, fk_o, *given, ends = features(*inputs, None)
+    came = [flipped(x, 1) for x in given]
+    far_ends = relayed(ends)
+    fq, fk, *kept = features(*inputs, fq_o)
     came[-1], far_ends = lax.optimization_barrier((came[-1], far_ends))
-    rims = flipped(relay(ends[0], far_ends), 1)
+    rims = flipped(relay(ends, far_ends), 1)
     pair, sent = zip(*(pair_sum(a, b) for a, b in zip(kept, came)))
     pair, sent = list(pair), list(sent)
     gots = [[] for _ in range(CHUNKS)]
@@ -513,15 +505,15 @@
     mine, others = zip(*(entering(kept[n], came[n], gots[n]) for n in range(CHUNKS)))
     back = [flipped(x, 1) for x in others]
     *windows, edge = window_part(wq, wk, v, g, rims, others[-1])
-    back, edge = lax.optimization_barrier((back, edge))
-    edge = passed_along(edge, -1)
     dpq, dpk, *terms = state_part(0, CHUNKS, (*rows, fq, fk), mine, (), (others[-1],))
     own = (*mine, fq, fk, dpq, dpk)
-    pairs = []
-    for n in range(CHUNKS):
-        dpq, dpk, *terms = state_part(n, 1, (*rows, *feats[n]), (back[n],), terms)
-        pairs += [*feats[n], dpq, dpk]
-    other = (*back, *pairs)
+    back[0], edge, terms = lax.optimization_barrier((back[0], edge, terms))
+    edge = passed_along(edge, -1)
+    pairs = [None] * CHUNKS
+    for n in reversed(range(CHUNKS)):
+        *pairs[n], keep, send = state_part(n, 1, (*rows, fq_o, fk_o), (back[n],), terms)
+        terms = (keep, send)
+    other = (*back, fq_o, fk_o, *(x for pair in pairs for x in pair))
     keep, send = terms
     near, a, b, c = near_sum(keep, flat_flipped(send, 0, 1))
     a, b, c = flat_flipped(a, 1, 0), flat_flipped(b, 0, 2), flat_flipped(c, 1, 2)

time: 85.4 us -> 81.9 us (0.959)
  waiting for transfers between devices: 34.5 us -> 32.2 us
  Pallas kernels: 18.4 us -> 17.5 us
    ppermute x5, waiting for transfers between devices: 9.89 us -> 7.2 us  [flipped(): return lax.ppermute(block, 'seq', [(i, i ^ bit) for i in range(count)])]
    pallas_call x19 -> x18, Pallas kernels: 18.4 us -> 17.5 us  [call(): pl.pallas_call(kernel, in_specs=[pl.BlockSpec(memory_space=pltpu.HBM)] *...]
  transfers between devices with their start and end apart: 27 -> 27, of which waited for: 13 -> 14; matrix products, arithmetic and copies ran while one was open for 0% -> 0% of each run, Pallas kernels for 16% -> 17%
where the time goes in v5:
time: 81.9 us; the launch traced here: 81.7 us
  waiting for transfers between devices  32.2 us (39%)
  starting transfers between devices  31 us (38%)
  Pallas kernels  17.5 us (21%)
  between operations  0.89 us (1%)
    pallas_call x18, Pallas kernels, call(): pl.pallas_call(kernel, in_specs=[pl.BlockSpec(memory_space=pltpu.HBM)] *...  17.5 us
    ppermute x14, waiting for transfers between devices, flat_flipped(): return lax.ppermute(block, ('seq', 'dp'), route)  15.8 us
    ppermute x14, starting transfers between devices, flat_flipped(): return lax.ppermute(block, ('seq', 'dp'), route)  12.4 us
    ppermute x5, starting transfers between devices, flipped(): return lax.ppermute(block, 'seq', [(i, i ^ bit) for i in range(count)])  9.36 us
    ppermute x6, waiting for transfers between devices, spread(): arrived.append(lax.ppermute(block, 'seq', route))  9.22 us
    ppermute x6, starting transfers between devices, spread(): arrived.append(lax.ppermute(block, 'seq', route))  7.28 us
    ppermute x5, waiting for transfers between devices, flipped(): return lax.ppermute(block, 'seq', [(i, i ^ bit) for i in range(count)])  7.2 us
  transfers between devices with their start and end apart: 27, of which 14 were waited for; matrix products, arithmetic and copies ran while one was open for 0% of the time, Pallas kernels for 17%

profile of v5, /device:TPU:0, one launch (start us, length us, event | category | flops | bytes accessed | tf_op | source)
XLA Modules:
  0.0 81.7 jit_solution(12567508611722877354)
XLA Ops:
  0.6 2.8 %features.2 = (bf16[128,1024]{1,0:T(8,128)(2,1)S(1)}, bf16[128,1024]{1,0:T(8,128)(2,1)S(1)}, bf16[2,4,128,128]{3,2,1,0:T(8,128)(2,1)S(1)}, bf16[2,4,128,128]{3,2,1,0:T(8,128)(2,1)S(1)}, bf16[2,64,2048]{2,1,0:T(8,128)(2,1)S(1)}) custom-call(bf16[128,2048]{1,0:T(8,128)(2,1)} %bitcast.26, bf16[128,2048]{1,0:T(8,128)(2,1)} %bitcast.31, ...), custom_call_target="tpu_custom_call" | custom-call | flops 3000 | bytes 1000 | tf_op jit(solution)/shard_map/features/pallas_call | solution.py:68
  4.1 5.8 %collective-permute-start.6 = (bf16[2,4,128,128]{3,2,1,0:T(8,128)(2,1)S(1)}, bf16[2,4,128,128]{3,2,1,0:T(8,128)(2,1)S(1)}, u32[]{:S(2)}, u32[]{:S(2)}) collective-permute-start(bf16[2,4,128,128]{3,2,1,0:T(8,128)(2,1)S(1)} %get-tuple-element.72), channel_id=1, source_target_pairs={{0,4},{4,0},{8,12},{12,8},{16,20},{20,16},{24,28},{28,24},{1,5},{5... | collective-permute-start | bytes 786440 | tf_op jit(solution)/shard_map/ppermute | solution.py:315
  10.0 2.8 %features.3 = (bf16[128,1024]{1,0:T(8,128)(2,1)S(1)}, bf16[128,1024]{1,0:T(8,128)(2,1)S(1)}, bf16[2,4,128,128]{3,2,1,0:T(8,128)(2,1)S(1)}, bf16[2,4,128,128]{3,2,1,0:T(8,128)(2,1)S(1)}) custom-call(bf16[128,2048]{1,0:T(8,128)(2,1)} %bitcast.27, bf16[128,2048]{1,0:T(8,128)(2,1)} %bitcast.32, bf16[128,2048]{1,0:T(8,128)(2,1)} %bitcast.13, ...), custom_call_target="tpu_custom_call" | custom-call | flops 3000 | bytes 1000 | tf_op jit(solution)/shard_map/features/pallas_call | solution.py:68
  12.8 4.3 %collective-permute-done.6.came = bf16[2,4,128,128]{3,2,1,0:T(8,128)(2,1)S(1)} collective-permute-done((bf16[2,4,128,128]{3,2,1,0:T(8,128)(2,1)S(1)}, bf16[2,4,128,128]{3,2,1,0:T(8,128)(2,1)S(1)}, u32[]{:S(2)}, u32[]{:S(2)}) %collective-permute-start.6) | collective-permute-done | bytes 262176 | tf_op jit(solution)/shard_map/ppermute | solution.py:315
  17.2 1.6 %collective-permute-start.7 = (bf16[4,128,128]{2,1,0:T(8,128)(2,1)S(1)}, bf16[4,128,128]{2,1,0:T(8,128)(2,1)S(1)}, u32[]{:S(2)}, u32[]{:S(2)}) collective-permute-start(bf16[4,128,128]{2,1,0:T(8,128)(2,1)S(1)} %get-tuple-element.73), channel_id=1, source_target_pairs={{0,8},{8,0},{4,12},{12,4},{16,24},{24,16},{20,28},{28,20},{1,9},{9... | collective-permute-start | bytes 393224 | tf_op jit(solution)/shard_map/ppermute | solution.py:358
  18.8 2.8 %collective-permute-done.came = bf16[2,4,128,128]{3,2,1,0:T(8,128)(2,1)S(1)} collective-permute-done((bf16[2,4,128,128]{3,2,1,0:T(8,128)(2,1)S(1)}, bf16[2,4,128,128]{3,2,1,0:T(8,128)(2,1)S(1)}, u32[]{:S(2)}, u32[]{:S(2)}) %collective-permute-start) | collective-permute-done | bytes 262176 | tf_op jit(solution)/shard_map/ppermute | solution.py:315
  21.7 1.8 %collective-permute-start.2 = (bf16[2,64,2048]{2,1,0:T(8,128)(2,1)S(1)}, bf16[2,64,2048]{2,1,0:T(8,128)(2,1)S(1)}, u32[]{:S(2)}, u32[]{:S(2)}) collective-permute-start(bf16[2,64,2048]{2,1,0:T(8,128)(2,1)S(1)} %relay.1), channel_id=1, source_target_pairs={{0,4},{4,0},{8,12},{12,8},{16,20},{20,16},{24,28},{28,24},{1,5},{5... | collective-permute-start | bytes 1572872 | tf_op jit(solution)/shard_map/ppermute | solution.py:315
  23.6 1.6 %collective-permute-start.3 = (bf16[4,128,128]{2,1,0:T(8,128)(2,1)S(1)}, bf16[4,128,128]{2,1,0:T(8,128)(2,1)S(1)}, u32[]{:S(2)}, u32[]{:S(2)}) collective-permute-start(bf16[4,128,128]{2,1,0:T(8,128)(2,1)S(1)} %get-tuple-element.64), channel_id=1, source_target_pairs={{0,8},{8,0},{4,12},{12,4},{16,24},{24,16},{20,28},{28,20},{1,9},{9... | collective-permute-start | bytes 393224 | tf_op jit(solution)/shard_map/ppermute | solution.py:358
  27.3 1.3 %collective-permute-done.3.refs_0_ = bf16[4,128,128]{2,1,0:T(8,128)(2,1)S(1)} collective-permute-done((bf16[4,128,128]{2,1,0:T(8,128)(2,1)S(1)}, bf16[4,128,128]{2,1,0:T(8,128)(2,1)S(1)}, u32[]{:S(2)}, u32[]{:S(2)}) %collective-permute-start.3) | collective-permute-done | bytes 131104 | tf_op jit(solution)/shard_map/ppermute | solution.py:358
  30.8 4.0 %collective-permute-done.9.refs_2_ = bf16[4,128,128]{2,1,0:T(8,128)(2,1)S(1)} collective-permute-done((bf16[4,128,128]{2,1,0:T(8,128)(2,1)S(1)}, bf16[4,128,128]{2,1,0:T(8,128)(2,1)S(1)}, u32[]{:S(2)}, u32[]{:S(2)}) %collective-permute-start.9) | collective-permute-done | bytes 131104 | tf_op jit(solution)/shard_map/ppermute | solution.py:358
  35.6 3.9 %collective-permute-done.5.refs_2_ = bf16[4,128,128]{2,1,0:T(8,128)(2,1)S(1)} collective-permute-done((bf16[4,128,128]{2,1,0:T(8,128)(2,1)S(1)}, bf16[4,128,128]{2,1,0:T(8,128)(2,1)S(1)}, u32[]{:S(2)}, u32[]{:S(2)}) %collective-permute-start.5) | collective-permute-done | bytes 131104 | tf_op jit(solution)/shard_map/ppermute | solution.py:358
  40.9 1.4 %state_part.3 = (bf16[128,1024]{1,0:T(8,128)(2,1)S(1)}, bf16[128,1024]{1,0:T(8,128)(2,1)S(1)}, bf16[2,2,2,128,128]{4,3,2,1,0:T(8,128)(2,1)S(1)}, bf16[2,2,2,128,128]{4,3,2,1,0:T(8,128)(2,1)S(1)}) custom-call(bf16[128,2048]{1,0:T(8,128)(2,1)S(1)} %bitcast.28, bf16[128,2048]{1,0:T(8,128)(2,1)S(1)} %bitcast.33, bf16[128,2048]{1,0:T(8,128)(2,1)S(1)} %bitcast.14, ...), custom_call_target="tpu_custom_call" | custom-call | flops 3000 | bytes 1000 | tf_op jit(solution)/shard_map/state_part/pallas_call | solution.py:68
  42.3 3.4 %window_part.1 = (f32[128,2048]{1,0:T(8,128)S(1)}, f32[128,2048]{1,0:T(8,128)S(1)}, bf16[128,2048]{1,0:T(8,128)(2,1)S(1)}, f32[128,2048]{1,0:T(8,128)S(1)}, bf16[2,64,2048]{2,1,0:T(8,128)(2,1)S(1)}) custom-call(bf16[128,2048]{1,0:T(8,128)(2,1)S(1)} %bitcast.39, bf16[128,2048]{1,0:T(8,128)(2,1)S(1)} %bitcast.38, bf16[128,2048]{1,0:T(8,128)(2,1)S(1)} %bitcast.15, ...), custom_call_target="tpu_custom_call" | custom-call | flops 3000 | bytes 1000 | tf_op jit(solution)/shard_map/window_part/pallas_call | solution.py:68
  48.8 1.5 %collective-permute-done.13.came = bf16[2,2,2,128,128]{4,3,2,1,0:T(8,128)(2,1)S(1)} collective-permute-done((bf16[2,2,2,128,128]{4,3,2,1,0:T(8,128)(2,1)S(1)}, bf16[2,2,2,128,128]{4,3,2,1,0:T(8,128)(2,1)S(1)}, u32[]{:S(2)}, u32[]{:S(2)}) %collective-permute-start.13) | collective-permute-done | bytes 262176 | tf_op jit(solution)/shard_map/ppermute | solution.py:325
  50.4 2.6 %collective-permute-start.14 = (bf16[2,128,128]{2,1,0:T(8,128)(2,1)S(1)}, bf16[2,128,128]{2,1,0:T(8,128)(2,1)S(1)}, u32[]{:S(2)}, u32[]{:S(2)}) collective-permute-start(bf16[2,128,128]{2,1,0:T(8,128)(2,1)S(1)} %get-tuple-element.105), channel_id=1, source_target_pairs={{0,4},{1,5},{2,6},{3,7},{4,0},{5,1},{6,2},{7,3},{8,12},{9,13},{10,... | collective-permute-start | bytes 196616 | tf_op jit(solution)/shard_map/ppermute | solution.py:325
  53.0 1.5 %collective-permute-start.15 = (bf16[2,128,128]{2,1,0:T(8,128)(2,1)S(1)}, bf16[2,128,128]{2,1,0:T(8,128)(2,1)S(1)}, u32[]{:S(2)}, u32[]{:S(2)}) collective-permute-start(bf16[2,128,128]{2,1,0:T(8,128)(2,1)S(1)} %get-tuple-element.106), channel_id=1, source_target_pairs={{0,2},{1,3},{2,0},{3,1},{4,6},{5,7},{6,4},{7,5},{8,10},{9,11},{10,... | collective-permute-start | bytes 196616 | tf_op jit(solution)/shard_map/ppermute | solution.py:325
  54.5 5.9 %collective-permute-done.14.refs_1_ = bf16[2,128,128]{2,1,0:T(8,128)(2,1)S(1)} collective-permute-done((bf16[2,128,128]{2,1,0:T(8,128)(2,1)S(1)}, bf16[2,128,128]{2,1,0:T(8,128)(2,1)S(1)}, u32[]{:S(2)}, u32[]{:S(2)}) %collective-permute-start.14) | collective-permute-done | bytes 65568 | tf_op jit(solution)/shard_map/ppermute | solution.py:325
  60.5 1.6 %collective-permute-done.16.refs_3_ = bf16[2,128,128]{2,1,0:T(8,128)(2,1)S(1)} collective-permute-done((bf16[2,128,128]{2,1,0:T(8,128)(2,1)S(1)}, bf16[2,128,128]{2,1,0:T(8,128)(2,1)S(1)}, u32[]{:S(2)}, u32[]{:S(2)}) %collective-permute-start.16) | collective-permute-done | bytes 65568 | tf_op jit(solution)/shard_map/ppermute | solution.py:325
  62.1 1.5 %collective-permute-start.17 = (bf16[2,128,128]{2,1,0:T(8,128)(2,1)S(1)}, bf16[2,128,128]{2,1,0:T(8,128)(2,1)S(1)}, u32[]{:S(2)}, u32[]{:S(2)}) collective-permute-start(bf16[2,128,128]{2,1,0:T(8,128)(2,1)S(1)} %total.2.refs_0_), channel_id=1, source_target_pairs={{0,8},{1,9},{2,10},{3,11},{4,12},{5,13},{6,14},{7,15},{8,0},{9,1},... | collective-permute-start | bytes 196616 | tf_op jit(solution)/shard_map/ppermute | solution.py:325
  63.6 3.1 %collective-permute-start.18 = (bf16[2,128,128]{2,1,0:T(8,128)(2,1)S(1)}, bf16[2,128,128]{2,1,0:T(8,128)(2,1)S(1)}, u32[]{:S(2)}, u32[]{:S(2)}) collective-permute-start(bf16[2,128,128]{2,1,0:T(8,128)(2,1)S(1)} %total.2.refs_0_), channel_id=1, source_target_pairs={{0,16},{1,17},{2,18},{3,19},{4,20},{5,21},{6,22},{7,23},{8,24},{9,... | collective-permute-start | bytes 196616 | tf_op jit(solution)/shard_map/ppermute | solution.py:325
  66.7 3.5 %output_part.1 = (bf16[128,2048]{1,0:T(8,128)(2,1)}, bf16[128,2048]{1,0:T(8,128)(2,1)}, bf16[128,2048]{1,0:T(8,128)(2,1)}, bf16[128,2048]{1,0:T(8,128)(2,1)}, bf...) custom-call(bf16[128,2048]{1,0:T(8,128)(2,1)S(1)} %bitcast.18, ...), custom_call_target="tpu_custom_call" | custom-call | flops 3000 | bytes 1000 | tf_op jit(solution)/shard_map/output_part/pallas_call | solution.py:68
  70.3 2.5 %collective-permute-done.19.refs_3_ = bf16[2,128,128]{2,1,0:T(8,128)(2,1)S(1)} collective-permute-done((bf16[2,128,128]{2,1,0:T(8,128)(2,1)S(1)}, bf16[2,128,128]{2,1,0:T(8,128)(2,1)S(1)}, u32[]{:S(2)}, u32[]{:S(2)}) %collective-permute-start.19) | collective-permute-done | bytes 65568 | tf_op jit(solution)/shard_map/ppermute | solution.py:325
  73.4 3.0 %collective-permute-start.24 = (bf16[2,128,128]{2,1,0:T(8,128)(2,1)S(1)}, bf16[2,128,128]{2,1,0:T(8,128)(2,1)S(1)}, u32[]{:S(2)}, u32[]{:S(2)}) collective-permute-start(bf16[2,128,128]{2,1,0:T(8,128)(2,1)S(1)} %total.3.refs_0_), channel_id=1, source_target_pairs={{0,6},{1,7},{2,4},{3,5},{4,2},{5,3},{6,0},{7,1},{8,14},{9,15},{10,... | collective-permute-start | bytes 196616 | tf_op jit(solution)/shard_map/ppermute | solution.py:325
  77.7 1.6 %collective-permute-done.24.refs_5_ = bf16[2,128,128]{2,1,0:T(8,128)(2,1)S(1)} collective-permute-done((bf16[2,128,128]{2,1,0:T(8,128)(2,1)S(1)}, bf16[2,128,128]{2,1,0:T(8,128)(2,1)S(1)}, u32[]{:S(2)}, u32[]{:S(2)}) %collective-permute-start.24) | collective-permute-done | bytes 65568 | tf_op jit(solution)/shard_map/ppermute | solution.py:325
  (62 shorter events, 14.8 us)
Async XLA Ops:
  3.4 18.2 %collective-permute-start.1 = (bf16[2,64,2048]{2,1,0:T(8,128)(2,1)S(1)}, bf16[2,64,2048]{2,1,0:T(8,128)(2,1)S(1)}, u32[]{:S(2)}, u32[]{:S(2)}) collective-permute-start(bf16[2,64,2048]{2,1,0:T(8,128)(2,1)S(1)} %get-tuple-element.58.own), channel_id=1, source_target_pairs={{4,12},{12,20},{20,28},{5,13},{13,21},{21,29},{6,14},{14,22},{22,3... | collective-permute-start | bytes 1572872 | tf_op jit(solution)/shard_map/ppermute | solution.py:330
  4.1 13.0 %collective-permute-start.6 = (bf16[2,4,128,128]{3,2,1,0:T(8,128)(2,1)S(1)}, bf16[2,4,128,128]{3,2,1,0:T(8,128)(2,1)S(1)}, u32[]{:S(2)}, u32[]{:S(2)}) collective-permute-start(bf16[2,4,128,128]{3,2,1,0:T(8,128)(2,1)S(1)} %get-tuple-element.72), channel_id=1, source_target_pairs={{0,4},{4,0},{8,12},{12,8},{16,20},{20,16},{24,28},{28,24},{1,5},{5... | collective-permute-start | bytes 786440 | tf_op jit(solution)/shard_map/ppermute | solution.py:315
  10.0 11.6 %collective-permute-start = (bf16[2,4,128,128]{3,2,1,0:T(8,128)(2,1)S(1)}, bf16[2,4,128,128]{3,2,1,0:T(8,128)(2,1)S(1)}, u32[]{:S(2)}, u32[]{:S(2)}) collective-permute-start(bf16[2,4,128,128]{3,2,1,0:T(8,128)(2,1)S(1)} %get-tuple-element.59), channel_id=1, source_target_pairs={{0,4},{4,0},{8,12},{12,8},{16,20},{20,16},{24,28},{28,24},{1,5},{5... | collective-permute-start | bytes 786440 | tf_op jit(solution)/shard_map/ppermute | solution.py:315
  17.2 8.0 %collective-permute-start.7 = (bf16[4,128,128]{2,1,0:T(8,128)(2,1)S(1)}, bf16[4,128,128]{2,1,0:T(8,128)(2,1)S(1)}, u32[]{:S(2)}, u32[]{:S(2)}) collective-permute-start(bf16[4,128,128]{2,1,0:T(8,128)(2,1)S(1)} %get-tuple-element.73), channel_id=1, source_target_pairs={{0,8},{8,0},{4,12},{12,4},{16,24},{24,16},{20,28},{28,20},{1,9},{9... | collective-permute-start | bytes 393224 | tf_op jit(solution)/shard_map/ppermute | solution.py:358
  21.7 20.6 %collective-permute-start.2 = (bf16[2,64,2048]{2,1,0:T(8,128)(2,1)S(1)}, bf16[2,64,2048]{2,1,0:T(8,128)(2,1)S(1)}, u32[]{:S(2)}, u32[]{:S(2)}) collective-permute-start(bf16[2,64,2048]{2,1,0:T(8,128)(2,1)S(1)} %relay.1), channel_id=1, source_target_pairs={{0,4},{4,0},{8,12},{12,8},{16,20},{20,16},{24,28},{28,24},{1,5},{5... | collective-permute-start | bytes 1572872 | tf_op jit(solution)/shard_map/ppermute | solution.py:315
  23.6 5.0 %collective-permute-start.3 = (bf16[4,128,128]{2,1,0:T(8,128)(2,1)S(1)}, bf16[4,128,128]{2,1,0:T(8,128)(2,1)S(1)}, u32[]{:S(2)}, u32[]{:S(2)}) collective-permute-start(bf16[4,128,128]{2,1,0:T(8,128)(2,1)S(1)} %get-tuple-element.64), channel_id=1, source_target_pairs={{0,8},{8,0},{4,12},{12,4},{16,24},{24,16},{20,28},{28,20},{1,9},{9... | collective-permute-start | bytes 393224 | tf_op jit(solution)/shard_map/ppermute | solution.py:358
  25.3 5.5 %collective-permute-start.8 = (bf16[4,128,128]{2,1,0:T(8,128)(2,1)S(1)}, bf16[4,128,128]{2,1,0:T(8,128)(2,1)S(1)}, u32[]{:S(2)}, u32[]{:S(2)}) collective-permute-start(bf16[4,128,128]{2,1,0:T(8,128)(2,1)S(1)} %level_sum.3), channel_id=1, source_target_pairs={{8,16},{16,8},{12,20},{20,12},{9,17},{17,9},{13,21},{21,13},{10,18... | collective-permute-start | bytes 393224 | tf_op jit(solution)/shard_map/ppermute | solution.py:358
  26.0 8.8 %collective-permute-start.9 = (bf16[4,128,128]{2,1,0:T(8,128)(2,1)S(1)}, bf16[4,128,128]{2,1,0:T(8,128)(2,1)S(1)}, u32[]{:S(2)}, u32[]{:S(2)}) collective-permute-start(bf16[4,128,128]{2,1,0:T(8,128)(2,1)S(1)} %level_sum.3), channel_id=1, source_target_pairs={{8,24},{16,0},{12,28},{20,4},{9,25},{17,1},{13,29},{21,5},{10,26},... | collective-permute-start | bytes 393224 | tf_op jit(solution)/shard_map/ppermute | solution.py:358
  28.7 6.9 %collective-permute-start.4 = (bf16[4,128,128]{2,1,0:T(8,128)(2,1)S(1)}, bf16[4,128,128]{2,1,0:T(8,128)(2,1)S(1)}, u32[]{:S(2)}, u32[]{:S(2)}) collective-permute-start(bf16[4,128,128]{2,1,0:T(8,128)(2,1)S(1)} %level_sum.2), channel_id=1, source_target_pairs={{8,16},{16,8},{12,20},{20,12},{9,17},{17,9},{13,21},{21,13},{10,18... | collective-permute-start | bytes 393224 | tf_op jit(solution)/shard_map/ppermute | solution.py:358
  29.5 10.0 %collective-permute-start.5 = (bf16[4,128,128]{2,1,0:T(8,128)(2,1)S(1)}, bf16[4,128,128]{2,1,0:T(8,128)(2,1)S(1)}, u32[]{:S(2)}, u32[]{:S(2)}) collective-permute-start(bf16[4,128,128]{2,1,0:T(8,128)(2,1)S(1)} %level_sum.2), channel_id=1, source_target_pairs={{8,24},{16,0},{12,28},{20,4},{9,25},{17,1},{13,29},{21,5},{10,26},... | collective-permute-start | bytes 393224 | tf_op jit(solution)/shard_map/ppermute | solution.py:358
  35.0 10.7 %collective-permute-start.10 = (bf16[2,4,128,128]{3,2,1,0:T(8,128)(2,1)S(1)}, bf16[2,4,128,128]{3,2,1,0:T(8,128)(2,1)S(1)}, u32[]{:S(2)}, u32[]{:S(2)}) collective-permute-start(bf16[2,4,128,128]{3,2,1,0:T(8,128)(2,1)S(1)} %get-tuple-element.75), channel_id=1, source_target_pairs={{0,4},{4,0},{8,12},{12,8},{16,20},{20,16},{24,28},{28,24},{1,5},{5... | collective-permute-start | bytes 786440 | tf_op jit(solution)/shard_map/ppermute | solution.py:315
  39.7 7.4 %collective-permute-start.12 = (bf16[2,4,128,128]{3,2,1,0:T(8,128)(2,1)S(1)}, bf16[2,4,128,128]{3,2,1,0:T(8,128)(2,1)S(1)}, u32[]{:S(2)}, u32[]{:S(2)}) collective-permute-start(bf16[2,4,128,128]{3,2,1,0:T(8,128)(2,1)S(1)} %get-tuple-element.66.rest_0_.rest_2_), channel_id=1, source_target_pairs={{0,4},{4,0},{8,12},{12,8},{16,20},{20,16},{24,28},{28,24},{1,5},{5... | collective-permute-start | bytes 786440 | tf_op jit(solution)/shard_map/ppermute | solution.py:315
  45.7 21.0 %collective-permute-start.11 = (bf16[2,64,2048]{2,1,0:T(8,128)(2,1)S(1)}, bf16[2,64,2048]{2,1,0:T(8,128)(2,1)S(1)}, u32[]{:S(2)}, u32[]{:S(2)}) collective-permute-start(bf16[2,64,2048]{2,1,0:T(8,128)(2,1)S(1)} %get-tuple-element.83), channel_id=1, source_target_pairs={{4,0},{8,4},{12,8},{16,12},{20,16},{24,20},{28,24},{5,1},{9,5},{13... | collective-permute-start | bytes 1572872 | tf_op jit(solution)/shard_map/ppermute | solution.py:344
  50.4 10.1 %collective-permute-start.14 = (bf16[2,128,128]{2,1,0:T(8,128)(2,1)S(1)}, bf16[2,128,128]{2,1,0:T(8,128)(2,1)S(1)}, u32[]{:S(2)}, u32[]{:S(2)}) collective-permute-start(bf16[2,128,128]{2,1,0:T(8,128)(2,1)S(1)} %get-tuple-element.105), channel_id=1, source_target_pairs={{0,4},{1,5},{2,6},{3,7},{4,0},{5,1},{6,2},{7,3},{8,12},{9,13},{10,... | collective-permute-start | bytes 196616 | tf_op jit(solution)/shard_map/ppermute | solution.py:325
  53.0 7.5 %collective-permute-start.15 = (bf16[2,128,128]{2,1,0:T(8,128)(2,1)S(1)}, bf16[2,128,128]{2,1,0:T(8,128)(2,1)S(1)}, u32[]{:S(2)}, u32[]{:S(2)}) collective-permute-start(bf16[2,128,128]{2,1,0:T(8,128)(2,1)S(1)} %get-tuple-element.106), channel_id=1, source_target_pairs={{0,2},{1,3},{2,0},{3,1},{4,6},{5,7},{6,4},{7,5},{8,10},{9,11},{10,... | collective-permute-start | bytes 196616 | tf_op jit(solution)/shard_map/ppermute | solution.py:325
  54.5 7.6 %collective-permute-start.16 = (bf16[2,128,128]{2,1,0:T(8,128)(2,1)S(1)}, bf16[2,128,128]{2,1,0:T(8,128)(2,1)S(1)}, u32[]{:S(2)}, u32[]{:S(2)}) collective-permute-start(bf16[2,128,128]{2,1,0:T(8,128)(2,1)S(1)} %get-tuple-element.107), channel_id=1, source_target_pairs={{0,6},{1,7},{2,4},{3,5},{4,2},{5,3},{6,0},{7,1},{8,14},{9,15},{10,... | collective-permute-start | bytes 196616 | tf_op jit(solution)/shard_map/ppermute | solution.py:325
  62.1 8.1 %collective-permute-start.17 = (bf16[2,128,128]{2,1,0:T(8,128)(2,1)S(1)}, bf16[2,128,128]{2,1,0:T(8,128)(2,1)S(1)}, u32[]{:S(2)}, u32[]{:S(2)}) collective-permute-start(bf16[2,128,128]{2,1,0:T(8,128)(2,1)S(1)} %total.2.refs_0_), channel_id=1, source_target_pairs={{0,8},{1,9},{2,10},{3,11},{4,12},{5,13},{6,14},{7,15},{8,0},{9,1},... | collective-permute-start | bytes 196616 | tf_op jit(solution)/shard_map/ppermute | solution.py:325
  63.6 6.6 %collective-permute-start.18 = (bf16[2,128,128]{2,1,0:T(8,128)(2,1)S(1)}, bf16[2,128,128]{2,1,0:T(8,128)(2,1)S(1)}, u32[]{:S(2)}, u32[]{:S(2)}) collective-permute-start(bf16[2,128,128]{2,1,0:T(8,128)(2,1)S(1)} %total.2.refs_0_), channel_id=1, source_target_pairs={{0,16},{1,17},{2,18},{3,19},{4,20},{5,21},{6,22},{7,23},{8,24},{9,... | collective-permute-start | bytes 196616 | tf_op jit(solution)/shard_map/ppermute | solution.py:325
  66.7 6.1 %collective-permute-start.19 = (bf16[2,128,128]{2,1,0:T(8,128)(2,1)S(1)}, bf16[2,128,128]{2,1,0:T(8,128)(2,1)S(1)}, u32[]{:S(2)}, u32[]{:S(2)}) collective-permute-start(bf16[2,128,128]{2,1,0:T(8,128)(2,1)S(1)} %total.2.refs_0_), channel_id=1, source_target_pairs={{0,24},{1,25},{2,26},{3,27},{4,28},{5,29},{6,30},{7,31},{8,16},{9,... | collective-permute-start | bytes 196616 | tf_op jit(solution)/shard_map/ppermute | solution.py:325
  72.8 4.3 %collective-permute-start.20 = (bf16[2,128,128]{2,1,0:T(8,128)(2,1)S(1)}, bf16[2,128,128]{2,1,0:T(8,128)(2,1)S(1)}, u32[]{:S(2)}, u32[]{:S(2)}) collective-permute-start(bf16[2,128,128]{2,1,0:T(8,128)(2,1)S(1)} %total.3.refs_0_), channel_id=1, source_target_pairs={{0,2},{1,3},{2,0},{3,1},{4,6},{5,7},{6,4},{7,5},{8,10},{9,11},{10,... | collective-permute-start | bytes 196616 | tf_op jit(solution)/shard_map/ppermute | solution.py:325
  73.4 4.3 %collective-permute-start.23 = (bf16[2,128,128]{2,1,0:T(8,128)(2,1)S(1)}, bf16[2,128,128]{2,1,0:T(8,128)(2,1)S(1)}, u32[]{:S(2)}, u32[]{:S(2)}) collective-permute-start(bf16[2,128,128]{2,1,0:T(8,128)(2,1)S(1)} %total.3.refs_0_), channel_id=1, source_target_pairs={{0,4},{1,5},{2,6},{3,7},{4,0},{5,1},{6,2},{7,3},{8,12},{9,13},{10,... | collective-permute-start | bytes 196616 | tf_op jit(solution)/shard_map/ppermute | solution.py:325
  73.4 5.9 %collective-permute-start.24 = (bf16[2,128,128]{2,1,0:T(8,128)(2,1)S(1)}, bf16[2,128,128]{2,1,0:T(8,128)(2,1)S(1)}, u32[]{:S(2)}, u32[]{:S(2)}) collective-permute-start(bf16[2,128,128]{2,1,0:T(8,128)(2,1)S(1)} %total.3.refs_0_), channel_id=1, source_target_pairs={{0,6},{1,7},{2,4},{3,5},{4,2},{5,3},{6,0},{7,1},{8,14},{9,15},{10,... | collective-permute-start | bytes 196616 | tf_op jit(solution)/shard_map/ppermute | solution.py:325
  76.4 2.9 %collective-permute-start.21 = (bf16[2,128,128]{2,1,0:T(8,128)(2,1)S(1)}, bf16[2,128,128]{2,1,0:T(8,128)(2,1)S(1)}, u32[]{:S(2)}, u32[]{:S(2)}) collective-permute-start(bf16[2,128,128]{2,1,0:T(8,128)(2,1)S(1)} %total.3.refs_0_), channel_id=1, source_target_pairs={{0,1},{1,0},{2,3},{3,2},{4,5},{5,4},{6,7},{7,6},{8,9},{9,8},{10,11... | collective-permute-start | bytes 196616 | tf_op jit(solution)/shard_map/ppermute | solution.py:325
  77.2 2.2 %collective-permute-start.22 = (bf16[2,128,128]{2,1,0:T(8,128)(2,1)S(1)}, bf16[2,128,128]{2,1,0:T(8,128)(2,1)S(1)}, u32[]{:S(2)}, u32[]{:S(2)}) collective-permute-start(bf16[2,128,128]{2,1,0:T(8,128)(2,1)S(1)} %collective-permute-done.20.refs_1_), channel_id=1, source_target_pairs={{0,1},{1,0},{2,3},{3,2},{4,5},{5,4},{6,7},{7,6},{8,9},{9,8},{10,11... | collective-permute-start | bytes 196616 | tf_op jit(solution)/shard_map/ppermute | solution.py:325
  (10 other events, 55.5 us)

commit v6 on v5

--- a/solution.py
+++ b/solution.py
@@ -13,7 +13,7 @@
 HALF = HEADS // 2
 CHUNKS = 2
 CHUNK = HALF // CHUNKS
-GROUP = 2
+GROUP = 4
 WINDOW_GROUP = 4
 WIDE = HEADS * HD
 VMEM = 8 * 1024 * 1024

time: 81.9 us -> 81.4 us (level)
  Pallas kernels: 17.5 us -> 16.5 us
    pallas_call x18, Pallas kernels: 17.5 us -> 16.5 us  [call(): pl.pallas_call(kernel, in_specs=[pl.BlockSpec(memory_space=pltpu.HBM)] *...]
  transfers between devices with their start and end apart: 27 -> 27, of which waited for: 14 -> 14; matrix products, arithmetic and copies ran while one was open for 0% -> 0% of each run, Pallas kernels for 17% -> 16%
where the time goes in v6:
time: 81.4 us; the launch traced here: 81.1 us
  waiting for transfers between devices  32.7 us (40%)
  starting transfers between devices  31.1 us (38%)
  Pallas kernels  16.5 us (20%)
  between operations  0.89 us (1%)
    pallas_call x18, Pallas kernels, call(): pl.pallas_call(kernel, in_specs=[pl.BlockSpec(memory_space=pltpu.HBM)] *...  16.5 us
    ppermute x14, waiting for transfers between devices, flat_flipped(): return lax.ppermute(block, ('seq', 'dp'), route)  15.8 us
    ppermute x14, starting transfers between devices, flat_flipped(): return lax.ppermute(block, ('seq', 'dp'), route)  12.4 us
    ppermute x5, starting transfers between devices, flipped(): return lax.ppermute(block, 'seq', [(i, i ^ bit) for i in range(count)])  9.38 us
    ppermute x6, waiting for transfers between devices, spread(): arrived.append(lax.ppermute(block, 'seq', route))  9.21 us
    ppermute x5, waiting for transfers between devices, flipped(): return lax.ppermute(block, 'seq', [(i, i ^ bit) for i in range(count)])  7.68 us
    ppermute x6, starting transfers between devices, spread(): arrived.append(lax.ppermute(block, 'seq', route))  7.28 us
  transfers between devices with their start and end apart: 27, of which 14 were waited for; matrix products, arithmetic and copies ran while one was open for 0% of the time, Pallas kernels for 16%

profile of v6, /device:TPU:0, one launch (start us, length us, event | category | flops | bytes accessed | tf_op | source)
XLA Modules:
  0.0 81.1 jit_solution(10628144547458184599)
XLA Ops:
  0.6 2.3 %features.2 = (bf16[128,1024]{1,0:T(8,128)(2,1)S(1)}, bf16[128,1024]{1,0:T(8,128)(2,1)S(1)}, bf16[2,4,128,128]{3,2,1,0:T(8,128)(2,1)S(1)}, bf16[2,4,128,128]{3,2,1,0:T(8,128)(2,1)S(1)}, bf16[2,64,2048]{2,1,0:T(8,128)(2,1)S(1)}) custom-call(bf16[128,2048]{1,0:T(8,128)(2,1)} %bitcast.26, bf16[128,2048]{1,0:T(8,128)(2,1)} %bitcast.31, ...), custom_call_target="tpu_custom_call" | custom-call | flops 3000 | bytes 1000 | tf_op jit(solution)/shard_map/features/pallas_call | solution.py:68
  3.6 5.8 %collective-permute-start.6 = (bf16[2,4,128,128]{3,2,1,0:T(8,128)(2,1)S(1)}, bf16[2,4,128,128]{3,2,1,0:T(8,128)(2,1)S(1)}, u32[]{:S(2)}, u32[]{:S(2)}) collective-permute-start(bf16[2,4,128,128]{3,2,1,0:T(8,128)(2,1)S(1)} %get-tuple-element.72), channel_id=1, source_target_pairs={{0,4},{4,0},{8,12},{12,8},{16,20},{20,16},{24,28},{28,24},{1,5},{5... | collective-permute-start | bytes 786440 | tf_op jit(solution)/shard_map/ppermute | solution.py:315
  9.5 2.3 %features.3 = (bf16[128,1024]{1,0:T(8,128)(2,1)S(1)}, bf16[128,1024]{1,0:T(8,128)(2,1)S(1)}, bf16[2,4,128,128]{3,2,1,0:T(8,128)(2,1)S(1)}, bf16[2,4,128,128]{3,2,1,0:T(8,128)(2,1)S(1)}) custom-call(bf16[128,2048]{1,0:T(8,128)(2,1)} %bitcast.27, bf16[128,2048]{1,0:T(8,128)(2,1)} %bitcast.32, bf16[128,2048]{1,0:T(8,128)(2,1)} %bitcast.13, ...), custom_call_target="tpu_custom_call" | custom-call | flops 3000 | bytes 1000 | tf_op jit(solution)/shard_map/features/pallas_call | solution.py:68
  11.8 4.8 %collective-permute-done.6.came = bf16[2,4,128,128]{3,2,1,0:T(8,128)(2,1)S(1)} collective-permute-done((bf16[2,4,128,128]{3,2,1,0:T(8,128)(2,1)S(1)}, bf16[2,4,128,128]{3,2,1,0:T(8,128)(2,1)S(1)}, u32[]{:S(2)}, u32[]{:S(2)}) %collective-permute-start.6) | collective-permute-done | bytes 262176 | tf_op jit(solution)/shard_map/ppermute | solution.py:315
  16.7 1.6 %collective-permute-start.7 = (bf16[4,128,128]{2,1,0:T(8,128)(2,1)S(1)}, bf16[4,128,128]{2,1,0:T(8,128)(2,1)S(1)}, u32[]{:S(2)}, u32[]{:S(2)}) collective-permute-start(bf16[4,128,128]{2,1,0:T(8,128)(2,1)S(1)} %get-tuple-element.73), channel_id=1, source_target_pairs={{0,8},{8,0},{4,12},{12,4},{16,24},{24,16},{20,28},{28,20},{1,9},{9... | collective-permute-start | bytes 393224 | tf_op jit(solution)/shard_map/ppermute | solution.py:358
  18.3 2.8 %collective-permute-done.came = bf16[2,4,128,128]{3,2,1,0:T(8,128)(2,1)S(1)} collective-permute-done((bf16[2,4,128,128]{3,2,1,0:T(8,128)(2,1)S(1)}, bf16[2,4,128,128]{3,2,1,0:T(8,128)(2,1)S(1)}, u32[]{:S(2)}, u32[]{:S(2)}) %collective-permute-start) | collective-permute-done | bytes 262176 | tf_op jit(solution)/shard_map/ppermute | solution.py:315
  21.2 1.8 %collective-permute-start.2 = (bf16[2,64,2048]{2,1,0:T(8,128)(2,1)S(1)}, bf16[2,64,2048]{2,1,0:T(8,128)(2,1)S(1)}, u32[]{:S(2)}, u32[]{:S(2)}) collective-permute-start(bf16[2,64,2048]{2,1,0:T(8,128)(2,1)S(1)} %relay.1), channel_id=1, source_target_pairs={{0,4},{4,0},{8,12},{12,8},{16,20},{20,16},{24,28},{28,24},{1,5},{5... | collective-permute-start | bytes 1572872 | tf_op jit(solution)/shard_map/ppermute | solution.py:315
  23.0 1.6 %collective-permute-start.3 = (bf16[4,128,128]{2,1,0:T(8,128)(2,1)S(1)}, bf16[4,128,128]{2,1,0:T(8,128)(2,1)S(1)}, u32[]{:S(2)}, u32[]{:S(2)}) collective-permute-start(bf16[4,128,128]{2,1,0:T(8,128)(2,1)S(1)} %get-tuple-element.64), channel_id=1, source_target_pairs={{0,8},{8,0},{4,12},{12,4},{16,24},{24,16},{20,28},{28,20},{1,9},{9... | collective-permute-start | bytes 393224 | tf_op jit(solution)/shard_map/ppermute | solution.py:358
  26.8 1.3 %collective-permute-done.3.refs_0_ = bf16[4,128,128]{2,1,0:T(8,128)(2,1)S(1)} collective-permute-done((bf16[4,128,128]{2,1,0:T(8,128)(2,1)S(1)}, bf16[4,128,128]{2,1,0:T(8,128)(2,1)S(1)}, u32[]{:S(2)}, u32[]{:S(2)}) %collective-permute-start.3) | collective-permute-done | bytes 131104 | tf_op jit(solution)/shard_map/ppermute | solution.py:358
  30.3 4.0 %collective-permute-done.9.refs_2_ = bf16[4,128,128]{2,1,0:T(8,128)(2,1)S(1)} collective-permute-done((bf16[4,128,128]{2,1,0:T(8,128)(2,1)S(1)}, bf16[4,128,128]{2,1,0:T(8,128)(2,1)S(1)}, u32[]{:S(2)}, u32[]{:S(2)}) %collective-permute-start.9) | collective-permute-done | bytes 131104 | tf_op jit(solution)/shard_map/ppermute | solution.py:358
  35.1 3.9 %collective-permute-done.5.refs_2_ = bf16[4,128,128]{2,1,0:T(8,128)(2,1)S(1)} collective-permute-done((bf16[4,128,128]{2,1,0:T(8,128)(2,1)S(1)}, bf16[4,128,128]{2,1,0:T(8,128)(2,1)S(1)}, u32[]{:S(2)}, u32[]{:S(2)}) %collective-permute-start.5) | collective-permute-done | bytes 131104 | tf_op jit(solution)/shard_map/ppermute | solution.py:358
  40.4 1.4 %state_part.3 = (bf16[128,1024]{1,0:T(8,128)(2,1)S(1)}, bf16[128,1024]{1,0:T(8,128)(2,1)S(1)}, bf16[2,2,2,128,128]{4,3,2,1,0:T(8,128)(2,1)S(1)}, bf16[2,2,2,128,128]{4,3,2,1,0:T(8,128)(2,1)S(1)}) custom-call(bf16[128,2048]{1,0:T(8,128)(2,1)S(1)} %bitcast.28, bf16[128,2048]{1,0:T(8,128)(2,1)S(1)} %bitcast.33, bf16[128,2048]{1,0:T(8,128)(2,1)S(1)} %bitcast.14, ...), custom_call_target="tpu_custom_call" | custom-call | flops 3000 | bytes 1000 | tf_op jit(solution)/shard_map/state_part/pallas_call | solution.py:68
  41.8 3.4 %window_part.1 = (f32[128,2048]{1,0:T(8,128)S(1)}, f32[128,2048]{1,0:T(8,128)S(1)}, bf16[128,2048]{1,0:T(8,128)(2,1)S(1)}, f32[128,2048]{1,0:T(8,128)S(1)}, bf16[2,64,2048]{2,1,0:T(8,128)(2,1)S(1)}) custom-call(bf16[128,2048]{1,0:T(8,128)(2,1)S(1)} %bitcast.39, bf16[128,2048]{1,0:T(8,128)(2,1)S(1)} %bitcast.38, bf16[128,2048]{1,0:T(8,128)(2,1)S(1)} %bitcast.15, ...), custom_call_target="tpu_custom_call" | custom-call | flops 3000 | bytes 1000 | tf_op jit(solution)/shard_map/window_part/pallas_call | solution.py:68
  48.2 1.5 %collective-permute-done.13.came = bf16[2,2,2,128,128]{4,3,2,1,0:T(8,128)(2,1)S(1)} collective-permute-done((bf16[2,2,2,128,128]{4,3,2,1,0:T(8,128)(2,1)S(1)}, bf16[2,2,2,128,128]{4,3,2,1,0:T(8,128)(2,1)S(1)}, u32[]{:S(2)}, u32[]{:S(2)}) %collective-permute-start.13) | collective-permute-done | bytes 262176 | tf_op jit(solution)/shard_map/ppermute | solution.py:325
  49.8 2.6 %collective-permute-start.14 = (bf16[2,128,128]{2,1,0:T(8,128)(2,1)S(1)}, bf16[2,128,128]{2,1,0:T(8,128)(2,1)S(1)}, u32[]{:S(2)}, u32[]{:S(2)}) collective-permute-start(bf16[2,128,128]{2,1,0:T(8,128)(2,1)S(1)} %get-tuple-element.105), channel_id=1, source_target_pairs={{0,4},{1,5},{2,6},{3,7},{4,0},{5,1},{6,2},{7,3},{8,12},{9,13},{10,... | collective-permute-start | bytes 196616 | tf_op jit(solution)/shard_map/ppermute | solution.py:325
  52.5 1.5 %collective-permute-start.15 = (bf16[2,128,128]{2,1,0:T(8,128)(2,1)S(1)}, bf16[2,128,128]{2,1,0:T(8,128)(2,1)S(1)}, u32[]{:S(2)}, u32[]{:S(2)}) collective-permute-start(bf16[2,128,128]{2,1,0:T(8,128)(2,1)S(1)} %get-tuple-element.106), channel_id=1, source_target_pairs={{0,2},{1,3},{2,0},{3,1},{4,6},{5,7},{6,4},{7,5},{8,10},{9,11},{10,... | collective-permute-start | bytes 196616 | tf_op jit(solution)/shard_map/ppermute | solution.py:325
  54.0 5.9 %collective-permute-done.14.refs_1_ = bf16[2,128,128]{2,1,0:T(8,128)(2,1)S(1)} collective-permute-done((bf16[2,128,128]{2,1,0:T(8,128)(2,1)S(1)}, bf16[2,128,128]{2,1,0:T(8,128)(2,1)S(1)}, u32[]{:S(2)}, u32[]{:S(2)}) %collective-permute-start.14) | collective-permute-done | bytes 65568 | tf_op jit(solution)/shard_map/ppermute | solution.py:325
  59.9 1.7 %collective-permute-done.16.refs_3_ = bf16[2,128,128]{2,1,0:T(8,128)(2,1)S(1)} collective-permute-done((bf16[2,128,128]{2,1,0:T(8,128)(2,1)S(1)}, bf16[2,128,128]{2,1,0:T(8,128)(2,1)S(1)}, u32[]{:S(2)}, u32[]{:S(2)}) %collective-permute-start.16) | collective-permute-done | bytes 65568 | tf_op jit(solution)/shard_map/ppermute | solution.py:325
  61.6 1.5 %collective-permute-start.17 = (bf16[2,128,128]{2,1,0:T(8,128)(2,1)S(1)}, bf16[2,128,128]{2,1,0:T(8,128)(2,1)S(1)}, u32[]{:S(2)}, u32[]{:S(2)}) collective-permute-start(bf16[2,128,128]{2,1,0:T(8,128)(2,1)S(1)} %total.2.refs_0_), channel_id=1, source_target_pairs={{0,8},{1,9},{2,10},{3,11},{4,12},{5,13},{6,14},{7,15},{8,0},{9,1},... | collective-permute-start | bytes 196616 | tf_op jit(solution)/shard_map/ppermute | solution.py:325
  63.1 3.1 %collective-permute-start.18 = (bf16[2,128,128]{2,1,0:T(8,128)(2,1)S(1)}, bf16[2,128,128]{2,1,0:T(8,128)(2,1)S(1)}, u32[]{:S(2)}, u32[]{:S(2)}) collective-permute-start(bf16[2,128,128]{2,1,0:T(8,128)(2,1)S(1)} %total.2.refs_0_), channel_id=1, source_target_pairs={{0,16},{1,17},{2,18},{3,19},{4,20},{5,21},{6,22},{7,23},{8,24},{9,... | collective-permute-start | bytes 196616 | tf_op jit(solution)/shard_map/ppermute | solution.py:325
  66.2 3.5 %output_part.1 = (bf16[128,2048]{1,0:T(8,128)(2,1)}, bf16[128,2048]{1,0:T(8,128)(2,1)}, bf16[128,2048]{1,0:T(8,128)(2,1)}, bf16[128,2048]{1,0:T(8,128)(2,1)}, bf...) custom-call(bf16[128,2048]{1,0:T(8,128)(2,1)S(1)} %bitcast.18, ...), custom_call_target="tpu_custom_call" | custom-call | flops 3000 | bytes 1000 | tf_op jit(solution)/shard_map/output_part/pallas_call | solution.py:68
  69.7 2.5 %collective-permute-done.19.refs_3_ = bf16[2,128,128]{2,1,0:T(8,128)(2,1)S(1)} collective-permute-done((bf16[2,128,128]{2,1,0:T(8,128)(2,1)S(1)}, bf16[2,128,128]{2,1,0:T(8,128)(2,1)S(1)}, u32[]{:S(2)}, u32[]{:S(2)}) %collective-permute-start.19) | collective-permute-done | bytes 65568 | tf_op jit(solution)/shard_map/ppermute | solution.py:325
  72.9 3.0 %collective-permute-start.24 = (bf16[2,128,128]{2,1,0:T(8,128)(2,1)S(1)}, bf16[2,128,128]{2,1,0:T(8,128)(2,1)S(1)}, u32[]{:S(2)}, u32[]{:S(2)}) collective-permute-start(bf16[2,128,128]{2,1,0:T(8,128)(2,1)S(1)} %total.3.refs_0_), channel_id=1, source_target_pairs={{0,6},{1,7},{2,4},{3,5},{4,2},{5,3},{6,0},{7,1},{8,14},{9,15},{10,... | collective-permute-start | bytes 196616 | tf_op jit(solution)/shard_map/ppermute | solution.py:325
  77.2 1.6 %collective-permute-done.24.refs_5_ = bf16[2,128,128]{2,1,0:T(8,128)(2,1)S(1)} collective-permute-done((bf16[2,128,128]{2,1,0:T(8,128)(2,1)S(1)}, bf16[2,128,128]{2,1,0:T(8,128)(2,1)S(1)}, u32[]{:S(2)}, u32[]{:S(2)}) %collective-permute-start.24) | collective-permute-done | bytes 65568 | tf_op jit(solution)/shard_map/ppermute | solution.py:325
  (62 shorter events, 14.7 us)
Async XLA Ops:
  2.9 18.2 %collective-permute-start.1 = (bf16[2,64,2048]{2,1,0:T(8,128)(2,1)S(1)}, bf16[2,64,2048]{2,1,0:T(8,128)(2,1)S(1)}, u32[]{:S(2)}, u32[]{:S(2)}) collective-permute-start(bf16[2,64,2048]{2,1,0:T(8,128)(2,1)S(1)} %get-tuple-element.58.own), channel_id=1, source_target_pairs={{4,12},{12,20},{20,28},{5,13},{13,21},{21,29},{6,14},{14,22},{22,3... | collective-permute-start | bytes 1572872 | tf_op jit(solution)/shard_map/ppermute | solution.py:330
  3.6 13.0 %collective-permute-start.6 = (bf16[2,4,128,128]{3,2,1,0:T(8,128)(2,1)S(1)}, bf16[2,4,128,128]{3,2,1,0:T(8,128)(2,1)S(1)}, u32[]{:S(2)}, u32[]{:S(2)}) collective-permute-start(bf16[2,4,128,128]{3,2,1,0:T(8,128)(2,1)S(1)} %get-tuple-element.72), channel_id=1, source_target_pairs={{0,4},{4,0},{8,12},{12,8},{16,20},{20,16},{24,28},{28,24},{1,5},{5... | collective-permute-start | bytes 786440 | tf_op jit(solution)/shard_map/ppermute | solution.py:315
  9.4 11.6 %collective-permute-start = (bf16[2,4,128,128]{3,2,1,0:T(8,128)(2,1)S(1)}, bf16[2,4,128,128]{3,2,1,0:T(8,128)(2,1)S(1)}, u32[]{:S(2)}, u32[]{:S(2)}) collective-permute-start(bf16[2,4,128,128]{3,2,1,0:T(8,128)(2,1)S(1)} %get-tuple-element.59), channel_id=1, source_target_pairs={{0,4},{4,0},{8,12},{12,8},{16,20},{20,16},{24,28},{28,24},{1,5},{5... | collective-permute-start | bytes 786440 | tf_op jit(solution)/shard_map/ppermute | solution.py:315
  16.7 8.0 %collective-permute-start.7 = (bf16[4,128,128]{2,1,0:T(8,128)(2,1)S(1)}, bf16[4,128,128]{2,1,0:T(8,128)(2,1)S(1)}, u32[]{:S(2)}, u32[]{:S(2)}) collective-permute-start(bf16[4,128,128]{2,1,0:T(8,128)(2,1)S(1)} %get-tuple-element.73), channel_id=1, source_target_pairs={{0,8},{8,0},{4,12},{12,4},{16,24},{24,16},{20,28},{28,20},{1,9},{9... | collective-permute-start | bytes 393224 | tf_op jit(solution)/shard_map/ppermute | solution.py:358
  21.2 20.6 %collective-permute-start.2 = (bf16[2,64,2048]{2,1,0:T(8,128)(2,1)S(1)}, bf16[2,64,2048]{2,1,0:T(8,128)(2,1)S(1)}, u32[]{:S(2)}, u32[]{:S(2)}) collective-permute-start(bf16[2,64,2048]{2,1,0:T(8,128)(2,1)S(1)} %relay.1), channel_id=1, source_target_pairs={{0,4},{4,0},{8,12},{12,8},{16,20},{20,16},{24,28},{28,24},{1,5},{5... | collective-permute-start | bytes 1572872 | tf_op jit(solution)/shard_map/ppermute | solution.py:315
  23.0 5.0 %collective-permute-start.3 = (bf16[4,128,128]{2,1,0:T(8,128)(2,1)S(1)}, bf16[4,128,128]{2,1,0:T(8,128)(2,1)S(1)}, u32[]{:S(2)}, u32[]{:S(2)}) collective-permute-start(bf16[4,128,128]{2,1,0:T(8,128)(2,1)S(1)} %get-tuple-element.64), channel_id=1, source_target_pairs={{0,8},{8,0},{4,12},{12,4},{16,24},{24,16},{20,28},{28,20},{1,9},{9... | collective-permute-start | bytes 393224 | tf_op jit(solution)/shard_map/ppermute | solution.py:358
  24.8 5.5 %collective-permute-start.8 = (bf16[4,128,128]{2,1,0:T(8,128)(2,1)S(1)}, bf16[4,128,128]{2,1,0:T(8,128)(2,1)S(1)}, u32[]{:S(2)}, u32[]{:S(2)}) collective-permute-start(bf16[4,128,128]{2,1,0:T(8,128)(2,1)S(1)} %level_sum.3), channel_id=1, source_target_pairs={{8,16},{16,8},{12,20},{20,12},{9,17},{17,9},{13,21},{21,13},{10,18... | collective-permute-start | bytes 393224 | tf_op jit(solution)/shard_map/ppermute | solution.py:358
  25.4 8.8 %collective-permute-start.9 = (bf16[4,128,128]{2,1,0:T(8,128)(2,1)S(1)}, bf16[4,128,128]{2,1,0:T(8,128)(2,1)S(1)}, u32[]{:S(2)}, u32[]{:S(2)}) collective-permute-start(bf16[4,128,128]{2,1,0:T(8,128)(2,1)S(1)} %level_sum.3), channel_id=1, source_target_pairs={{8,24},{16,0},{12,28},{20,4},{9,25},{17,1},{13,29},{21,5},{10,26},... | collective-permute-start | bytes 393224 | tf_op jit(solution)/shard_map/ppermute | solution.py:358
  28.2 6.9 %collective-permute-start.4 = (bf16[4,128,128]{2,1,0:T(8,128)(2,1)S(1)}, bf16[4,128,128]{2,1,0:T(8,128)(2,1)S(1)}, u32[]{:S(2)}, u32[]{:S(2)}) collective-permute-start(bf16[4,128,128]{2,1,0:T(8,128)(2,1)S(1)} %level_sum.2), channel_id=1, source_target_pairs={{8,16},{16,8},{12,20},{20,12},{9,17},{17,9},{13,21},{21,13},{10,18... | collective-permute-start | bytes 393224 | tf_op jit(solution)/shard_map/ppermute | solution.py:358
  29.0 10.0 %collective-permute-start.5 = (bf16[4,128,128]{2,1,0:T(8,128)(2,1)S(1)}, bf16[4,128,128]{2,1,0:T(8,128)(2,1)S(1)}, u32[]{:S(2)}, u32[]{:S(2)}) collective-permute-start(bf16[4,128,128]{2,1,0:T(8,128)(2,1)S(1)} %level_sum.2), channel_id=1, source_target_pairs={{8,24},{16,0},{12,28},{20,4},{9,25},{17,1},{13,29},{21,5},{10,26},... | collective-permute-start | bytes 393224 | tf_op jit(solution)/shard_map/ppermute | solution.py:358
  34.5 10.7 %collective-permute-start.10 = (bf16[2,4,128,128]{3,2,1,0:T(8,128)(2,1)S(1)}, bf16[2,4,128,128]{3,2,1,0:T(8,128)(2,1)S(1)}, u32[]{:S(2)}, u32[]{:S(2)}) collective-permute-start(bf16[2,4,128,128]{3,2,1,0:T(8,128)(2,1)S(1)} %get-tuple-element.75), channel_id=1, source_target_pairs={{0,4},{4,0},{8,12},{12,8},{16,20},{20,16},{24,28},{28,24},{1,5},{5... | collective-permute-start | bytes 786440 | tf_op jit(solution)/shard_map/ppermute | solution.py:315
  39.2 7.3 %collective-permute-start.12 = (bf16[2,4,128,128]{3,2,1,0:T(8,128)(2,1)S(1)}, bf16[2,4,128,128]{3,2,1,0:T(8,128)(2,1)S(1)}, u32[]{:S(2)}, u32[]{:S(2)}) collective-permute-start(bf16[2,4,128,128]{3,2,1,0:T(8,128)(2,1)S(1)} %get-tuple-element.66.rest_0_.rest_2_), channel_id=1, source_target_pairs={{0,4},{4,0},{8,12},{12,8},{16,20},{20,16},{24,28},{28,24},{1,5},{5... | collective-permute-start | bytes 786440 | tf_op jit(solution)/shard_map/ppermute | solution.py:315
  45.2 21.0 %collective-permute-start.11 = (bf16[2,64,2048]{2,1,0:T(8,128)(2,1)S(1)}, bf16[2,64,2048]{2,1,0:T(8,128)(2,1)S(1)}, u32[]{:S(2)}, u32[]{:S(2)}) collective-permute-start(bf16[2,64,2048]{2,1,0:T(8,128)(2,1)S(1)} %get-tuple-element.83), channel_id=1, source_target_pairs={{4,0},{8,4},{12,8},{16,12},{20,16},{24,20},{28,24},{5,1},{9,5},{13... | collective-permute-start | bytes 1572872 | tf_op jit(solution)/shard_map/ppermute | solution.py:344
  49.8 10.1 %collective-permute-start.14 = (bf16[2,128,128]{2,1,0:T(8,128)(2,1)S(1)}, bf16[2,128,128]{2,1,0:T(8,128)(2,1)S(1)}, u32[]{:S(2)}, u32[]{:S(2)}) collective-permute-start(bf16[2,128,128]{2,1,0:T(8,128)(2,1)S(1)} %get-tuple-element.105), channel_id=1, source_target_pairs={{0,4},{1,5},{2,6},{3,7},{4,0},{5,1},{6,2},{7,3},{8,12},{9,13},{10,... | collective-permute-start | bytes 196616 | tf_op jit(solution)/shard_map/ppermute | solution.py:325
  52.5 7.4 %collective-permute-start.15 = (bf16[2,128,128]{2,1,0:T(8,128)(2,1)S(1)}, bf16[2,128,128]{2,1,0:T(8,128)(2,1)S(1)}, u32[]{:S(2)}, u32[]{:S(2)}) collective-permute-start(bf16[2,128,128]{2,1,0:T(8,128)(2,1)S(1)} %get-tuple-element.106), channel_id=1, source_target_pairs={{0,2},{1,3},{2,0},{3,1},{4,6},{5,7},{6,4},{7,5},{8,10},{9,11},{10,... | collective-permute-start | bytes 196616 | tf_op jit(solution)/shard_map/ppermute | solution.py:325
  54.0 7.6 %collective-permute-start.16 = (bf16[2,128,128]{2,1,0:T(8,128)(2,1)S(1)}, bf16[2,128,128]{2,1,0:T(8,128)(2,1)S(1)}, u32[]{:S(2)}, u32[]{:S(2)}) collective-permute-start(bf16[2,128,128]{2,1,0:T(8,128)(2,1)S(1)} %get-tuple-element.107), channel_id=1, source_target_pairs={{0,6},{1,7},{2,4},{3,5},{4,2},{5,3},{6,0},{7,1},{8,14},{9,15},{10,... | collective-permute-start | bytes 196616 | tf_op jit(solution)/shard_map/ppermute | solution.py:325
  61.6 8.1 %collective-permute-start.17 = (bf16[2,128,128]{2,1,0:T(8,128)(2,1)S(1)}, bf16[2,128,128]{2,1,0:T(8,128)(2,1)S(1)}, u32[]{:S(2)}, u32[]{:S(2)}) collective-permute-start(bf16[2,128,128]{2,1,0:T(8,128)(2,1)S(1)} %total.2.refs_0_), channel_id=1, source_target_pairs={{0,8},{1,9},{2,10},{3,11},{4,12},{5,13},{6,14},{7,15},{8,0},{9,1},... | collective-permute-start | bytes 196616 | tf_op jit(solution)/shard_map/ppermute | solution.py:325
  63.1 6.6 %collective-permute-start.18 = (bf16[2,128,128]{2,1,0:T(8,128)(2,1)S(1)}, bf16[2,128,128]{2,1,0:T(8,128)(2,1)S(1)}, u32[]{:S(2)}, u32[]{:S(2)}) collective-permute-start(bf16[2,128,128]{2,1,0:T(8,128)(2,1)S(1)} %total.2.refs_0_), channel_id=1, source_target_pairs={{0,16},{1,17},{2,18},{3,19},{4,20},{5,21},{6,22},{7,23},{8,24},{9,... | collective-permute-start | bytes 196616 | tf_op jit(solution)/shard_map/ppermute | solution.py:325
  66.2 6.1 %collective-permute-start.19 = (bf16[2,128,128]{2,1,0:T(8,128)(2,1)S(1)}, bf16[2,128,128]{2,1,0:T(8,128)(2,1)S(1)}, u32[]{:S(2)}, u32[]{:S(2)}) collective-permute-start(bf16[2,128,128]{2,1,0:T(8,128)(2,1)S(1)} %total.2.refs_0_), channel_id=1, source_target_pairs={{0,24},{1,25},{2,26},{3,27},{4,28},{5,29},{6,30},{7,31},{8,16},{9,... | collective-permute-start | bytes 196616 | tf_op jit(solution)/shard_map/ppermute | solution.py:325
  72.3 4.3 %collective-permute-start.20 = (bf16[2,128,128]{2,1,0:T(8,128)(2,1)S(1)}, bf16[2,128,128]{2,1,0:T(8,128)(2,1)S(1)}, u32[]{:S(2)}, u32[]{:S(2)}) collective-permute-start(bf16[2,128,128]{2,1,0:T(8,128)(2,1)S(1)} %total.3.refs_0_), channel_id=1, source_target_pairs={{0,2},{1,3},{2,0},{3,1},{4,6},{5,7},{6,4},{7,5},{8,10},{9,11},{10,... | collective-permute-start | bytes 196616 | tf_op jit(solution)/shard_map/ppermute | solution.py:325
  72.9 4.3 %collective-permute-start.23 = (bf16[2,128,128]{2,1,0:T(8,128)(2,1)S(1)}, bf16[2,128,128]{2,1,0:T(8,128)(2,1)S(1)}, u32[]{:S(2)}, u32[]{:S(2)}) collective-permute-start(bf16[2,128,128]{2,1,0:T(8,128)(2,1)S(1)} %total.3.refs_0_), channel_id=1, source_target_pairs={{0,4},{1,5},{2,6},{3,7},{4,0},{5,1},{6,2},{7,3},{8,12},{9,13},{10,... | collective-permute-start | bytes 196616 | tf_op jit(solution)/shard_map/ppermute | solution.py:325
  72.9 5.9 %collective-permute-start.24 = (bf16[2,128,128]{2,1,0:T(8,128)(2,1)S(1)}, bf16[2,128,128]{2,1,0:T(8,128)(2,1)S(1)}, u32[]{:S(2)}, u32[]{:S(2)}) collective-permute-start(bf16[2,128,128]{2,1,0:T(8,128)(2,1)S(1)} %total.3.refs_0_), channel_id=1, source_target_pairs={{0,6},{1,7},{2,4},{3,5},{4,2},{5,3},{6,0},{7,1},{8,14},{9,15},{10,... | collective-permute-start | bytes 196616 | tf_op jit(solution)/shard_map/ppermute | solution.py:325
  75.9 2.9 %collective-permute-start.21 = (bf16[2,128,128]{2,1,0:T(8,128)(2,1)S(1)}, bf16[2,128,128]{2,1,0:T(8,128)(2,1)S(1)}, u32[]{:S(2)}, u32[]{:S(2)}) collective-permute-start(bf16[2,128,128]{2,1,0:T(8,128)(2,1)S(1)} %total.3.refs_0_), channel_id=1, source_target_pairs={{0,1},{1,0},{2,3},{3,2},{4,5},{5,4},{6,7},{7,6},{8,9},{9,8},{10,11... | collective-permute-start | bytes 196616 | tf_op jit(solution)/shard_map/ppermute | solution.py:325
  76.6 2.2 %collective-permute-start.22 = (bf16[2,128,128]{2,1,0:T(8,128)(2,1)S(1)}, bf16[2,128,128]{2,1,0:T(8,128)(2,1)S(1)}, u32[]{:S(2)}, u32[]{:S(2)}) collective-permute-start(bf16[2,128,128]{2,1,0:T(8,128)(2,1)S(1)} %collective-permute-done.20.refs_1_), channel_id=1, source_target_pairs={{0,1},{1,0},{2,3},{3,2},{4,5},{5,4},{6,7},{7,6},{8,9},{9,8},{10,11... | collective-permute-start | bytes 196616 | tf_op jit(solution)/shard_map/ppermute | solution.py:325
  (10 other events, 55.6 us)
